TPU v7x, 32 devices: a whole 2x2x4 slice. The times are simulated.
32 devices in a mesh: grp: 1, zs: 32 (over z, y, x, core).
Axes of the slice: x: 2, y: 2, z: 4, core: 2. Of those that a mesh axis runs over, the one named last changes fastest.
Arguments:
- quark_up: bfloat16 [2, 3, 256, 384], P(None, None, 'zs', 'grp'), may hold values from -3 to 3
- quark_down: bfloat16 [2, 3, 256, 384], P(None, None, 'zs', 'grp'), may hold values from -3 to 3
- forward: bfloat16 [2, 3, 32, 6, 2, 256], P(None, None, 'zs', None, None, 'grp'), may hold values from -3 to 3
- gauge_links: bfloat16 [2, 3, 3, 32, 6, 2, 256], P(None, None, None, 'zs', None, None, 'grp'), may hold values from -2.5 to 2.5
- corner_weight: float32 [8], replicated, may hold values from 0.25 to 2
- corner_offset: int32 [8, 3], replicated, may hold values from 0 to 1, as said below
- lengths: int32 [1024], P('grp'), may hold values from 0 to 7
- separations: int32 [1024], P('grp'), may hold values from 0 to 7
- owner_map: int32 [1024, 1], P('grp'), may hold values from 0 to 31; in each aligned block of 1024 rows (0 to 1023, 1024 to 2047, ...) at most 96 rows name the same one
Outputs:
- seq_source: float32 [2, 3, 32, 6, 2, 256], P(None, None, 'zs', None, None, 'grp')
- elements: float32 [3072, 2], P('zs', 'grp')
Inputs may be any that keep to these rules, and one draw needn't show every extreme that they name: `corner_offset`: the eight rows are the eight corners of the unit cube, each once. `owner_map`: every owner gets one request or more and at most 96; some owner gets exactly 96.
All inputs are finite; a program needn't handle non-finite values.
Results may differ from a plain program's by a relative error of at most 0.0004.
Values may be sent and summed in bfloat16 or wider, within the bound.
No kernel may reach another device: no remote copies, remote signals or barrier semaphores. Data moves between devices by JAX's collectives and lax.ppermute only.
A program may use at most 192 MiB of HBM per device.

v0:
```python
import functools
import math

import jax
import jax.numpy as jnp
from jax import lax
from jax.experimental import pallas as pl
from jax.experimental.pallas import tpu as pltpu
from jax.sharding import PartitionSpec as P

NT = 8
LMAX = 8
PMOM = 3
G = 8
MOST = 96
LANES = 128
XH = 3
CROWS = 16

F32 = jnp.float32
BF16 = jnp.bfloat16
NT_DIMS = (((1,), (1,)), ((), ()))


def passed_along(block, axis, distance):
    devices = range(lax.axis_size(axis))
    route = [((i - distance) % len(devices), i) for i in devices]
    return lax.ppermute(block, axis, route)


def split_two(value):
    high = value.astype(BF16)
    return high, (value - high.astype(F32)).astype(BF16)


def iota(shape, axis):
    return lax.broadcasted_iota(jnp.int32, shape, axis)


def pack_kernel(block_z, block_x, up_ref, down_ref, links_ref, forward_ref, out_ref, edge_ref):
    edge_ref[0:18] = links_ref[:, 0]
    edge_ref[18:24] = forward_ref[:, 0]
    edge_ref[24:30] = forward_ref[:, 1]
    zh = block_z + 1
    slot_lanes = zh * XH
    width_x = block_x * G
    cells = up_ref.shape[3]
    z_blocks = cells // (block_z * width_x)
    up = up_ref[...].astype(F32)
    down = down_ref[...].astype(F32)

    def cross(a, b, c):
        d, e = (c + 1) % 3, (c + 2) % 3
        return up[a, d] * down[b, e] - up[a, e] * down[b, d]

    planes = [cross(0, 0, c) - cross(1, 1, c) for c in range(3)]
    planes += [cross(0, 1, c) + cross(1, 0, c) for c in range(3)]
    lane = iota((1, 2 * LANES), 1)
    half = lane // LANES
    within = lane % LANES
    slot = within // slot_lanes
    cell = within % slot_lanes
    source_row = iota((LANES, 2 * LANES), 0)
    results = []
    for comp in range(6):
        turned = (slot + 12 - comp - 4 * half) % 6
        source = (cell % zh) * width_x + (block_x * (turned + 4 * half) + cell // zh) % width_x
        source = jnp.where((turned < 4) & (slot < 6), source, -1)
        pick = jnp.where(source_row == source, 1.0, 0.0).astype(BF16)
        wide = jnp.concatenate([planes[comp], planes[comp][:, :LANES]], axis=1)
        rows = []
        for zb in range(z_blocks):
            begin = zb * block_z * width_x
            part = wide[:, begin : begin + LANES]
            high = part.astype(BF16).astype(F32)
            rows += [high, part - high]
        left = jnp.concatenate(rows, axis=0).astype(BF16)
        got = jnp.dot(left, pick, preferred_element_type=F32)
        got = got.reshape(z_blocks, 2, NT, 2 * LANES)
        results.append(got[:, 0] + got[:, 1])
    one_slot = iota((NT, LANES), 1) // slot_lanes
    for zb in range(z_blocks):
        for g in range(G):
            at = (g // 4) * LANES
            value = jnp.zeros((NT, LANES), F32)
            for comp in range(6):
                value = jnp.where(
                    one_slot == (comp + g) % 6, results[comp][zb, :, at : at + LANES], value
                )
            out_ref[zb * G + g] = value


def chain_kernel(
    depth_z,
    scale,
    block_z,
    block_x,
    weight_ref,
    offset_ref,
    links_ref,
    links_next_ref,
    forward_ref,
    forward_next_ref,
    edge_ref,
    lengths_ref,
    separations_ref,
    owners_ref,
    chain_ref,
    corner_ref,
    picked_ref,
    link_rows,
    field_rows,
):
    place = lax.axis_index("zs")
    rows_y = links_ref.shape[3]
    zh = block_z + 1
    slot_lanes = zh * XH
    count = block_z * block_x
    link_rows[...] = jnp.zeros_like(link_rows)
    field_rows[...] = jnp.zeros_like(field_rows)

    def fill_links(i, carry):
        for z in range(block_z):
            link_rows[i, block_x * z : block_x * (z + 1)] = links_ref[i, z].astype(F32)
            at = count + block_x * z
            link_rows[i, at : at + block_x] = links_next_ref[i, z].astype(F32)
        link_rows[i, 2 * count : 2 * count + block_x] = edge_ref[i].astype(F32)
        return carry

    def fill_field(i, carry):
        for z in range(block_z):
            field_rows[i, block_x * z : block_x * (z + 1)] = forward_ref[i, z].astype(F32)
            at = count + block_x * z
            field_rows[i, at : at + block_x] = forward_next_ref[i, z].astype(F32)
        field_rows[i, 2 * count : 2 * count + block_x] = edge_ref[18 + i].astype(F32)
        at = 2 * count + block_x
        field_rows[i, at : at + block_x] = edge_ref[24 + i].astype(F32)
        return carry

    lax.fori_loop(0, 18, fill_links, 0)
    lax.fori_loop(0, 6, fill_field, 0)

    row = iota((CROWS, LANES), 0)
    z_of_row = (place // G) * block_z + row // block_x
    angle = (z_of_row * PMOM % depth_z).astype(F32) * (2.0 * math.pi / depth_z)
    inside = row < count
    cos_z = jnp.where(inside, jnp.cos(angle) * scale, 0.0)[:, :1]
    sin_z = jnp.where(inside, jnp.sin(angle) * scale, 0.0)[:, :1]
    total_rows = link_rows.shape[1]

    def step(length, carry):
        for at in range(0, rows_y, LANES):
            lanes = slice(at, at + LANES)
            vec = [
                pltpu.roll(field_rows[c, :, lanes], total_rows - block_x, 0) for c in range(6)
            ]
            for a in range(3):
                real = None
                imag = None
                for b in range(3):
                    link_real = link_rows[a * 3 + b, :, lanes]
                    link_imag = link_rows[9 + a * 3 + b, :, lanes]
                    term_real = link_real * vec[b] - link_imag * vec[3 + b]
                    term_imag = link_real * vec[3 + b] + link_imag * vec[b]
                    real = term_real if real is None else real + term_real
                    imag = term_imag if imag is None else imag + term_imag
                field_rows[a, :, lanes] = real
                field_rows[3 + a, :, lanes] = imag
                top_real, top_imag = real[:CROWS], imag[:CROWS]
                chain_ref[length, a * CROWS : (a + 1) * CROWS, lanes] = (
                    top_real * cos_z - top_imag * sin_z
                )
                chain_ref[length, (3 + a) * CROWS : (4 + a) * CROWS, lanes] = (
                    top_real * sin_z + top_imag * cos_z
                )
        return carry

    lax.fori_loop(0, LMAX, step, 0)

    shape = (6 * CROWS, LANES)
    row = iota(shape, 0)
    lane = iota(shape, 1)
    comp = row // CROWS
    z_step = lane % slot_lanes % zh - row % CROWS // block_x
    x_step = lane % slot_lanes // zh - row % block_x
    here = (lane // slot_lanes == (comp + place % G) % 6) & (row % CROWS < count)
    sums = [jnp.zeros(shape, F32), jnp.zeros(shape, F32)]
    for k in range(8):
        match = here & (x_step == offset_ref[0, k]) & (z_step == offset_ref[2, k])
        for y_step in range(2):
            taken = jnp.where(offset_ref[1, k] == y_step, weight_ref[k], 0.0)
            sums[y_step] = sums[y_step] + jnp.where(match, taken, 0.0)
    for y_step in range(2):
        high, low = split_two(sums[y_step])
        corner_ref[0, y_step * 6 * CROWS : (y_step + 1) * 6 * CROWS] = high
        corner_ref[1, y_step * 6 * CROWS : (y_step + 1) * 6 * CROWS] = low

    mine = owners_ref[...] == place
    codes = (lengths_ref[...] * (2 * NT) + separations_ref[...]).astype(F32)
    member = jnp.where(mine, 1.0, 0.0)
    below = jnp.where(iota((LANES, LANES), 0) < iota((LANES, LANES), 1), 1.0, 0.0)
    earlier = jnp.dot(member.astype(BF16), below.astype(BF16), preferred_element_type=F32)
    running = jnp.zeros((1, 1), F32)
    picked = jnp.zeros((8, LANES), F32)
    slots = iota((LANES, LANES), 0).astype(F32)
    head = iota((8, LANES), 0) == 0
    for i in range(member.shape[0]):
        key = jnp.where(member[i : i + 1] > 0.5, earlier[i : i + 1] + running, -1.0)
        hits = jnp.where(slots == key, 1.0, 0.0).astype(BF16)
        left = jnp.where(head, codes[i : i + 1], 1.0).astype(BF16)
        picked = picked + lax.dot_general(left, hits, NT_DIMS, preferred_element_type=F32)
        running = running + jnp.sum(member[i : i + 1], axis=1, keepdims=True)
    lane_of = picked[0:1].astype(jnp.int32) + iota((8, LANES), 0) % 2 * NT
    picked_ref[...] = jnp.where(picked[1:2] > 0.5, lane_of, -1)


def meet_kernel(block_z, block_x, got_ref, corner_ref, chain_ref, seq_ref, table_ref):
    rows_y = got_ref.shape[0] * NT
    got = got_ref[...].reshape(rows_y, LANES)
    high, low = split_two(got)
    dot = functools.partial(
        lax.dot_general, dimension_numbers=NT_DIMS, preferred_element_type=F32
    )
    both = dot(corner_ref[0], high) + dot(corner_ref[0], low) + dot(corner_ref[1], high)
    size = 6 * CROWS
    seq = both[:size] + pltpu.roll(both[size:], rows_y - NT, 1)
    for comp in range(6):
        for z in range(block_z):
            at = comp * CROWS + z * block_x
            seq_ref[comp, z] = seq[at : at + block_x]
    turned = jnp.concatenate([-seq[3 * CROWS :], seq[: 3 * CROWS]], axis=0)
    sums = []
    for length in range(LMAX):
        chain = chain_ref[length]
        for field in (seq, turned):
            prod = field * chain
            part = prod[:8]
            for at in range(8, size, 8):
                part = part + prod[at : at + 8]
            narrow = part[:, :LANES]
            for at in range(LANES, rows_y, LANES):
                narrow = narrow + part[:, at : at + LANES]
            sums.append(jnp.sum(narrow, axis=0, keepdims=True))
    table = jnp.concatenate(sums, axis=0)
    for shift in (64, 32, 16, 8):
        table = table + pltpu.roll(table, shift, 1)
    mine = iota((2 * LMAX, LANES), 1) // NT == iota((2 * LMAX, LANES), 0)
    flat = jnp.sum(jnp.where(mine, table, 0.0), axis=0, keepdims=True)
    table_ref[...] = jnp.broadcast_to(flat, table_ref.shape)


def final_kernel(tables_ref, picked_ref, out_ref):
    total = jnp.sum(tables_ref[...], axis=0, keepdims=True)
    picked = picked_ref[...]
    value = jnp.take_along_axis(
        jnp.broadcast_to(total, picked.shape), jnp.maximum(picked, 0), axis=1
    )
    value = jnp.where(picked >= 0, value, 0.0)
    out_ref[...] = value[:2, : out_ref.shape[1]]


VMEM = pl.BlockSpec(memory_space=pltpu.VMEM)
SMEM = pl.BlockSpec(memory_space=pltpu.SMEM)


def cost(flops, moved):
    return pl.CostEstimate(flops=flops, bytes_accessed=moved, transcendentals=0)


def shards(
    quark_up,
    quark_down,
    forward,
    gauge_links,
    corner_weight,
    corner_offset,
    lengths,
    separations,
    owner_map,
):
    devices = lax.axis_size("zs")
    block_z, block_x, rows_y = forward.shape[3:]
    cells = quark_up.shape[3]
    depth_z = cells // (block_x * G)
    scale = 1.0 / math.sqrt(cells * (rows_y // NT))
    links = gauge_links.reshape(18, block_z, block_x, rows_y)
    field = forward.reshape(6, block_z, block_x, rows_y)

    links_next = passed_along(links, "zs", -G)
    field_next = passed_along(field, "zs", -G)
    payload, edge = pl.pallas_call(
        functools.partial(pack_kernel, block_z, block_x),
        out_shape=(
            jax.ShapeDtypeStruct((devices, NT, LANES), F32),
            jax.ShapeDtypeStruct((30, block_x, rows_y), BF16),
        ),
        grid=(1,),
        in_specs=[
            pl.BlockSpec(quark_up.shape, lambda i: (0, 0, 0, 0)),
            pl.BlockSpec(quark_down.shape, lambda i: (0, 0, 0, 0)),
            pl.BlockSpec((18, 1, block_x, rows_y), lambda i: (0, 0, 0, 0)),
            pl.BlockSpec((6, 2, block_x, rows_y), lambda i: (0, 0, 0, 0)),
        ],
        out_specs=(
            pl.BlockSpec((devices, NT, LANES), lambda i: (0, 0, 0)),
            pl.BlockSpec((30, block_x, rows_y), lambda i: (0, 0, 0)),
        ),
        cost_estimate=cost(10_000_000, 400_000),
        name="pack",
    )(quark_up, quark_down, links, field)
    edge_next = passed_along(edge, "zs", -2 * G)
    got = lax.all_to_all(payload, "zs", split_axis=0, concat_axis=0, tiled=True)

    requests = (lengths.shape[0] // LANES, LANES)
    chain, corner, picked = pl.pallas_call(
        functools.partial(chain_kernel, depth_z, scale, block_z, block_x),
        out_shape=(
            jax.ShapeDtypeStruct((LMAX, 6 * CROWS, rows_y), F32),
            jax.ShapeDtypeStruct((2, 12 * CROWS, LANES), BF16),
            jax.ShapeDtypeStruct((8, LANES), jnp.int32),
        ),
        in_specs=[SMEM, SMEM] + [VMEM] * 8,
        out_specs=(VMEM, VMEM, VMEM),
        scratch_shapes=[
            pltpu.VMEM((18, 32, rows_y), F32),
            pltpu.VMEM((6, 32, rows_y), F32),
        ],
        cost_estimate=cost(20_000_000, 2_000_000),
        name="chain",
    )(
        corner_weight,
        corner_offset.T,
        links,
        links_next,
        field,
        field_next,
        edge_next,
        lengths.reshape(requests),
        separations.reshape(requests),
        owner_map.reshape(requests),
    )

    seq, table = pl.pallas_call(
        functools.partial(meet_kernel, block_z, block_x),
        out_shape=(
            jax.ShapeDtypeStruct((6, block_z, block_x, rows_y), F32),
            jax.ShapeDtypeStruct((devices, LANES), F32),
        ),
        in_specs=[VMEM] * 3,
        out_specs=(VMEM, VMEM),
        cost_estimate=cost(20_000_000, 1_000_000),
        name="meet",
    )(got, corner, chain)
    tables = lax.all_to_all(
        table.reshape(devices, 1, LANES), "zs", split_axis=0, concat_axis=0, tiled=True
    )
    owned = pl.pallas_call(
        final_kernel,
        out_shape=jax.ShapeDtypeStruct((2, MOST), F32),
        in_specs=[VMEM] * 2,
        out_specs=VMEM,
        name="final",
    )(tables.reshape(devices, LANES), picked)
    return (seq.reshape(2, 3, 1, block_z, block_x, rows_y), owned.T)


def solution(mesh):
    in_specs = (
        P(None, None, "zs", "grp"),
        P(None, None, "zs", "grp"),
        P(None, None, "zs", None, None, "grp"),
        P(None, None, None, "zs", None, None, "grp"),
        P(),
        P(),
        P("grp"),
        P("grp"),
        P("grp", None),
    )
    out_specs = (P(None, None, "zs", None, None, "grp"), P("zs", "grp"))
    return jax.shard_map(shards, mesh=mesh, in_specs=in_specs, out_specs=out_specs, check_vma=False)
```

profile of v0, /device:TPU:0, one launch (start us, length us, event | category | flops | bytes accessed | tf_op | source)
XLA Modules:
  0.0 40.3 jit_solution(9976620965817610051)
XLA Ops:
  0.6 1.8 %pack.1 = (f32[32,8,128]{2,1,0:T(8,128)}, bf16[30,2,256]{2,1,0:T(2,128)(2,1)}) custom-call(bf16[2,3,8,384]{3,2,1,0:T(8,128)(2,1)} %up_ref.1, bf16[2,3,8,384]{3,2,1,0:T(8,128)(2,1)} %down_ref.1, bf16[18,6,2,256]{3,2,1,0:T(2,128)(2,1)} %bitcast.14, bf16[6,6,2,256]{3,2,1,0:T(2,128)(2,1)} %bitcast.17), custom_call_target="tpu_custom_call" | custom-call | flops 10000000 | bytes 400000 | tf_op jit(solution)/shard_map/pack/pallas_call | solution.py:291
  2.4 0.0 copy-start.1
  2.4 0.0 copy-start.2
  2.4 0.0 copy-start.6
  2.4 7.3 %all-to-all-start = ((f32[32,8,128]{2,1,0:T(8,128)}), f32[32,8,128]{2,1,0:T(8,128)S(1)}, u32[]{:S(2)}, u32[]{:S(2)}) async-start(f32[32,8,128]{2,1,0:T(8,128)} %get-tuple-element.9), calls=%async_computation | async-start | bytes 262144 | tf_op jit(solution)/shard_map/all_to_all | solution.py:312
  9.7 0.0 copy-done.1
  9.7 3.7 %collective-permute-start = (bf16[18,6,2,256]{3,2,1,0:T(2,128)(2,1)S(1)}, bf16[18,6,2,256]{3,2,1,0:T(2,128)(2,1)S(1)}, u32[]{:S(2)}, u32[]{:S(2)}) collective-permute-start(bf16[18,6,2,256]{3,2,1,0:T(2,128)(2,1)S(1)} %bitcast.16), channel_id=1, source_target_pairs={{8,0},{9,1},{10,2},{11,3},{12,4},{13,5},{14,6},{15,7},{16,8},{17,9... | collective-permute-start | bytes 331784 | tf_op jit(solution)/shard_map/ppermute | solution.py:28
  13.4 0.0 copy-done.2
  13.4 0.5 %collective-permute-start.1 = (bf16[6,6,2,256]{3,2,1,0:T(2,128)(2,1)S(1)}, bf16[6,6,2,256]{3,2,1,0:T(2,128)(2,1)S(1)}, u32[]{:S(2)}, u32[]{:S(2)}) collective-permute-start(bf16[6,6,2,256]{3,2,1,0:T(2,128)(2,1)S(1)} %bitcast.19), channel_id=1, source_target_pairs={{8,0},{9,1},{10,2},{11,3},{12,4},{13,5},{14,6},{15,7},{16,8},{17,9... | collective-permute-start | bytes 110600 | tf_op jit(solution)/shard_map/ppermute | solution.py:28
  13.9 0.0 copy-done.6
  13.9 0.0 collective-permute-start.2
  13.9 6.8 %collective-permute-done.2.edge_ref = bf16[30,2,256]{2,1,0:T(2,128)(2,1)S(1)} collective-permute-done((bf16[30,2,256]{2,1,0:T(2,128)(2,1)S(1)}, bf16[30,2,256]{2,1,0:T(2,128)(2,1)S(1)}, u32[]{:S(2)}, u32[]{:S(2)}) %collective-permute-start.2) | collective-permute-done | bytes 30752 | tf_op jit(solution)/shard_map/ppermute | solution.py:28
  20.8 0.0 copy-start.5
  20.8 0.0 collective-permute-done.1.forward_next_ref
  20.8 0.0 copy-start.4
  20.8 0.0 collective-permute-done.links_next_ref
  20.8 0.0 copy-start.3
  20.8 0.6 %copy-done.5 = bf16[30,2,256]{2,1,0:T(2,128)(2,1)} copy-done((bf16[30,2,256]{2,1,0:T(2,128)(2,1)}, bf16[30,2,256]{2,1,0:T(2,128)(2,1)S(1)}, u32[]{:S(2)}) %copy-start.5) | copy-done | bytes 30744
  21.4 0.0 copy-done.4
  21.4 0.0 copy-done.3
  21.4 3.3 %chain.1 = (f32[8,96,256]{2,1,0:T(8,128)}, bf16[2,192,128]{2,1,0:T(8,128)(2,1)}, s32[8,128]{1,0:T(8,128)}) custom-call(f32[8]{0:T(128)} %weight_ref.1, s32[3,8]{1,0:T(4,128)} %bitcast.25, bf16[18,6,2,256]{3,2,1,0:T(2,128)(2,1)} %bitcast.15, bf16[18,6,2,256]{3,2,1,0:T(2,128)(2,1)} %copy-done.3, bf16[6,6,2,256]{3,2,1,0:T(2,128)(2,1)} %bitcast.18, ...), custom_call_target="tpu_custom_call" | custom-call | flops 20000000 | bytes 2000000 | tf_op jit(solution)/shard_map/chain/pallas_call | solution.py:315
  24.8 0.0 all-to-all-done.got_ref
  24.8 0.0 copy-start
  24.8 0.6 %copy-done = f32[32,8,128]{2,1,0:T(8,128)} copy-done((f32[32,8,128]{2,1,0:T(8,128)}, f32[32,8,128]{2,1,0:T(8,128)S(1)}, u32[]{:S(2)}) %copy-start) | copy-done | bytes 131096
  25.4 2.6 %meet.1 = (f32[6,6,2,256]{3,2,1,0:T(2,128)}, f32[32,128]{1,0:T(8,128)}) custom-call(f32[32,8,128]{2,1,0:T(8,128)} %copy-done, bf16[2,192,128]{2,1,0:T(8,128)(2,1)} %get-tuple-element.11.corner_ref, f32[8,96,256]{2,1,0:T(8,128)} %get-tuple-element.12.chain_ref), custom_call_target="tpu_custom_call" | custom-call | flops 20000000 | bytes 1000000 | tf_op jit(solution)/shard_map/meet/pallas_call | solution.py:343
  28.0 11.0 %all_to_all.10 = f32[32,1,128]{2,1,0:T(1,128)} all-to-all(f32[32,1,128]{2,1,0:T(1,128)} %bitcast.21), channel_id=1, replica_groups=mesh['grp'=1,'zs'=32] {'zs'}, dimensions={0} | all-to-all | bytes 32768 | tf_op jit(solution)/shard_map/all_to_all | solution.py:354
  39.0 1.4 %final.1 = f32[2,96]{1,0:T(2,128)} custom-call(f32[32,128]{1,0:T(8,128)} %bitcast.20, s32[8,128]{1,0:T(8,128)} %get-tuple-element.15.picked_ref), custom_call_target="tpu_custom_call" | custom-call | tf_op jit(solution)/shard_map/final/pallas_call | solution.py:357
Async XLA Ops:
  2.4 7.3 %copy-start.1 = (bf16[2,3,3,1,6,2,256]{6,5,4,3,2,1,0:T(2,128)(2,1)S(1)}, bf16[2,3,3,1,6,2,256]{6,5,4,3,2,1,0:T(2,128)(2,1)}, u32[]{:S(2)}) copy-start(bf16[2,3,3,1,6,2,256]{6,5,4,3,2,1,0:T(2,128)(2,1)} %param.12) | copy-start | bytes 331780
  2.4 11.0 %copy-start.2 = (bf16[2,3,1,6,2,256]{5,4,3,2,1,0:T(2,128)(2,1)S(1)}, bf16[2,3,1,6,2,256]{5,4,3,2,1,0:T(2,128)(2,1)}, u32[]{:S(2)}) copy-start(bf16[2,3,1,6,2,256]{5,4,3,2,1,0:T(2,128)(2,1)} %param.11) | copy-start | bytes 110596
  2.4 11.5 %copy-start.6 = (bf16[30,2,256]{2,1,0:T(2,128)(2,1)S(1)}, bf16[30,2,256]{2,1,0:T(2,128)(2,1)}, u32[]{:S(2)}) copy-start(bf16[30,2,256]{2,1,0:T(2,128)(2,1)} %get-tuple-element.10) | copy-start | bytes 92164
  2.4 22.4 %all-to-all-start = ((f32[32,8,128]{2,1,0:T(8,128)}), f32[32,8,128]{2,1,0:T(8,128)S(1)}, u32[]{:S(2)}, u32[]{:S(2)}) async-start(f32[32,8,128]{2,1,0:T(8,128)} %get-tuple-element.9), calls=%async_computation | async-start | bytes 262144 | tf_op jit(solution)/shard_map/all_to_all | solution.py:312
  9.7 11.1 %collective-permute-start = (bf16[18,6,2,256]{3,2,1,0:T(2,128)(2,1)S(1)}, bf16[18,6,2,256]{3,2,1,0:T(2,128)(2,1)S(1)}, u32[]{:S(2)}, u32[]{:S(2)}) collective-permute-start(bf16[18,6,2,256]{3,2,1,0:T(2,128)(2,1)S(1)} %bitcast.16), channel_id=1, source_target_pairs={{8,0},{9,1},{10,2},{11,3},{12,4},{13,5},{14,6},{15,7},{16,8},{17,9... | collective-permute-start | bytes 331784 | tf_op jit(solution)/shard_map/ppermute | solution.py:28
  13.4 7.3 %collective-permute-start.1 = (bf16[6,6,2,256]{3,2,1,0:T(2,128)(2,1)S(1)}, bf16[6,6,2,256]{3,2,1,0:T(2,128)(2,1)S(1)}, u32[]{:S(2)}, u32[]{:S(2)}) collective-permute-start(bf16[6,6,2,256]{3,2,1,0:T(2,128)(2,1)S(1)} %bitcast.19), channel_id=1, source_target_pairs={{8,0},{9,1},{10,2},{11,3},{12,4},{13,5},{14,6},{15,7},{16,8},{17,9... | collective-permute-start | bytes 110600 | tf_op jit(solution)/shard_map/ppermute | solution.py:28
  13.9 6.8 %collective-permute-start.2 = (bf16[30,2,256]{2,1,0:T(2,128)(2,1)S(1)}, bf16[30,2,256]{2,1,0:T(2,128)(2,1)S(1)}, u32[]{:S(2)}, u32[]{:S(2)}) collective-permute-start(bf16[30,2,256]{2,1,0:T(2,128)(2,1)S(1)} %copy-done.6), channel_id=1, source_target_pairs={{16,0},{17,1},{18,2},{19,3},{20,4},{21,5},{22,6},{23,7},{24,8},{25... | collective-permute-start | bytes 92168 | tf_op jit(solution)/shard_map/ppermute | solution.py:28
  20.8 0.6 %copy-start.5 = (bf16[30,2,256]{2,1,0:T(2,128)(2,1)}, bf16[30,2,256]{2,1,0:T(2,128)(2,1)S(1)}, u32[]{:S(2)}) copy-start(bf16[30,2,256]{2,1,0:T(2,128)(2,1)S(1)} %collective-permute-done.2.edge_ref) | copy-start | bytes 92164
  20.8 0.6 %copy-start.4 = (bf16[6,6,2,256]{3,2,1,0:T(2,128)(2,1)}, bf16[6,6,2,256]{3,2,1,0:T(2,128)(2,1)S(1)}, u32[]{:S(2)}) copy-start(bf16[6,6,2,256]{3,2,1,0:T(2,128)(2,1)S(1)} %collective-permute-done.1.forward_next_ref) | copy-start | bytes 110596
  20.8 0.6 %copy-start.3 = (bf16[18,6,2,256]{3,2,1,0:T(2,128)(2,1)}, bf16[18,6,2,256]{3,2,1,0:T(2,128)(2,1)S(1)}, u32[]{:S(2)}) copy-start(bf16[18,6,2,256]{3,2,1,0:T(2,128)(2,1)S(1)} %collective-permute-done.links_next_ref) | copy-start | bytes 331780
  24.8 0.6 %copy-start = (f32[32,8,128]{2,1,0:T(8,128)}, f32[32,8,128]{2,1,0:T(8,128)S(1)}, u32[]{:S(2)}) copy-start(f32[32,8,128]{2,1,0:T(8,128)S(1)} %all-to-all-done.got_ref) | copy-start | bytes 393220
where the time goes:
time: 40.7 us; the launch traced here: 40.3 us
  starting transfers between devices  11.5 us (28%)
  blocking collectives  11 us (27%)
  Pallas kernels  9.03 us (22%)
  waiting for transfers between devices  6.85 us (17%)
  local copies, waits for them, and re-layouts  1.3 us (3%)
  between operations  0.68 us (2%)
    all_to_all x1, blocking collectives, shards(): lax.all_to_all(table.reshape(devices, 1, LANES), 'zs', split_axis=0, conc...  11 us
    all_to_all x1, starting transfers between devices, shards(): got = lax.all_to_all(payload, 'zs', split_axis=0, concat_axis=0, tiled=True)  7.3 us
    ppermute x3, waiting for transfers between devices, passed_along(): return lax.ppermute(block, axis, route)  6.85 us
    ppermute x3, starting transfers between devices, passed_along(): return lax.ppermute(block, axis, route)  4.19 us
    pallas_call x1, Pallas kernels, shards(): pl.pallas_call(functools.partial(chain_kernel, depth_z, scale, block_z, b...  3.33 us
    pallas_call x1, Pallas kernels, shards(): pl.pallas_call(functools.partial(meet_kernel, block_z, block_x), out_shap...  2.57 us
    pallas_call x1, Pallas kernels, shards(): pl.pallas_call(functools.partial(pack_kernel, block_z, block_x), out_shap...  1.77 us
    pallas_call x1, Pallas kernels, shards(): pl.pallas_call(final_kernel, out_shape=jax.ShapeDtypeStruct((2, MOST), F3...  1.36 us
  transfers between devices with their start and end apart: 4, of which 1 were waited for; matrix products, arithmetic and copies ran while one was open for 0% of the time, Pallas kernels for 8%

commit v1 on v0

--- a/solution.py
+++ b/solution.py
@@ -246,11 +246,11 @@
         table = table + pltpu.roll(table, shift, 1)
     mine = iota((2 * LMAX, LANES), 1) // NT == iota((2 * LMAX, LANES), 0)
     flat = jnp.sum(jnp.where(mine, table, 0.0), axis=0, keepdims=True)
-    table_ref[...] = jnp.broadcast_to(flat, table_ref.shape)
-
-
-def final_kernel(tables_ref, picked_ref, out_ref):
-    total = jnp.sum(tables_ref[...], axis=0, keepdims=True)
+    table_ref[...] = flat
+
+
+def final_kernel(total_ref, picked_ref, out_ref):
+    total = total_ref[...]
     picked = picked_ref[...]
     value = jnp.take_along_axis(
         jnp.broadcast_to(total, picked.shape), jnp.maximum(picked, 0), axis=1
@@ -265,6 +265,10 @@
 
 def cost(flops, moved):
     return pl.CostEstimate(flops=flops, bytes_accessed=moved, transcendentals=0)
+
+
+PARAMS = pltpu.CompilerParams(vmem_limit_bytes=16 * 1024 * 1024)
+WIDE_PARAMS = pltpu.CompilerParams(vmem_limit_bytes=60 * 1024 * 1024)
 
 
 def shards(
@@ -305,7 +309,8 @@
             pl.BlockSpec((devices, NT, LANES), lambda i: (0, 0, 0)),
             pl.BlockSpec((30, block_x, rows_y), lambda i: (0, 0, 0)),
         ),
-        cost_estimate=cost(10_000_000, 400_000),
+        compiler_params=WIDE_PARAMS,
+        cost_estimate=cost(2_000_000_000, 400_000),
         name="pack",
     )(quark_up, quark_down, links, field)
     edge_next = passed_along(edge, "zs", -2 * G)
@@ -325,7 +330,8 @@
             pltpu.VMEM((18, 32, rows_y), F32),
             pltpu.VMEM((6, 32, rows_y), F32),
         ],
-        cost_estimate=cost(20_000_000, 2_000_000),
+        compiler_params=PARAMS,
+        cost_estimate=cost(3_000_000_000, 2_000_000),
         name="chain",
     )(
         corner_weight,
@@ -344,23 +350,23 @@
         functools.partial(meet_kernel, block_z, block_x),
         out_shape=(
             jax.ShapeDtypeStruct((6, block_z, block_x, rows_y), F32),
-            jax.ShapeDtypeStruct((devices, LANES), F32),
+            jax.ShapeDtypeStruct((1, LANES), F32),
         ),
         in_specs=[VMEM] * 3,
         out_specs=(VMEM, VMEM),
-        cost_estimate=cost(20_000_000, 1_000_000),
+        compiler_params=PARAMS,
+        cost_estimate=cost(2_000_000_000, 1_000_000),
         name="meet",
     )(got, corner, chain)
-    tables = lax.all_to_all(
-        table.reshape(devices, 1, LANES), "zs", split_axis=0, concat_axis=0, tiled=True
-    )
+    total = lax.psum(table, "zs")
     owned = pl.pallas_call(
         final_kernel,
         out_shape=jax.ShapeDtypeStruct((2, MOST), F32),
         in_specs=[VMEM] * 2,
         out_specs=VMEM,
+        compiler_params=PARAMS,
         name="final",
-    )(tables.reshape(devices, LANES), picked)
+    )(total, picked)
     return (seq.reshape(2, 3, 1, block_z, block_x, rows_y), owned.T)
 
 

time: 40.7 us -> 62.8 us (1.54)
  blocking collectives: 11 us -> 38.3 us
  Pallas kernels: 9.03 us -> 5.79 us
  waiting for transfers between devices: 6.85 us -> 5.2 us
  local copies, waits for them, and re-layouts: 1.3 us -> 0.66 us
    psum x0 -> x1, blocking collectives: none -> 38.3 us  [shards(): total = lax.psum(table, 'zs')]
    all_to_all x1 -> x0, blocking collectives: 11 us -> none  [shards(): lax.all_to_all(table.reshape(devices, 1, LANES), 'zs', split_axis=0, conc...]
    ppermute x3, waiting for transfers between devices: 6.85 us -> 0.01 us  [passed_along(): return lax.ppermute(block, axis, route)]
    all_to_all x1, waiting for transfers between devices: 0.01 us -> 5.19 us  [shards(): got = lax.all_to_all(payload, 'zs', split_axis=0, concat_axis=0, tiled=True)]
    pallas_call x1, Pallas kernels: 2.57 us -> 1.08 us  [shards(): pl.pallas_call(functools.partial(meet_kernel, block_z, block_x), out_shap...]
    ppermute x3, starting transfers between devices: 4.19 us -> 5.55 us  [passed_along(): return lax.ppermute(block, axis, route)]
    all_to_all x1, starting transfers between devices: 7.3 us -> 6.16 us  [shards(): got = lax.all_to_all(payload, 'zs', split_axis=0, concat_axis=0, tiled=True)]
    pallas_call x1, Pallas kernels: 3.33 us -> 2.31 us  [shards(): pl.pallas_call(functools.partial(chain_kernel, depth_z, scale, block_z, b...]
  transfers between devices with their start and end apart: 4 -> 4, of which waited for: 1 -> 1; matrix products, arithmetic and copies ran while one was open for 0% -> 0% of each run, Pallas kernels for 8% -> 7%
where the time goes in v1:
time: 62.8 us; the launch traced here: 62.4 us
  blocking collectives  38.3 us (61%)
  starting transfers between devices  11.7 us (19%)
  Pallas kernels  5.79 us (9%)
  waiting for transfers between devices  5.2 us (8%)
  between operations  0.75 us (1%)
  local copies, waits for them, and re-layouts  0.66 us (1%)
    psum x1, blocking collectives, shards(): total = lax.psum(table, 'zs')  38.3 us
    all_to_all x1, starting transfers between devices, shards(): got = lax.all_to_all(payload, 'zs', split_axis=0, concat_axis=0, tiled=True)  6.16 us
    ppermute x3, starting transfers between devices, passed_along(): return lax.ppermute(block, axis, route)  5.55 us
    all_to_all x1, waiting for transfers between devices, shards(): got = lax.all_to_all(payload, 'zs', split_axis=0, concat_axis=0, tiled=True)  5.19 us
    pallas_call x1, Pallas kernels, shards(): pl.pallas_call(functools.partial(chain_kernel, depth_z, scale, block_z, b...  2.31 us
    pallas_call x1, Pallas kernels, shards(): pl.pallas_call(functools.partial(pack_kernel, block_z, block_x), out_shap...  1.77 us
  transfers between devices with their start and end apart: 4, of which 1 were waited for; matrix products, arithmetic and copies ran while one was open for 0% of the time, Pallas kernels for 7%

profile of v1, /device:TPU:0, one launch (start us, length us, event | category | flops | bytes accessed | tf_op | source)
XLA Modules:
  0.0 62.4 jit_solution(10696445052726728851)
XLA Ops:
  0.6 5.1 %collective-permute-start.1 = (bf16[6,6,2,256]{3,2,1,0:T(2,128)(2,1)}, bf16[6,6,2,256]{3,2,1,0:T(2,128)(2,1)S(1)}, u32[]{:S(2)}, u32[]{:S(2)}) collective-permute-start(bf16[6,6,2,256]{3,2,1,0:T(2,128)(2,1)} %bitcast.13), channel_id=1, source_target_pairs={{8,0},{9,1},{10,2},{11,3},{12,4},{13,5},{14,6},{15,7},{16,8},{17,9... | collective-permute-start | bytes 110600 | tf_op jit(solution)/shard_map/ppermute | solution.py:28
  5.7 0.4 collective-permute-start
  6.2 1.8 %pack.1 = (f32[32,8,128]{2,1,0:T(8,128)}, bf16[30,2,256]{2,1,0:T(2,128)(2,1)}) custom-call(bf16[2,3,8,384]{3,2,1,0:T(8,128)(2,1)} %up_ref.1, bf16[2,3,8,384]{3,2,1,0:T(8,128)(2,1)} %down_ref.1, bf16[18,6,2,256]{3,2,1,0:T(2,128)(2,1)} %bitcast.11, bf16[6,6,2,256]{3,2,1,0:T(2,128)(2,1)} %bitcast.14), custom_call_target="tpu_custom_call" | custom-call | flops 2000000000 | bytes 400000 | tf_op jit(solution)/shard_map/pack/pallas_call | solution.py:295
  8.0 0.0 collective-permute-start.2
  8.0 0.0 copy-start
  8.0 0.0 copy-start.1
  8.0 0.0 copy-start.3
  8.0 0.0 copy-start.4
  8.0 6.2 %all-to-all-start = ((f32[32,8,128]{2,1,0:T(8,128)}), f32[32,8,128]{2,1,0:T(8,128)S(1)}, u32[]{:S(2)}, u32[]{:S(2)}) async-start(f32[32,8,128]{2,1,0:T(8,128)} %get-tuple-element.9), calls=%async_computation | async-start | bytes 262144 | tf_op jit(solution)/shard_map/all_to_all | solution.py:317
  14.2 0.0 copy-start.2
  14.2 0.0 collective-permute-done.2.edge_ref
  14.2 0.0 collective-permute-done.1.forward_next_ref
  14.2 0.0 collective-permute-done.links_next_ref
  14.2 0.0 copy-start.5
  14.2 0.0 copy-start.6
  14.2 0.0 copy-done
  14.2 0.0 copy-done.1
  14.3 0.0 copy-done.3
  14.3 0.0 copy-done.4
  14.3 0.6 copy-done.2
  14.9 0.0 copy-done.5
  14.9 0.0 copy-done.6
  14.9 2.3 %chain.1 = (f32[8,96,256]{2,1,0:T(8,128)S(1)}, bf16[2,192,128]{2,1,0:T(8,128)(2,1)S(1)}, s32[8,128]{1,0:T(8,128)S(1)}) custom-call(f32[8]{0:T(128)S(1)} %copy-done.6, s32[3,8]{1,0:T(4,128)S(1)} %bitcast.19, bf16[18,6,2,256]{3,2,1,0:T(2,128)(2,1)S(1)} %bitcast.12, bf16[18,6,2,256]{3,2,1,0:T(2,128)(2,1)S(1)} %collective-permute-done.links_next_ref, ...), custom_call_target="tpu_custom_call" | custom-call | flops 3000000000 | bytes 2000000 | tf_op jit(solution)/shard_map/chain/pallas_call | solution.py:320
  17.2 5.2 %all-to-all-done.got_ref = f32[32,8,128]{2,1,0:T(8,128)S(1)} async-done(((f32[32,8,128]{2,1,0:T(8,128)}), f32[32,8,128]{2,1,0:T(8,128)S(1)}, u32[]{:S(2)}, u32[]{:S(2)}) %all-to-all-start) | async-done | bytes 131104 | tf_op jit(solution)/shard_map/all_to_all | solution.py:317
  22.4 1.1 %meet.1 = (f32[6,6,2,256]{3,2,1,0:T(2,128)}, f32[1,128]{1,0:T(1,128)S(1)}) custom-call(f32[32,8,128]{2,1,0:T(8,128)S(1)} %all-to-all-done.got_ref, bf16[2,192,128]{2,1,0:T(8,128)(2,1)S(1)} %get-tuple-element.11.corner_ref, f32[8,96,256]{2,1,0:T(8,128)S(1)} %get-tuple-element.12.chain_ref), custom_call_target="tpu_custom_call" | custom-call | flops 2000000000 | bytes 1000000 | tf_op jit(solution)/shard_map/meet/pallas_call | solution.py:349
  23.5 38.3 %psum.7.total_ref = f32[1,128]{1,0:T(1,128)S(1)} all-reduce(f32[1,128]{1,0:T(1,128)S(1)} %get-tuple-element.14), channel_id=1, replica_groups=mesh['grp'=1,'zs'=32] {'zs'}, use_global_device_ids=true, to_apply=%region_0.0 | all-reduce | flops 128 | bytes 1024 | tf_op jit(solution)/shard_map/psum | solution.py:361
  61.8 0.6 %final.1 = f32[2,96]{1,0:T(2,128)} custom-call(f32[1,128]{1,0:T(1,128)S(1)} %psum.7.total_ref, s32[8,128]{1,0:T(8,128)S(1)} %get-tuple-element.15.picked_ref), custom_call_target="tpu_custom_call" | custom-call | tf_op jit(solution)/shard_map/final/pallas_call | solution.py:362
Async XLA Ops:
  0.6 13.6 %collective-permute-start.1 = (bf16[6,6,2,256]{3,2,1,0:T(2,128)(2,1)}, bf16[6,6,2,256]{3,2,1,0:T(2,128)(2,1)S(1)}, u32[]{:S(2)}, u32[]{:S(2)}) collective-permute-start(bf16[6,6,2,256]{3,2,1,0:T(2,128)(2,1)} %bitcast.13), channel_id=1, source_target_pairs={{8,0},{9,1},{10,2},{11,3},{12,4},{13,5},{14,6},{15,7},{16,8},{17,9... | collective-permute-start | bytes 110600 | tf_op jit(solution)/shard_map/ppermute | solution.py:28
  5.7 8.5 %collective-permute-start = (bf16[18,6,2,256]{3,2,1,0:T(2,128)(2,1)}, bf16[18,6,2,256]{3,2,1,0:T(2,128)(2,1)S(1)}, u32[]{:S(2)}, u32[]{:S(2)}) collective-permute-start(bf16[18,6,2,256]{3,2,1,0:T(2,128)(2,1)} %bitcast.10), channel_id=1, source_target_pairs={{8,0},{9,1},{10,2},{11,3},{12,4},{13,5},{14,6},{15,7},{16,8},{17,9... | collective-permute-start | bytes 331784 | tf_op jit(solution)/shard_map/ppermute | solution.py:28
  8.0 6.2 %collective-permute-start.2 = (bf16[30,2,256]{2,1,0:T(2,128)(2,1)}, bf16[30,2,256]{2,1,0:T(2,128)(2,1)S(1)}, u32[]{:S(2)}, u32[]{:S(2)}) collective-permute-start(bf16[30,2,256]{2,1,0:T(2,128)(2,1)} %get-tuple-element.10), channel_id=1, source_target_pairs={{16,0},{17,1},{18,2},{19,3},{20,4},{21,5},{22,6},{23,7},{24,8},{25... | collective-permute-start | bytes 92168 | tf_op jit(solution)/shard_map/ppermute | solution.py:28
  8.0 6.3 %copy-start = (bf16[2,3,3,1,6,2,256]{6,5,4,3,2,1,0:T(2,128)(2,1)S(1)}, bf16[2,3,3,1,6,2,256]{6,5,4,3,2,1,0:T(2,128)(2,1)}, u32[]{:S(2)}) copy-start(bf16[2,3,3,1,6,2,256]{6,5,4,3,2,1,0:T(2,128)(2,1)} %param.12) | copy-start | bytes 331780
  8.0 6.3 %copy-start.1 = (bf16[2,3,1,6,2,256]{5,4,3,2,1,0:T(2,128)(2,1)S(1)}, bf16[2,3,1,6,2,256]{5,4,3,2,1,0:T(2,128)(2,1)}, u32[]{:S(2)}) copy-start(bf16[2,3,1,6,2,256]{5,4,3,2,1,0:T(2,128)(2,1)} %param.11) | copy-start | bytes 110596
  8.0 6.3 %copy-start.3 = (s32[1024]{0:T(1024)S(1)}, s32[1024]{0:T(1024)}, u32[]{:S(2)}) copy-start(s32[1024]{0:T(1024)} %param.16) | copy-start | bytes 12292
  8.0 6.3 %copy-start.4 = (s32[1024,1]{0,1:T(1,128)S(1)}, s32[1024,1]{0,1:T(1,128)}, u32[]{:S(2)}) copy-start(s32[1024,1]{0,1:T(1,128)} %param.17) | copy-start | bytes 12292
  8.0 14.4 %all-to-all-start = ((f32[32,8,128]{2,1,0:T(8,128)}), f32[32,8,128]{2,1,0:T(8,128)S(1)}, u32[]{:S(2)}, u32[]{:S(2)}) async-start(f32[32,8,128]{2,1,0:T(8,128)} %get-tuple-element.9), calls=%async_computation | async-start | bytes 262144 | tf_op jit(solution)/shard_map/all_to_all | solution.py:317
  14.2 0.7 %copy-start.2 = (s32[1024]{0:T(1024)S(1)}, s32[1024]{0:T(1024)}, u32[]{:S(2)}) copy-start(s32[1024]{0:T(1024)} %param.15) | copy-start | bytes 12292
  14.2 0.7 %copy-start.5 = (s32[8,3]{0,1:T(4,128)S(1)}, s32[8,3]{0,1:T(4,128)}, u32[]{:S(2)}) copy-start(s32[8,3]{0,1:T(4,128)} %param.14) | copy-start | bytes 292
  14.2 0.7 %copy-start.6 = (f32[8]{0:T(128)S(1)}, f32[8]{0:T(128)}, u32[]{:S(2)}) copy-start(f32[8]{0:T(128)} %weight_ref.1) | copy-start | bytes 100

commit v2 on v1

--- a/solution.py
+++ b/solution.py
@@ -28,6 +28,12 @@
     return lax.ppermute(block, axis, route)
 
 
+def within_group(block, axis, distance):
+    devices = range(lax.axis_size(axis))
+    route = [(i, i // G * G + (i % G + distance) % G) for i in devices]
+    return lax.ppermute(block, axis, route)
+
+
 def split_two(value):
     high = value.astype(BF16)
     return high, (value - high.astype(F32)).astype(BF16)
@@ -37,7 +43,8 @@
     return lax.broadcasted_iota(jnp.int32, shape, axis)
 
 
-def pack_kernel(block_z, block_x, up_ref, down_ref, links_ref, forward_ref, out_ref, edge_ref):
+def pack_kernel(block_z, block_x, up_ref, down_ref, links_ref, forward_ref, *refs):
+    out_refs, edge_ref, result_rows = refs[:G], refs[G], refs[G + 1]
     edge_ref[0:18] = links_ref[:, 0]
     edge_ref[18:24] = forward_ref[:, 0]
     edge_ref[24:30] = forward_ref[:, 1]
@@ -61,7 +68,6 @@
     slot = within // slot_lanes
     cell = within % slot_lanes
     source_row = iota((LANES, 2 * LANES), 0)
-    results = []
     for comp in range(6):
         turned = (slot + 12 - comp - 4 * half) % 6
         source = (cell % zh) * width_x + (block_x * (turned + 4 * half) + cell // zh) % width_x
@@ -77,17 +83,26 @@
         left = jnp.concatenate(rows, axis=0).astype(BF16)
         got = jnp.dot(left, pick, preferred_element_type=F32)
         got = got.reshape(z_blocks, 2, NT, 2 * LANES)
-        results.append(got[:, 0] + got[:, 1])
+        got = got[:, 0] + got[:, 1]
+        result_rows[0, comp] = got[..., :LANES]
+        result_rows[1, comp] = got[..., LANES:]
     one_slot = iota((NT, LANES), 1) // slot_lanes
-    for zb in range(z_blocks):
-        for g in range(G):
-            at = (g // 4) * LANES
-            value = jnp.zeros((NT, LANES), F32)
-            for comp in range(6):
-                value = jnp.where(
-                    one_slot == (comp + g) % 6, results[comp][zb, :, at : at + LANES], value
-                )
-            out_ref[zb * G + g] = value
+    place = lax.axis_index("zs") % G
+    for step in range(G):
+        g = (place + step) % G
+        value = jnp.zeros((z_blocks, NT, LANES), F32)
+        for comp in range(6):
+            mask = (one_slot == (comp + g) % 6)[None]
+            value = jnp.where(mask, result_rows[g // 4, comp], value)
+        out_refs[step][...] = value
+
+
+def regroup_kernel(*refs):
+    z_blocks = refs[0].shape[0]
+    place = lax.axis_index("zs")
+    for j in range(z_blocks):
+        for step in range(G):
+            refs[G + j][(place + G - step) % G] = refs[step][(place // G + j) % z_blocks]
 
 
 def chain_kernel(
@@ -214,9 +229,13 @@
     picked_ref[...] = jnp.where(picked[1:2] > 0.5, lane_of, -1)
 
 
-def meet_kernel(block_z, block_x, got_ref, corner_ref, chain_ref, seq_ref, table_ref):
-    rows_y = got_ref.shape[0] * NT
-    got = got_ref[...].reshape(rows_y, LANES)
+def meet_kernel(block_z, block_x, z_blocks, *refs):
+    corner_ref, chain_ref, seq_ref, table_ref, got_rows = refs[z_blocks:]
+    group = lax.axis_index("zs") // G
+    for j in range(z_blocks):
+        got_rows[(group + z_blocks - j) % z_blocks] = refs[j][...]
+    rows_y = z_blocks * G * NT
+    got = got_rows[...].reshape(rows_y, LANES)
     high, low = split_two(got)
     dot = functools.partial(
         lax.dot_general, dimension_numbers=NT_DIMS, preferred_element_type=F32
@@ -249,8 +268,18 @@
     table_ref[...] = flat
 
 
-def final_kernel(total_ref, picked_ref, out_ref):
-    total = total_ref[...]
+def sum_kernel(*refs):
+    total = refs[0][...]
+    for ref in refs[1:-1]:
+        total = total + ref[...]
+    refs[-1][...] = total
+
+
+def final_kernel(*refs):
+    picked_ref, out_ref = refs[-2:]
+    total = refs[0][...]
+    for ref in refs[1:-2]:
+        total = total + ref[...]
     picked = picked_ref[...]
     value = jnp.take_along_axis(
         jnp.broadcast_to(total, picked.shape), jnp.maximum(picked, 0), axis=1
@@ -292,12 +321,12 @@
 
     links_next = passed_along(links, "zs", -G)
     field_next = passed_along(field, "zs", -G)
-    payload, edge = pl.pallas_call(
+    z_blocks = devices // G
+    part = (z_blocks, NT, LANES)
+    *payload, edge = pl.pallas_call(
         functools.partial(pack_kernel, block_z, block_x),
-        out_shape=(
-            jax.ShapeDtypeStruct((devices, NT, LANES), F32),
-            jax.ShapeDtypeStruct((30, block_x, rows_y), BF16),
-        ),
+        out_shape=(jax.ShapeDtypeStruct(part, F32),) * G
+        + (jax.ShapeDtypeStruct((30, block_x, rows_y), BF16),),
         grid=(1,),
         in_specs=[
             pl.BlockSpec(quark_up.shape, lambda i: (0, 0, 0, 0)),
@@ -305,16 +334,25 @@
             pl.BlockSpec((18, 1, block_x, rows_y), lambda i: (0, 0, 0, 0)),
             pl.BlockSpec((6, 2, block_x, rows_y), lambda i: (0, 0, 0, 0)),
         ],
-        out_specs=(
-            pl.BlockSpec((devices, NT, LANES), lambda i: (0, 0, 0)),
-            pl.BlockSpec((30, block_x, rows_y), lambda i: (0, 0, 0)),
-        ),
+        out_specs=(pl.BlockSpec(part, lambda i: (0, 0, 0)),) * G
+        + (pl.BlockSpec((30, block_x, rows_y), lambda i: (0, 0, 0)),),
+        scratch_shapes=[pltpu.VMEM((2, 6) + part, F32)],
         compiler_params=WIDE_PARAMS,
         cost_estimate=cost(2_000_000_000, 400_000),
         name="pack",
     )(quark_up, quark_down, links, field)
     edge_next = passed_along(edge, "zs", -2 * G)
-    got = lax.all_to_all(payload, "zs", split_axis=0, concat_axis=0, tiled=True)
+    came = [payload[0]] + [within_group(payload[k], "zs", k) for k in range(1, G)]
+    parts = pl.pallas_call(
+        regroup_kernel,
+        out_shape=(jax.ShapeDtypeStruct((G, NT, LANES), F32),) * z_blocks,
+        in_specs=[VMEM] * G,
+        out_specs=(VMEM,) * z_blocks,
+        compiler_params=PARAMS,
+        cost_estimate=cost(500_000_000, 300_000),
+        name="regroup",
+    )(*came)
+    got = [parts[0]] + [passed_along(parts[j], "zs", j * G) for j in range(1, z_blocks)]
 
     requests = (lengths.shape[0] // LANES, LANES)
     chain, corner, picked = pl.pallas_call(
@@ -347,26 +385,36 @@
     )
 
     seq, table = pl.pallas_call(
-        functools.partial(meet_kernel, block_z, block_x),
+        functools.partial(meet_kernel, block_z, block_x, z_blocks),
         out_shape=(
             jax.ShapeDtypeStruct((6, block_z, block_x, rows_y), F32),
             jax.ShapeDtypeStruct((1, LANES), F32),
         ),
-        in_specs=[VMEM] * 3,
+        in_specs=[VMEM] * (z_blocks + 2),
         out_specs=(VMEM, VMEM),
+        scratch_shapes=[pltpu.VMEM((z_blocks, G, NT, LANES), F32)],
         compiler_params=PARAMS,
         cost_estimate=cost(2_000_000_000, 1_000_000),
         name="meet",
-    )(got, corner, chain)
-    total = lax.psum(table, "zs")
+    )(*got, corner, chain)
+    tables = [table] + [within_group(table, "zs", k) for k in range(1, G)]
+    table = pl.pallas_call(
+        sum_kernel,
+        out_shape=jax.ShapeDtypeStruct((1, LANES), F32),
+        in_specs=[VMEM] * G,
+        out_specs=VMEM,
+        compiler_params=PARAMS,
+        name="sum",
+    )(*tables)
+    tables = [table] + [passed_along(table, "zs", j * G) for j in range(1, z_blocks)]
     owned = pl.pallas_call(
         final_kernel,
         out_shape=jax.ShapeDtypeStruct((2, MOST), F32),
-        in_specs=[VMEM] * 2,
+        in_specs=[VMEM] * (z_blocks + 1),
         out_specs=VMEM,
         compiler_params=PARAMS,
         name="final",
-    )(total, picked)
+    )(*tables, picked)
     return (seq.reshape(2, 3, 1, block_z, block_x, rows_y), owned.T)
 
 

time: 62.8 us -> 44.9 us (0.71)
  blocking collectives: 38.3 us -> 0 us
  starting transfers between devices: 11.7 us -> 27.8 us
  waiting for transfers between devices: 5.2 us -> 9.55 us
    psum x1 -> x0, blocking collectives: 38.3 us -> none  [shards(): total = lax.psum(table, 'zs')]
    ppermute x0 -> x14, starting transfers between devices: none -> 13.4 us  [within_group(): return lax.ppermute(block, axis, route)]
    ppermute x3 -> x9, starting transfers between devices: 5.55 us -> 14.4 us  [passed_along(): return lax.ppermute(block, axis, route)]
    all_to_all x1 -> x0, starting transfers between devices: 6.16 us -> none  [shards(): got = lax.all_to_all(payload, 'zs', split_axis=0, concat_axis=0, tiled=True)]
    ppermute x0 -> x14, waiting for transfers between devices: none -> 5.44 us  [within_group(): return lax.ppermute(block, axis, route)]
    all_to_all x1 -> x0, waiting for transfers between devices: 5.19 us -> none  [shards(): got = lax.all_to_all(payload, 'zs', split_axis=0, concat_axis=0, tiled=True)]
    ppermute x3 -> x9, waiting for transfers between devices: 0.01 us -> 4.11 us  [passed_along(): return lax.ppermute(block, axis, route)]
  transfers between devices with their start and end apart: 4 -> 23, of which waited for: 1 -> 9; matrix products, arithmetic and copies ran while one was open for 0% -> 0% of each run, Pallas kernels for 7% -> 9%
where the time goes in v2:
time: 44.9 us; the launch traced here: 44.7 us
  starting transfers between devices  27.8 us (62%)
  waiting for transfers between devices  9.55 us (21%)
  Pallas kernels  5.98 us (13%)
  between operations  0.75 us (2%)
  local copies, waits for them, and re-layouts  0.63 us (1%)
    ppermute x9, starting transfers between devices, passed_along(): return lax.ppermute(block, axis, route)  14.4 us
    ppermute x14, starting transfers between devices, within_group(): return lax.ppermute(block, axis, route)  13.4 us
    ppermute x14, waiting for transfers between devices, within_group(): return lax.ppermute(block, axis, route)  5.44 us
    ppermute x9, waiting for transfers between devices, passed_along(): return lax.ppermute(block, axis, route)  4.11 us
    pallas_call x1, Pallas kernels, shards(): pl.pallas_call(functools.partial(chain_kernel, depth_z, scale, block_z, b...  2.31 us
    pallas_call x1, Pallas kernels, shards(): pl.pallas_call(functools.partial(pack_kernel, block_z, block_x), out_shap...  1.84 us
    pallas_call x1, Pallas kernels, shards(): pl.pallas_call(functools.partial(meet_kernel, block_z, block_x, z_blocks)...  1.11 us
  transfers between devices with their start and end apart: 23, of which 9 were waited for; matrix products, arithmetic and copies ran while one was open for 0% of the time, Pallas kernels for 9%

profile of v2, /device:TPU:0, one launch (start us, length us, event | category | flops | bytes accessed | tf_op | source)
XLA Modules:
  0.0 44.7 jit_solution(1398635663121401283)
XLA Ops:
  0.6 5.1 %collective-permute-start.10 = (bf16[18,6,2,256]{3,2,1,0:T(2,128)(2,1)}, bf16[18,6,2,256]{3,2,1,0:T(2,128)(2,1)S(1)}, u32[]{:S(2)}, u32[]{:S(2)}) collective-permute-start(bf16[18,6,2,256]{3,2,1,0:T(2,128)(2,1)} %bitcast.10), channel_id=1, source_target_pairs={{8,0},{9,1},{10,2},{11,3},{12,4},{13,5},{14,6},{15,7},{16,8},{17,9... | collective-permute-start | bytes 331784 | tf_op jit(solution)/shard_map/ppermute | solution.py:28
  5.7 1.8 %pack.1 = (f32[4,8,128]{2,1,0:T(8,128)}, f32[4,8,128]{2,1,0:T(8,128)}, f32[4,8,128]{2,1,0:T(8,128)}, f32[4,8,128]{2,1,0:T(8,128)}, f32[4,8,128]{2,1,0:T(8,128)},...) custom-call(bf16[2,3,8,384]{3,2,1,0:T(8,128)(2,1)} %up_ref.1, ...), custom_call_target="tpu_custom_call" | custom-call | flops 2000000000 | bytes 400000 | tf_op jit(solution)/shard_map/pack/pallas_call | solution.py:326
  7.6 1.5 %collective-permute-start.1 = (f32[4,8,128]{2,1,0:T(8,128)}, f32[4,8,128]{2,1,0:T(8,128)S(1)}, u32[]{:S(2)}, u32[]{:S(2)}) collective-permute-start(f32[4,8,128]{2,1,0:T(8,128)} %get-tuple-element.22), channel_id=1, source_target_pairs={{0,2},{1,3},{2,4},{3,5},{4,6},{5,7},{6,0},{7,1},{8,10},{9,11},{10,... | collective-permute-start | bytes 49160 | tf_op jit(solution)/shard_map/ppermute | solution.py:34
  9.2 2.4 %collective-permute-start.2 = (f32[4,8,128]{2,1,0:T(8,128)}, f32[4,8,128]{2,1,0:T(8,128)S(1)}, u32[]{:S(2)}, u32[]{:S(2)}) collective-permute-start(f32[4,8,128]{2,1,0:T(8,128)} %get-tuple-element.23), channel_id=1, source_target_pairs={{0,3},{1,4},{2,5},{3,6},{4,7},{5,0},{6,1},{7,2},{8,11},{9,12},{10,... | collective-permute-start | bytes 49160 | tf_op jit(solution)/shard_map/ppermute | solution.py:34
  11.5 0.5 %collective-permute-start.3 = (f32[4,8,128]{2,1,0:T(8,128)}, f32[4,8,128]{2,1,0:T(8,128)S(1)}, u32[]{:S(2)}, u32[]{:S(2)}) collective-permute-start(f32[4,8,128]{2,1,0:T(8,128)} %get-tuple-element.24), channel_id=1, source_target_pairs={{0,4},{1,5},{2,6},{3,7},{4,0},{5,1},{6,2},{7,3},{8,12},{9,13},{10,... | collective-permute-start | bytes 49160 | tf_op jit(solution)/shard_map/ppermute | solution.py:34
  12.2 0.4 collective-permute-done.1.refs_2_
  12.5 1.5 %collective-permute-start.5 = (f32[4,8,128]{2,1,0:T(8,128)}, f32[4,8,128]{2,1,0:T(8,128)S(1)}, u32[]{:S(2)}, u32[]{:S(2)}) collective-permute-start(f32[4,8,128]{2,1,0:T(8,128)} %get-tuple-element.26), channel_id=1, source_target_pairs={{0,6},{1,7},{2,0},{3,1},{4,2},{5,3},{6,4},{7,5},{8,14},{9,15},{10,... | collective-permute-start | bytes 49160 | tf_op jit(solution)/shard_map/ppermute | solution.py:34
  14.1 1.8 %collective-permute-start.6 = (f32[4,8,128]{2,1,0:T(8,128)}, f32[4,8,128]{2,1,0:T(8,128)S(1)}, u32[]{:S(2)}, u32[]{:S(2)}) collective-permute-start(f32[4,8,128]{2,1,0:T(8,128)} %get-tuple-element.27), channel_id=1, source_target_pairs={{0,7},{1,0},{2,1},{3,2},{4,3},{5,4},{6,5},{7,6},{8,15},{9,8},{10,9... | collective-permute-start | bytes 49160 | tf_op jit(solution)/shard_map/ppermute | solution.py:34
  15.9 0.5 %collective-permute-start.11 = (bf16[6,6,2,256]{3,2,1,0:T(2,128)(2,1)S(1)}, bf16[6,6,2,256]{3,2,1,0:T(2,128)(2,1)S(1)}, u32[]{:S(2)}, u32[]{:S(2)}) collective-permute-start(bf16[6,6,2,256]{3,2,1,0:T(2,128)(2,1)S(1)} %bitcast.14), channel_id=1, source_target_pairs={{8,0},{9,1},{10,2},{11,3},{12,4},{13,5},{14,6},{15,7},{16,8},{17,9... | collective-permute-start | bytes 110600 | tf_op jit(solution)/shard_map/ppermute | solution.py:28
  16.4 0.2 collective-permute-done.5.refs_6_
  16.6 1.0 %collective-permute-done.6.refs_7_ = f32[4,8,128]{2,1,0:T(8,128)S(1)} collective-permute-done((f32[4,8,128]{2,1,0:T(8,128)}, f32[4,8,128]{2,1,0:T(8,128)S(1)}, u32[]{:S(2)}, u32[]{:S(2)}) %collective-permute-start.6) | collective-permute-done | bytes 16416 | tf_op jit(solution)/shard_map/ppermute | solution.py:34
  17.6 0.5 %collective-permute-start.7 = (f32[8,8,128]{2,1,0:T(8,128)S(1)}, f32[8,8,128]{2,1,0:T(8,128)S(1)}, u32[]{:S(2)}, u32[]{:S(2)}) collective-permute-start(f32[8,8,128]{2,1,0:T(8,128)S(1)} %get-tuple-element.29), channel_id=1, source_target_pairs={{24,0},{25,1},{26,2},{27,3},{28,4},{29,5},{30,6},{31,7},{0,8},{1,9... | collective-permute-start | bytes 98312 | tf_op jit(solution)/shard_map/ppermute | solution.py:28
  18.1 2.9 %collective-permute-start.8 = (f32[8,8,128]{2,1,0:T(8,128)S(1)}, f32[8,8,128]{2,1,0:T(8,128)S(1)}, u32[]{:S(2)}, u32[]{:S(2)}) collective-permute-start(f32[8,8,128]{2,1,0:T(8,128)S(1)} %get-tuple-element.30), channel_id=1, source_target_pairs={{16,0},{17,1},{18,2},{19,3},{20,4},{21,5},{22,6},{23,7},{24,8},{25... | collective-permute-start | bytes 98312 | tf_op jit(solution)/shard_map/ppermute | solution.py:28
  21.0 0.3 collective-permute-done.12.edge_ref
  21.4 1.7 %collective-permute-start.9 = (f32[8,8,128]{2,1,0:T(8,128)S(1)}, f32[8,8,128]{2,1,0:T(8,128)S(1)}, u32[]{:S(2)}, u32[]{:S(2)}) collective-permute-start(f32[8,8,128]{2,1,0:T(8,128)S(1)} %get-tuple-element.31), channel_id=1, source_target_pairs={{8,0},{9,1},{10,2},{11,3},{12,4},{13,5},{14,6},{15,7},{16,8},{17,9... | collective-permute-start | bytes 98312 | tf_op jit(solution)/shard_map/ppermute | solution.py:28
  23.2 0.6 %copy-done.6 = f32[8]{0:T(128)S(1)} copy-done((f32[8]{0:T(128)S(1)}, f32[8]{0:T(128)}, u32[]{:S(2)}) %copy-start.6) | copy-done | bytes 56
  23.8 2.3 %chain.1 = (f32[8,96,256]{2,1,0:T(8,128)S(1)}, bf16[2,192,128]{2,1,0:T(8,128)(2,1)S(1)}, s32[8,128]{1,0:T(8,128)S(1)}) custom-call(f32[8]{0:T(128)S(1)} %copy-done.6, s32[3,8]{1,0:T(4,128)S(1)} %bitcast.19, bf16[18,6,2,256]{3,2,1,0:T(2,128)(2,1)S(1)} %bitcast.12, bf16[18,6,2,256]{3,2,1,0:T(2,128)(2,1)S(1)} %collective-permute-done.10.links_next_ref, ...), custom_call_target="tpu_custom_call" | custom-call | flops 3000000000 | bytes 2000000 | tf_op jit(solution)/shard_map/chain/pallas_call | solution.py:358
  26.1 1.1 %meet.1 = (f32[6,6,2,256]{3,2,1,0:T(2,128)}, f32[1,128]{1,0:T(1,128)S(1)}) custom-call(f32[8,8,128]{2,1,0:T(8,128)S(1)} %get-tuple-element.28.refs_0_, f32[8,8,128]{2,1,0:T(8,128)S(1)} %collective-permute-done.7.refs_1_, f32[8,8,128]{2,1,0:T(8,128)S(1)} %collective-permute-done.8.refs_2_, f32[8,8,128]{2,1,0:T(8,128)S(1)} %collective-permute-done.9.refs_3_, ...), custom_call_target="tpu_custom_call" | custom-call | flops 2000000000 | bytes 1000000 | tf_op jit(solution)/shard_map/meet/pallas_call | solution.py:387
  27.2 0.6 %collective-permute-start.19 = (f32[1,128]{1,0:T(1,128)S(1)}, f32[1,128]{1,0:T(1,128)S(1)}, u32[]{:S(2)}, u32[]{:S(2)}) collective-permute-start(f32[1,128]{1,0:T(1,128)S(1)} %get-tuple-element.36.refs_0_), channel_id=1, source_target_pairs={{0,7},{1,0},{2,1},{3,2},{4,3},{5,4},{6,5},{7,6},{8,15},{9,8},{10,9... | collective-permute-start | bytes 1544 | tf_op jit(solution)/shard_map/ppermute | solution.py:34
  27.8 0.2 collective-permute-start.18
  28.0 1.4 %collective-permute-start.17 = (f32[1,128]{1,0:T(1,128)S(1)}, f32[1,128]{1,0:T(1,128)S(1)}, u32[]{:S(2)}, u32[]{:S(2)}) collective-permute-start(f32[1,128]{1,0:T(1,128)S(1)} %get-tuple-element.36.refs_0_), channel_id=1, source_target_pairs={{0,5},{1,6},{2,7},{3,0},{4,1},{5,2},{6,3},{7,4},{8,13},{9,14},{10,... | collective-permute-start | bytes 1544 | tf_op jit(solution)/shard_map/ppermute | solution.py:34
  29.4 0.5 %collective-permute-start.16 = (f32[1,128]{1,0:T(1,128)S(1)}, f32[1,128]{1,0:T(1,128)S(1)}, u32[]{:S(2)}, u32[]{:S(2)}) collective-permute-start(f32[1,128]{1,0:T(1,128)S(1)} %get-tuple-element.36.refs_0_), channel_id=1, source_target_pairs={{0,4},{1,5},{2,6},{3,7},{4,0},{5,1},{6,2},{7,3},{8,12},{9,13},{10,... | collective-permute-start | bytes 1544 | tf_op jit(solution)/shard_map/ppermute | solution.py:34
  29.9 1.2 %collective-permute-start.15 = (f32[1,128]{1,0:T(1,128)S(1)}, f32[1,128]{1,0:T(1,128)S(1)}, u32[]{:S(2)}, u32[]{:S(2)}) collective-permute-start(f32[1,128]{1,0:T(1,128)S(1)} %get-tuple-element.36.refs_0_), channel_id=1, source_target_pairs={{0,3},{1,4},{2,5},{3,6},{4,7},{5,0},{6,1},{7,2},{8,11},{9,12},{10,... | collective-permute-start | bytes 1544 | tf_op jit(solution)/shard_map/ppermute | solution.py:34
  31.1 1.6 %collective-permute-start.14 = (f32[1,128]{1,0:T(1,128)S(1)}, f32[1,128]{1,0:T(1,128)S(1)}, u32[]{:S(2)}, u32[]{:S(2)}) collective-permute-start(f32[1,128]{1,0:T(1,128)S(1)} %get-tuple-element.36.refs_0_), channel_id=1, source_target_pairs={{0,2},{1,3},{2,4},{3,5},{4,6},{5,7},{6,0},{7,1},{8,10},{9,11},{10,... | collective-permute-start | bytes 1544 | tf_op jit(solution)/shard_map/ppermute | solution.py:34
  32.7 0.3 collective-permute-done.16.refs_4_
  33.0 2.5 %collective-permute-done.14.refs_2_ = f32[1,128]{1,0:T(1,128)S(1)} collective-permute-done((f32[1,128]{1,0:T(1,128)S(1)}, f32[1,128]{1,0:T(1,128)S(1)}, u32[]{:S(2)}, u32[]{:S(2)}) %collective-permute-start.14) | collective-permute-done | bytes 544 | tf_op jit(solution)/shard_map/ppermute | solution.py:34
  35.5 1.0 %collective-permute-done.13.refs_1_ = f32[1,128]{1,0:T(1,128)S(1)} collective-permute-done((f32[1,128]{1,0:T(1,128)S(1)}, f32[1,128]{1,0:T(1,128)S(1)}, u32[]{:S(2)}, u32[]{:S(2)}) %collective-permute-start.13) | collective-permute-done | bytes 544 | tf_op jit(solution)/shard_map/ppermute | solution.py:34
  36.6 2.2 %collective-permute-start.22 = (f32[1,128]{1,0:T(1,128)S(1)}, f32[1,128]{1,0:T(1,128)S(1)}, u32[]{:S(2)}, u32[]{:S(2)}) collective-permute-start(f32[1,128]{1,0:T(1,128)S(1)} %sum.1.refs_0_), channel_id=1, source_target_pairs={{8,0},{9,1},{10,2},{11,3},{12,4},{13,5},{14,6},{15,7},{16,8},{17,9... | collective-permute-start | bytes 1544 | tf_op jit(solution)/shard_map/ppermute | solution.py:28
  38.7 1.6 %collective-permute-start.20 = (f32[1,128]{1,0:T(1,128)S(1)}, f32[1,128]{1,0:T(1,128)S(1)}, u32[]{:S(2)}, u32[]{:S(2)}) collective-permute-start(f32[1,128]{1,0:T(1,128)S(1)} %sum.1.refs_0_), channel_id=1, source_target_pairs={{24,0},{25,1},{26,2},{27,3},{28,4},{29,5},{30,6},{31,7},{0,8},{1,9... | collective-permute-start | bytes 1544 | tf_op jit(solution)/shard_map/ppermute | solution.py:28
  40.3 2.9 %collective-permute-done.21.refs_2_ = f32[1,128]{1,0:T(1,128)S(1)} collective-permute-done((f32[1,128]{1,0:T(1,128)S(1)}, f32[1,128]{1,0:T(1,128)S(1)}, u32[]{:S(2)}, u32[]{:S(2)}) %collective-permute-start.21) | collective-permute-done | bytes 544 | tf_op jit(solution)/shard_map/ppermute | solution.py:28
  43.2 0.9 %collective-permute-done.20.refs_1_ = f32[1,128]{1,0:T(1,128)S(1)} collective-permute-done((f32[1,128]{1,0:T(1,128)S(1)}, f32[1,128]{1,0:T(1,128)S(1)}, u32[]{:S(2)}, u32[]{:S(2)}) %collective-permute-start.20) | collective-permute-done | bytes 544 | tf_op jit(solution)/shard_map/ppermute | solution.py:28
  44.1 0.6 %final.1 = f32[2,96]{1,0:T(2,128)} custom-call(f32[1,128]{1,0:T(1,128)S(1)} %sum.1.refs_0_, f32[1,128]{1,0:T(1,128)S(1)} %collective-permute-done.20.refs_1_, f32[1,128]{1,0:T(1,128)S(1)} %collective-permute-done.21.refs_2_, f32[1,128]{1,0:T(1,128)S(1)} %collective-permute-done.22.refs_3_, s32[8,128]{1,0:T(8,128)S(1)} %get-tuple-element.37.refs_4_), custom_call_target="tpu_custom_call" | custom-call | tf_op jit(solution)/shard_map/final/pallas_call | solution.py:410
  (36 shorter events, 0.3 us)
Async XLA Ops:
  0.6 22.5 %collective-permute-start.10 = (bf16[18,6,2,256]{3,2,1,0:T(2,128)(2,1)}, bf16[18,6,2,256]{3,2,1,0:T(2,128)(2,1)S(1)}, u32[]{:S(2)}, u32[]{:S(2)}) collective-permute-start(bf16[18,6,2,256]{3,2,1,0:T(2,128)(2,1)} %bitcast.10), channel_id=1, source_target_pairs={{8,0},{9,1},{10,2},{11,3},{12,4},{13,5},{14,6},{15,7},{16,8},{17,9... | collective-permute-start | bytes 331784 | tf_op jit(solution)/shard_map/ppermute | solution.py:28
  5.7 10.2 %copy-start.1 = (bf16[2,3,1,6,2,256]{5,4,3,2,1,0:T(2,128)(2,1)S(1)}, bf16[2,3,1,6,2,256]{5,4,3,2,1,0:T(2,128)(2,1)}, u32[]{:S(2)}) copy-start(bf16[2,3,1,6,2,256]{5,4,3,2,1,0:T(2,128)(2,1)} %param.11) | copy-start | bytes 110596
  7.6 10.0 %copy-start.7 = (f32[4,8,128]{2,1,0:T(8,128)S(1)}, f32[4,8,128]{2,1,0:T(8,128)}, u32[]{:S(2)}) copy-start(f32[4,8,128]{2,1,0:T(8,128)} %get-tuple-element.20.refs_0_) | copy-start | bytes 49156
  7.6 4.5 %collective-permute-start = (f32[4,8,128]{2,1,0:T(8,128)}, f32[4,8,128]{2,1,0:T(8,128)S(1)}, u32[]{:S(2)}, u32[]{:S(2)}) collective-permute-start(f32[4,8,128]{2,1,0:T(8,128)} %get-tuple-element.21), channel_id=1, source_target_pairs={{0,1},{1,2},{2,3},{3,4},{4,5},{5,6},{6,7},{7,0},{8,9},{9,10},{10,1... | collective-permute-start | bytes 49160 | tf_op jit(solution)/shard_map/ppermute | solution.py:34
  7.6 4.9 %collective-permute-start.1 = (f32[4,8,128]{2,1,0:T(8,128)}, f32[4,8,128]{2,1,0:T(8,128)S(1)}, u32[]{:S(2)}, u32[]{:S(2)}) collective-permute-start(f32[4,8,128]{2,1,0:T(8,128)} %get-tuple-element.22), channel_id=1, source_target_pairs={{0,2},{1,3},{2,4},{3,5},{4,6},{5,7},{6,0},{7,1},{8,10},{9,11},{10,... | collective-permute-start | bytes 49160 | tf_op jit(solution)/shard_map/ppermute | solution.py:34
  9.2 4.9 %collective-permute-start.2 = (f32[4,8,128]{2,1,0:T(8,128)}, f32[4,8,128]{2,1,0:T(8,128)S(1)}, u32[]{:S(2)}, u32[]{:S(2)}) collective-permute-start(f32[4,8,128]{2,1,0:T(8,128)} %get-tuple-element.23), channel_id=1, source_target_pairs={{0,3},{1,4},{2,5},{3,6},{4,7},{5,0},{6,1},{7,2},{8,11},{9,12},{10,... | collective-permute-start | bytes 49160 | tf_op jit(solution)/shard_map/ppermute | solution.py:34
  11.5 4.4 %collective-permute-start.3 = (f32[4,8,128]{2,1,0:T(8,128)}, f32[4,8,128]{2,1,0:T(8,128)S(1)}, u32[]{:S(2)}, u32[]{:S(2)}) collective-permute-start(f32[4,8,128]{2,1,0:T(8,128)} %get-tuple-element.24), channel_id=1, source_target_pairs={{0,4},{1,5},{2,6},{3,7},{4,0},{5,1},{6,2},{7,3},{8,12},{9,13},{10,... | collective-permute-start | bytes 49160 | tf_op jit(solution)/shard_map/ppermute | solution.py:34
  12.0 4.3 %collective-permute-start.4 = (f32[4,8,128]{2,1,0:T(8,128)}, f32[4,8,128]{2,1,0:T(8,128)S(1)}, u32[]{:S(2)}, u32[]{:S(2)}) collective-permute-start(f32[4,8,128]{2,1,0:T(8,128)} %get-tuple-element.25), channel_id=1, source_target_pairs={{0,5},{1,6},{2,7},{3,0},{4,1},{5,2},{6,3},{7,4},{8,13},{9,14},{10,... | collective-permute-start | bytes 49160 | tf_op jit(solution)/shard_map/ppermute | solution.py:34
  12.5 4.0 %collective-permute-start.5 = (f32[4,8,128]{2,1,0:T(8,128)}, f32[4,8,128]{2,1,0:T(8,128)S(1)}, u32[]{:S(2)}, u32[]{:S(2)}) collective-permute-start(f32[4,8,128]{2,1,0:T(8,128)} %get-tuple-element.26), channel_id=1, source_target_pairs={{0,6},{1,7},{2,0},{3,1},{4,2},{5,3},{6,4},{7,5},{8,14},{9,15},{10,... | collective-permute-start | bytes 49160 | tf_op jit(solution)/shard_map/ppermute | solution.py:34
  14.1 3.5 %collective-permute-start.6 = (f32[4,8,128]{2,1,0:T(8,128)}, f32[4,8,128]{2,1,0:T(8,128)S(1)}, u32[]{:S(2)}, u32[]{:S(2)}) collective-permute-start(f32[4,8,128]{2,1,0:T(8,128)} %get-tuple-element.27), channel_id=1, source_target_pairs={{0,7},{1,0},{2,1},{3,2},{4,3},{5,4},{6,5},{7,6},{8,15},{9,8},{10,9... | collective-permute-start | bytes 49160 | tf_op jit(solution)/shard_map/ppermute | solution.py:34
  15.9 7.2 %collective-permute-start.11 = (bf16[6,6,2,256]{3,2,1,0:T(2,128)(2,1)S(1)}, bf16[6,6,2,256]{3,2,1,0:T(2,128)(2,1)S(1)}, u32[]{:S(2)}, u32[]{:S(2)}) collective-permute-start(bf16[6,6,2,256]{3,2,1,0:T(2,128)(2,1)S(1)} %bitcast.14), channel_id=1, source_target_pairs={{8,0},{9,1},{10,2},{11,3},{12,4},{13,5},{14,6},{15,7},{16,8},{17,9... | collective-permute-start | bytes 110600 | tf_op jit(solution)/shard_map/ppermute | solution.py:28
  16.4 5.0 %collective-permute-start.12 = (bf16[30,2,256]{2,1,0:T(2,128)(2,1)}, bf16[30,2,256]{2,1,0:T(2,128)(2,1)S(1)}, u32[]{:S(2)}, u32[]{:S(2)}) collective-permute-start(bf16[30,2,256]{2,1,0:T(2,128)(2,1)} %get-tuple-element.32), channel_id=1, source_target_pairs={{16,0},{17,1},{18,2},{19,3},{20,4},{21,5},{22,6},{23,7},{24,8},{25... | collective-permute-start | bytes 92168 | tf_op jit(solution)/shard_map/ppermute | solution.py:28
  17.6 5.6 %copy-start = (bf16[2,3,3,1,6,2,256]{6,5,4,3,2,1,0:T(2,128)(2,1)S(1)}, bf16[2,3,3,1,6,2,256]{6,5,4,3,2,1,0:T(2,128)(2,1)}, u32[]{:S(2)}) copy-start(bf16[2,3,3,1,6,2,256]{6,5,4,3,2,1,0:T(2,128)(2,1)} %param.12) | copy-start | bytes 331780
  17.6 5.6 %copy-start.4 = (s32[1024,1]{0,1:T(1,128)S(1)}, s32[1024,1]{0,1:T(1,128)}, u32[]{:S(2)}) copy-start(s32[1024,1]{0,1:T(1,128)} %param.17) | copy-start | bytes 12292
  17.6 5.6 %copy-start.5 = (s32[8,3]{0,1:T(4,128)S(1)}, s32[8,3]{0,1:T(4,128)}, u32[]{:S(2)}) copy-start(s32[8,3]{0,1:T(4,128)} %param.14) | copy-start | bytes 292
  17.6 8.5 %collective-permute-start.7 = (f32[8,8,128]{2,1,0:T(8,128)S(1)}, f32[8,8,128]{2,1,0:T(8,128)S(1)}, u32[]{:S(2)}, u32[]{:S(2)}) collective-permute-start(f32[8,8,128]{2,1,0:T(8,128)S(1)} %get-tuple-element.29), channel_id=1, source_target_pairs={{24,0},{25,1},{26,2},{27,3},{28,4},{29,5},{30,6},{31,7},{0,8},{1,9... | collective-permute-start | bytes 98312 | tf_op jit(solution)/shard_map/ppermute | solution.py:28
  18.1 8.0 %collective-permute-start.8 = (f32[8,8,128]{2,1,0:T(8,128)S(1)}, f32[8,8,128]{2,1,0:T(8,128)S(1)}, u32[]{:S(2)}, u32[]{:S(2)}) collective-permute-start(f32[8,8,128]{2,1,0:T(8,128)S(1)} %get-tuple-element.30), channel_id=1, source_target_pairs={{16,0},{17,1},{18,2},{19,3},{20,4},{21,5},{22,6},{23,7},{24,8},{25... | collective-permute-start | bytes 98312 | tf_op jit(solution)/shard_map/ppermute | solution.py:28
  21.4 1.8 %copy-start.3 = (s32[1024]{0:T(1024)S(1)}, s32[1024]{0:T(1024)}, u32[]{:S(2)}) copy-start(s32[1024]{0:T(1024)} %param.16) | copy-start | bytes 12292
  21.4 1.8 %copy-start.2 = (s32[1024]{0:T(1024)S(1)}, s32[1024]{0:T(1024)}, u32[]{:S(2)}) copy-start(s32[1024]{0:T(1024)} %param.15) | copy-start | bytes 12292
  21.4 4.8 %collective-permute-start.9 = (f32[8,8,128]{2,1,0:T(8,128)S(1)}, f32[8,8,128]{2,1,0:T(8,128)S(1)}, u32[]{:S(2)}, u32[]{:S(2)}) collective-permute-start(f32[8,8,128]{2,1,0:T(8,128)S(1)} %get-tuple-element.31), channel_id=1, source_target_pairs={{8,0},{9,1},{10,2},{11,3},{12,4},{13,5},{14,6},{15,7},{16,8},{17,9... | collective-permute-start | bytes 98312 | tf_op jit(solution)/shard_map/ppermute | solution.py:28
  23.1 0.7 %copy-start.6 = (f32[8]{0:T(128)S(1)}, f32[8]{0:T(128)}, u32[]{:S(2)}) copy-start(f32[8]{0:T(128)} %weight_ref.1) | copy-start | bytes 100
  27.2 3.8 %collective-permute-start.19 = (f32[1,128]{1,0:T(1,128)S(1)}, f32[1,128]{1,0:T(1,128)S(1)}, u32[]{:S(2)}, u32[]{:S(2)}) collective-permute-start(f32[1,128]{1,0:T(1,128)S(1)} %get-tuple-element.36.refs_0_), channel_id=1, source_target_pairs={{0,7},{1,0},{2,1},{3,2},{4,3},{5,4},{6,5},{7,6},{8,15},{9,8},{10,9... | collective-permute-start | bytes 1544 | tf_op jit(solution)/shard_map/ppermute | solution.py:34
  27.8 4.9 %collective-permute-start.18 = (f32[1,128]{1,0:T(1,128)S(1)}, f32[1,128]{1,0:T(1,128)S(1)}, u32[]{:S(2)}, u32[]{:S(2)}) collective-permute-start(f32[1,128]{1,0:T(1,128)S(1)} %get-tuple-element.36.refs_0_), channel_id=1, source_target_pairs={{0,6},{1,7},{2,0},{3,1},{4,2},{5,3},{6,4},{7,5},{8,14},{9,15},{10,... | collective-permute-start | bytes 1544 | tf_op jit(solution)/shard_map/ppermute | solution.py:34
  28.0 4.7 %collective-permute-start.17 = (f32[1,128]{1,0:T(1,128)S(1)}, f32[1,128]{1,0:T(1,128)S(1)}, u32[]{:S(2)}, u32[]{:S(2)}) collective-permute-start(f32[1,128]{1,0:T(1,128)S(1)} %get-tuple-element.36.refs_0_), channel_id=1, source_target_pairs={{0,5},{1,6},{2,7},{3,0},{4,1},{5,2},{6,3},{7,4},{8,13},{9,14},{10,... | collective-permute-start | bytes 1544 | tf_op jit(solution)/shard_map/ppermute | solution.py:34
  29.4 3.5 %collective-permute-start.16 = (f32[1,128]{1,0:T(1,128)S(1)}, f32[1,128]{1,0:T(1,128)S(1)}, u32[]{:S(2)}, u32[]{:S(2)}) collective-permute-start(f32[1,128]{1,0:T(1,128)S(1)} %get-tuple-element.36.refs_0_), channel_id=1, source_target_pairs={{0,4},{1,5},{2,6},{3,7},{4,0},{5,1},{6,2},{7,3},{8,12},{9,13},{10,... | collective-permute-start | bytes 1544 | tf_op jit(solution)/shard_map/ppermute | solution.py:34
  29.9 3.1 %collective-permute-start.15 = (f32[1,128]{1,0:T(1,128)S(1)}, f32[1,128]{1,0:T(1,128)S(1)}, u32[]{:S(2)}, u32[]{:S(2)}) collective-permute-start(f32[1,128]{1,0:T(1,128)S(1)} %get-tuple-element.36.refs_0_), channel_id=1, source_target_pairs={{0,3},{1,4},{2,5},{3,6},{4,7},{5,0},{6,1},{7,2},{8,11},{9,12},{10,... | collective-permute-start | bytes 1544 | tf_op jit(solution)/shard_map/ppermute | solution.py:34
  31.1 4.4 %collective-permute-start.14 = (f32[1,128]{1,0:T(1,128)S(1)}, f32[1,128]{1,0:T(1,128)S(1)}, u32[]{:S(2)}, u32[]{:S(2)}) collective-permute-start(f32[1,128]{1,0:T(1,128)S(1)} %get-tuple-element.36.refs_0_), channel_id=1, source_target_pairs={{0,2},{1,3},{2,4},{3,5},{4,6},{5,7},{6,0},{7,1},{8,10},{9,11},{10,... | collective-permute-start | bytes 1544 | tf_op jit(solution)/shard_map/ppermute | solution.py:34
  32.7 3.9 %collective-permute-start.13 = (f32[1,128]{1,0:T(1,128)S(1)}, f32[1,128]{1,0:T(1,128)S(1)}, u32[]{:S(2)}, u32[]{:S(2)}) collective-permute-start(f32[1,128]{1,0:T(1,128)S(1)} %get-tuple-element.36.refs_0_), channel_id=1, source_target_pairs={{0,1},{1,2},{2,3},{3,4},{4,5},{5,6},{6,7},{7,0},{8,9},{9,10},{10,1... | collective-permute-start | bytes 1544 | tf_op jit(solution)/shard_map/ppermute | solution.py:34
  36.6 3.7 %collective-permute-start.22 = (f32[1,128]{1,0:T(1,128)S(1)}, f32[1,128]{1,0:T(1,128)S(1)}, u32[]{:S(2)}, u32[]{:S(2)}) collective-permute-start(f32[1,128]{1,0:T(1,128)S(1)} %sum.1.refs_0_), channel_id=1, source_target_pairs={{8,0},{9,1},{10,2},{11,3},{12,4},{13,5},{14,6},{15,7},{16,8},{17,9... | collective-permute-start | bytes 1544 | tf_op jit(solution)/shard_map/ppermute | solution.py:28
  38.7 4.4 %collective-permute-start.21 = (f32[1,128]{1,0:T(1,128)S(1)}, f32[1,128]{1,0:T(1,128)S(1)}, u32[]{:S(2)}, u32[]{:S(2)}) collective-permute-start(f32[1,128]{1,0:T(1,128)S(1)} %sum.1.refs_0_), channel_id=1, source_target_pairs={{16,0},{17,1},{18,2},{19,3},{20,4},{21,5},{22,6},{23,7},{24,8},{25... | collective-permute-start | bytes 1544 | tf_op jit(solution)/shard_map/ppermute | solution.py:28
  38.7 5.3 %collective-permute-start.20 = (f32[1,128]{1,0:T(1,128)S(1)}, f32[1,128]{1,0:T(1,128)S(1)}, u32[]{:S(2)}, u32[]{:S(2)}) collective-permute-start(f32[1,128]{1,0:T(1,128)S(1)} %sum.1.refs_0_), channel_id=1, source_target_pairs={{24,0},{25,1},{26,2},{27,3},{28,4},{29,5},{30,6},{31,7},{0,8},{1,9... | collective-permute-start | bytes 1544 | tf_op jit(solution)/shard_map/ppermute | solution.py:28

commit v3 on v1

--- a/solution.py
+++ b/solution.py
@@ -26,6 +26,18 @@
     devices = range(lax.axis_size(axis))
     route = [((i - distance) % len(devices), i) for i in devices]
     return lax.ppermute(block, axis, route)
+
+
+def swapped_within(block, axis):
+    count = lax.axis_size(axis)
+    groups = [[first + k for k in range(G)] for first in range(0, count, G)]
+    return lax.all_to_all(block, axis, 0, 0, tiled=True, axis_index_groups=groups)
+
+
+def swapped_between(block, axis):
+    count = lax.axis_size(axis)
+    groups = [list(range(first, count, G)) for first in range(G)]
+    return lax.all_to_all(block, axis, 0, 0, tiled=True, axis_index_groups=groups)
 
 
 def split_two(value):
@@ -87,7 +99,13 @@
                 value = jnp.where(
                     one_slot == (comp + g) % 6, results[comp][zb, :, at : at + LANES], value
                 )
-            out_ref[zb * G + g] = value
+            out_ref[g, zb] = value
+
+
+def regroup_kernel(came_ref, out_ref):
+    for g in range(came_ref.shape[0]):
+        for zb in range(came_ref.shape[1]):
+            out_ref[zb, g] = came_ref[g, zb]
 
 
 def chain_kernel(
@@ -246,11 +264,16 @@
         table = table + pltpu.roll(table, shift, 1)
     mine = iota((2 * LMAX, LANES), 1) // NT == iota((2 * LMAX, LANES), 0)
     flat = jnp.sum(jnp.where(mine, table, 0.0), axis=0, keepdims=True)
-    table_ref[...] = flat
-
-
-def final_kernel(total_ref, picked_ref, out_ref):
-    total = total_ref[...]
+    table_ref[...] = jnp.broadcast_to(flat, table_ref.shape)
+
+
+def sum_kernel(tables_ref, out_ref):
+    total = jnp.sum(tables_ref[...], axis=0, keepdims=True)
+    out_ref[...] = jnp.broadcast_to(total, out_ref.shape)
+
+
+def final_kernel(tables_ref, picked_ref, out_ref):
+    total = jnp.sum(tables_ref[...], axis=0, keepdims=True)
     picked = picked_ref[...]
     value = jnp.take_along_axis(
         jnp.broadcast_to(total, picked.shape), jnp.maximum(picked, 0), axis=1
@@ -292,10 +315,11 @@
 
     links_next = passed_along(links, "zs", -G)
     field_next = passed_along(field, "zs", -G)
+    z_blocks = devices // G
     payload, edge = pl.pallas_call(
         functools.partial(pack_kernel, block_z, block_x),
         out_shape=(
-            jax.ShapeDtypeStruct((devices, NT, LANES), F32),
+            jax.ShapeDtypeStruct((G, z_blocks, NT, LANES), F32),
             jax.ShapeDtypeStruct((30, block_x, rows_y), BF16),
         ),
         grid=(1,),
@@ -306,7 +330,7 @@
             pl.BlockSpec((6, 2, block_x, rows_y), lambda i: (0, 0, 0, 0)),
         ],
         out_specs=(
-            pl.BlockSpec((devices, NT, LANES), lambda i: (0, 0, 0)),
+            pl.BlockSpec((G, z_blocks, NT, LANES), lambda i: (0, 0, 0, 0)),
             pl.BlockSpec((30, block_x, rows_y), lambda i: (0, 0, 0)),
         ),
         compiler_params=WIDE_PARAMS,
@@ -314,7 +338,16 @@
         name="pack",
     )(quark_up, quark_down, links, field)
     edge_next = passed_along(edge, "zs", -2 * G)
-    got = lax.all_to_all(payload, "zs", split_axis=0, concat_axis=0, tiled=True)
+    parts = pl.pallas_call(
+        regroup_kernel,
+        out_shape=jax.ShapeDtypeStruct((z_blocks, G, NT, LANES), F32),
+        in_specs=[VMEM],
+        out_specs=VMEM,
+        compiler_params=PARAMS,
+        cost_estimate=cost(500_000_000, 300_000),
+        name="regroup",
+    )(swapped_within(payload, "zs"))
+    got = swapped_between(parts, "zs").reshape(devices, NT, LANES)
 
     requests = (lengths.shape[0] // LANES, LANES)
     chain, corner, picked = pl.pallas_call(
@@ -350,7 +383,7 @@
         functools.partial(meet_kernel, block_z, block_x),
         out_shape=(
             jax.ShapeDtypeStruct((6, block_z, block_x, rows_y), F32),
-            jax.ShapeDtypeStruct((1, LANES), F32),
+            jax.ShapeDtypeStruct((G, LANES), F32),
         ),
         in_specs=[VMEM] * 3,
         out_specs=(VMEM, VMEM),
@@ -358,7 +391,16 @@
         cost_estimate=cost(2_000_000_000, 1_000_000),
         name="meet",
     )(got, corner, chain)
-    total = lax.psum(table, "zs")
+    tables = swapped_within(table.reshape(G, 1, LANES), "zs").reshape(G, LANES)
+    table = pl.pallas_call(
+        sum_kernel,
+        out_shape=jax.ShapeDtypeStruct((z_blocks, LANES), F32),
+        in_specs=[VMEM],
+        out_specs=VMEM,
+        compiler_params=PARAMS,
+        name="sum",
+    )(tables)
+    tables = swapped_between(table.reshape(z_blocks, 1, LANES), "zs").reshape(z_blocks, LANES)
     owned = pl.pallas_call(
         final_kernel,
         out_shape=jax.ShapeDtypeStruct((2, MOST), F32),
@@ -366,7 +408,7 @@
         out_specs=VMEM,
         compiler_params=PARAMS,
         name="final",
-    )(total, picked)
+    )(tables, picked)
     return (seq.reshape(2, 3, 1, block_z, block_x, rows_y), owned.T)
 
 

time: 62.8 us -> 42.6 us (0.68)
  blocking collectives: 38.3 us -> 15.4 us
  starting transfers between devices: 11.7 us -> 14.4 us
  waiting for transfers between devices: 5.2 us -> 4.48 us
  Pallas kernels: 5.79 us -> 6.45 us
    psum x1 -> x0, blocking collectives: 38.3 us -> none  [shards(): total = lax.psum(table, 'zs')]
    all_to_all x0 -> x2, blocking collectives: none -> 15.4 us  [the longest x1 8.01 us: swapped_between(): lax.all_to_all(block, axis, 0, 0, tiled=True, axis_index_groups=groups)]
    all_to_all x1 -> x2, starting transfers between devices: 6.16 us -> 10.3 us  [the longest x1 5.31 us: swapped_within(): lax.all_to_all(block, axis, 0, 0, tiled=True, axis_index_groups=groups)]
    ppermute x3, starting transfers between devices: 5.55 us -> 4.11 us  [passed_along(): return lax.ppermute(block, axis, route)]
    all_to_all x1 -> x2, waiting for transfers between devices: 5.19 us -> 4.47 us  [the longest x1 3.06 us: swapped_between(): lax.all_to_all(block, axis, 0, 0, tiled=True, axis_index_groups=groups)]
    pallas_call x0 -> x2, Pallas kernels: none -> 0.67 us  [the longest x1 0.66 us: shards(): pl.pallas_call(regroup_kernel, out_shape=jax.ShapeDtypeStruct((z_blocks,...]
  transfers between devices with their start and end apart: 4 -> 5, of which waited for: 1 -> 2; matrix products, arithmetic and copies ran while one was open for 0% -> 0% of each run, Pallas kernels for 7% -> 7%
where the time goes in v3:
time: 42.6 us; the launch traced here: 42.1 us
  blocking collectives  15.4 us (36%)
  starting transfers between devices  14.4 us (34%)
  Pallas kernels  6.45 us (15%)
  waiting for transfers between devices  4.48 us (11%)
  between operations  0.69 us (2%)
  local copies, waits for them, and re-layouts  0.67 us (2%)
    all_to_all x1, blocking collectives, swapped_between(): lax.all_to_all(block, axis, 0, 0, tiled=True, axis_index_groups=groups)  8.01 us
    all_to_all x1, blocking collectives, swapped_within(): lax.all_to_all(block, axis, 0, 0, tiled=True, axis_index_groups=groups)  7.37 us
    all_to_all x1, starting transfers between devices, swapped_within(): lax.all_to_all(block, axis, 0, 0, tiled=True, axis_index_groups=groups)  5.31 us
    all_to_all x1, starting transfers between devices, swapped_between(): lax.all_to_all(block, axis, 0, 0, tiled=True, axis_index_groups=groups)  5.01 us
    ppermute x3, starting transfers between devices, passed_along(): return lax.ppermute(block, axis, route)  4.11 us
    all_to_all x1, waiting for transfers between devices, swapped_between(): lax.all_to_all(block, axis, 0, 0, tiled=True, axis_index_groups=groups)  3.06 us
    pallas_call x1, Pallas kernels, shards(): pl.pallas_call(functools.partial(chain_kernel, depth_z, scale, block_z, b...  2.29 us
    pallas_call x1, Pallas kernels, shards(): pl.pallas_call(functools.partial(pack_kernel, block_z, block_x), out_shap...  1.77 us
  transfers between devices with their start and end apart: 5, of which 2 were waited for; matrix products, arithmetic and copies ran while one was open for 0% of the time, Pallas kernels for 7%

profile of v3, /device:TPU:0, one launch (start us, length us, event | category | flops | bytes accessed | tf_op | source)
XLA Modules:
  0.0 42.1 jit_solution(6248340535296765401)
XLA Ops:
  0.6 1.8 %pack.1 = (f32[8,4,8,128]{3,2,1,0:T(8,128)}, bf16[30,2,256]{2,1,0:T(2,128)(2,1)}) custom-call(bf16[2,3,8,384]{3,2,1,0:T(8,128)(2,1)} %up_ref.1, bf16[2,3,8,384]{3,2,1,0:T(8,128)(2,1)} %down_ref.1, bf16[18,6,2,256]{3,2,1,0:T(2,128)(2,1)} %bitcast.24, bf16[6,6,2,256]{3,2,1,0:T(2,128)(2,1)} %bitcast.27), custom_call_target="tpu_custom_call" | custom-call | flops 2000000000 | bytes 400000 | tf_op jit(solution)/shard_map/pack/pallas_call | solution.py:319
  2.4 0.0 copy-start
  2.4 0.0 copy-start.1
  2.4 0.0 copy-start.7
  2.4 5.3 %all-to-all-start = ((f32[8,4,8,128]{3,2,1,0:T(8,128)}), f32[8,4,8,128]{3,2,1,0:T(8,128)S(1)}, u32[]{:S(2)}, u32[]{:S(2)}) async-start(f32[8,4,8,128]{3,2,1,0:T(8,128)} %get-tuple-element.9), calls=%async_computation | async-start | bytes 262144 | tf_op jit(solution)/shard_map/all_to_all | solution.py:34
  7.7 0.0 copy-done
  7.7 3.7 %collective-permute-start = (bf16[18,6,2,256]{3,2,1,0:T(2,128)(2,1)S(1)}, bf16[18,6,2,256]{3,2,1,0:T(2,128)(2,1)S(1)}, u32[]{:S(2)}, u32[]{:S(2)}) collective-permute-start(bf16[18,6,2,256]{3,2,1,0:T(2,128)(2,1)S(1)} %bitcast.25), channel_id=1, source_target_pairs={{8,0},{9,1},{10,2},{11,3},{12,4},{13,5},{14,6},{15,7},{16,8},{17,9... | collective-permute-start | bytes 331784 | tf_op jit(solution)/shard_map/ppermute | solution.py:28
  11.4 0.0 copy-done.1
  11.4 0.4 %collective-permute-start.1 = (bf16[6,6,2,256]{3,2,1,0:T(2,128)(2,1)S(1)}, bf16[6,6,2,256]{3,2,1,0:T(2,128)(2,1)S(1)}, u32[]{:S(2)}, u32[]{:S(2)}) collective-permute-start(bf16[6,6,2,256]{3,2,1,0:T(2,128)(2,1)S(1)} %bitcast.28), channel_id=1, source_target_pairs={{8,0},{9,1},{10,2},{11,3},{12,4},{13,5},{14,6},{15,7},{16,8},{17,9... | collective-permute-start | bytes 110600 | tf_op jit(solution)/shard_map/ppermute | solution.py:28
  11.8 0.0 copy-done.7
  11.8 0.0 collective-permute-start.2
  11.8 1.4 %all-to-all-done.came_ref = f32[8,4,8,128]{3,2,1,0:T(8,128)S(1)} async-done(((f32[8,4,8,128]{3,2,1,0:T(8,128)}), f32[8,4,8,128]{3,2,1,0:T(8,128)S(1)}, u32[]{:S(2)}, u32[]{:S(2)}) %all-to-all-start) | async-done | bytes 131104 | tf_op jit(solution)/shard_map/all_to_all | solution.py:34
  13.3 0.7 %regroup.1 = f32[4,8,8,128]{3,2,1,0:T(8,128)} custom-call(f32[8,4,8,128]{3,2,1,0:T(8,128)S(1)} %all-to-all-done.came_ref), custom_call_target="tpu_custom_call" | custom-call | flops 500000000 | bytes 300000 | tf_op jit(solution)/shard_map/regroup/pallas_call | solution.py:341
  13.9 0.0 copy-start.3
  13.9 0.0 copy-start.4
  13.9 5.0 %all-to-all-start.1 = ((f32[4,8,8,128]{3,2,1,0:T(8,128)}), f32[4,8,8,128]{3,2,1,0:T(8,128)S(1)}, u32[]{:S(2)}, u32[]{:S(2)}) async-start(f32[4,8,8,128]{3,2,1,0:T(8,128)} %regroup.1), calls=%async_computation.1 | async-start | bytes 262144 | tf_op jit(solution)/shard_map/all_to_all | solution.py:40
  18.9 0.0 collective-permute-done.2.edge_ref
  18.9 0.0 collective-permute-done.1.forward_next_ref
  18.9 0.0 collective-permute-done.links_next_ref
  19.0 0.0 copy-start.5
  19.0 0.0 copy-start.6
  19.0 0.0 copy-done.3
  19.0 0.0 copy-done.4
  19.0 0.6 %copy-done.2 = s32[1024]{0:T(1024)S(1)} copy-done((s32[1024]{0:T(1024)S(1)}, s32[1024]{0:T(1024)}, u32[]{:S(2)}) %copy-start.2) | copy-done | bytes 4120
  19.6 0.0 copy-done.5
  19.6 0.0 copy-done.6
  19.6 2.3 %chain.1 = (f32[8,96,256]{2,1,0:T(8,128)S(1)}, bf16[2,192,128]{2,1,0:T(8,128)(2,1)S(1)}, s32[8,128]{1,0:T(8,128)S(1)}) custom-call(f32[8]{0:T(128)S(1)} %copy-done.6, s32[3,8]{1,0:T(4,128)S(1)} %bitcast.33, bf16[18,6,2,256]{3,2,1,0:T(2,128)(2,1)S(1)} %bitcast.26, bf16[18,6,2,256]{3,2,1,0:T(2,128)(2,1)S(1)} %collective-permute-done.links_next_ref, ...), custom_call_target="tpu_custom_call" | custom-call | flops 3000000000 | bytes 2000000 | tf_op jit(solution)/shard_map/chain/pallas_call | solution.py:353
  21.9 3.1 %all-to-all-done.1 = f32[4,8,8,128]{3,2,1,0:T(8,128)S(1)} async-done(((f32[4,8,8,128]{3,2,1,0:T(8,128)}), f32[4,8,8,128]{3,2,1,0:T(8,128)S(1)}, u32[]{:S(2)}, u32[]{:S(2)}) %all-to-all-start.1) | async-done | bytes 131104 | tf_op jit(solution)/shard_map/all_to_all | solution.py:40
  25.0 1.1 %meet.1 = (f32[6,6,2,256]{3,2,1,0:T(2,128)}, f32[8,128]{1,0:T(8,128)S(1)}) custom-call(f32[32,8,128]{2,1,0:T(8,128)S(1)} %bitcast.19, bf16[2,192,128]{2,1,0:T(8,128)(2,1)S(1)} %get-tuple-element.11.corner_ref, f32[8,96,256]{2,1,0:T(8,128)S(1)} %get-tuple-element.12.chain_ref), custom_call_target="tpu_custom_call" | custom-call | flops 2000000000 | bytes 1000000 | tf_op jit(solution)/shard_map/meet/pallas_call | solution.py:382
  26.1 7.4 %all_to_all.20 = f32[8,1,128]{2,1,0:T(1,128)S(1)} all-to-all(f32[8,1,128]{2,1,0:T(1,128)S(1)} %bitcast.23), channel_id=1, replica_groups={{0,1,2,3,4,5,6,7},{8,9,10,11,12,13,14,15},{16,17,18,19,20,21,22,23},{24..., dimensions={0} | all-to-all | bytes 8192 | tf_op jit(solution)/shard_map/all_to_all | solution.py:34
  33.5 8.0 %all_to_all.21 = f32[4,1,128]{2,1,0:T(1,128)S(1)} all-to-all(f32[4,1,128]{2,1,0:T(1,128)S(1)} %bitcast.22), channel_id=1, replica_groups={{0,8,16,24},{1,9,17,25},{2,10,18,26},{3,11,19,27},{4,12,20,28},{5,13,21..., dimensions={0} | all-to-all | bytes 4096 | tf_op jit(solution)/shard_map/all_to_all | solution.py:40
  41.5 0.6 %final.1 = f32[2,96]{1,0:T(2,128)} custom-call(f32[4,128]{1,0:T(4,128)S(1)} %bitcast.21, s32[8,128]{1,0:T(8,128)S(1)} %get-tuple-element.15.picked_ref), custom_call_target="tpu_custom_call" | custom-call | tf_op jit(solution)/shard_map/final/pallas_call | solution.py:404
  (2 shorter events, 0.0 us)
Async XLA Ops:
  2.4 5.3 %copy-start = (bf16[2,3,3,1,6,2,256]{6,5,4,3,2,1,0:T(2,128)(2,1)S(1)}, bf16[2,3,3,1,6,2,256]{6,5,4,3,2,1,0:T(2,128)(2,1)}, u32[]{:S(2)}) copy-start(bf16[2,3,3,1,6,2,256]{6,5,4,3,2,1,0:T(2,128)(2,1)} %param.12) | copy-start | bytes 331780
  2.4 9.0 %copy-start.1 = (bf16[2,3,1,6,2,256]{5,4,3,2,1,0:T(2,128)(2,1)S(1)}, bf16[2,3,1,6,2,256]{5,4,3,2,1,0:T(2,128)(2,1)}, u32[]{:S(2)}) copy-start(bf16[2,3,1,6,2,256]{5,4,3,2,1,0:T(2,128)(2,1)} %param.11) | copy-start | bytes 110596
  2.4 9.4 %copy-start.7 = (bf16[30,2,256]{2,1,0:T(2,128)(2,1)S(1)}, bf16[30,2,256]{2,1,0:T(2,128)(2,1)}, u32[]{:S(2)}) copy-start(bf16[30,2,256]{2,1,0:T(2,128)(2,1)} %get-tuple-element.10) | copy-start | bytes 92164
  2.4 10.8 %all-to-all-start = ((f32[8,4,8,128]{3,2,1,0:T(8,128)}), f32[8,4,8,128]{3,2,1,0:T(8,128)S(1)}, u32[]{:S(2)}, u32[]{:S(2)}) async-start(f32[8,4,8,128]{3,2,1,0:T(8,128)} %get-tuple-element.9), calls=%async_computation | async-start | bytes 262144 | tf_op jit(solution)/shard_map/all_to_all | solution.py:34
  7.7 11.2 %collective-permute-start = (bf16[18,6,2,256]{3,2,1,0:T(2,128)(2,1)S(1)}, bf16[18,6,2,256]{3,2,1,0:T(2,128)(2,1)S(1)}, u32[]{:S(2)}, u32[]{:S(2)}) collective-permute-start(bf16[18,6,2,256]{3,2,1,0:T(2,128)(2,1)S(1)} %bitcast.25), channel_id=1, source_target_pairs={{8,0},{9,1},{10,2},{11,3},{12,4},{13,5},{14,6},{15,7},{16,8},{17,9... | collective-permute-start | bytes 331784 | tf_op jit(solution)/shard_map/ppermute | solution.py:28
  11.4 7.5 %collective-permute-start.1 = (bf16[6,6,2,256]{3,2,1,0:T(2,128)(2,1)S(1)}, bf16[6,6,2,256]{3,2,1,0:T(2,128)(2,1)S(1)}, u32[]{:S(2)}, u32[]{:S(2)}) collective-permute-start(bf16[6,6,2,256]{3,2,1,0:T(2,128)(2,1)S(1)} %bitcast.28), channel_id=1, source_target_pairs={{8,0},{9,1},{10,2},{11,3},{12,4},{13,5},{14,6},{15,7},{16,8},{17,9... | collective-permute-start | bytes 110600 | tf_op jit(solution)/shard_map/ppermute | solution.py:28
  11.8 7.1 %collective-permute-start.2 = (bf16[30,2,256]{2,1,0:T(2,128)(2,1)S(1)}, bf16[30,2,256]{2,1,0:T(2,128)(2,1)S(1)}, u32[]{:S(2)}, u32[]{:S(2)}) collective-permute-start(bf16[30,2,256]{2,1,0:T(2,128)(2,1)S(1)} %copy-done.7), channel_id=1, source_target_pairs={{16,0},{17,1},{18,2},{19,3},{20,4},{21,5},{22,6},{23,7},{24,8},{25... | collective-permute-start | bytes 92168 | tf_op jit(solution)/shard_map/ppermute | solution.py:28
  13.9 5.1 %copy-start.3 = (s32[1024]{0:T(1024)S(1)}, s32[1024]{0:T(1024)}, u32[]{:S(2)}) copy-start(s32[1024]{0:T(1024)} %param.16) | copy-start | bytes 12292
  13.9 5.1 %copy-start.4 = (s32[1024,1]{0,1:T(1,128)S(1)}, s32[1024,1]{0,1:T(1,128)}, u32[]{:S(2)}) copy-start(s32[1024,1]{0,1:T(1,128)} %param.17) | copy-start | bytes 12292
  13.9 11.1 %all-to-all-start.1 = ((f32[4,8,8,128]{3,2,1,0:T(8,128)}), f32[4,8,8,128]{3,2,1,0:T(8,128)S(1)}, u32[]{:S(2)}, u32[]{:S(2)}) async-start(f32[4,8,8,128]{3,2,1,0:T(8,128)} %regroup.1), calls=%async_computation.1 | async-start | bytes 262144 | tf_op jit(solution)/shard_map/all_to_all | solution.py:40
  18.9 0.7 %copy-start.2 = (s32[1024]{0:T(1024)S(1)}, s32[1024]{0:T(1024)}, u32[]{:S(2)}) copy-start(s32[1024]{0:T(1024)} %param.15) | copy-start | bytes 12292
  19.0 0.7 %copy-start.5 = (s32[8,3]{0,1:T(4,128)S(1)}, s32[8,3]{0,1:T(4,128)}, u32[]{:S(2)}) copy-start(s32[8,3]{0,1:T(4,128)} %param.14) | copy-start | bytes 292
  19.0 0.7 %copy-start.6 = (f32[8]{0:T(128)S(1)}, f32[8]{0:T(128)}, u32[]{:S(2)}) copy-start(f32[8]{0:T(128)} %weight_ref.1) | copy-start | bytes 100

commit v4 on v1

--- a/solution.py
+++ b/solution.py
@@ -37,10 +37,7 @@
     return lax.broadcasted_iota(jnp.int32, shape, axis)
 
 
-def pack_kernel(block_z, block_x, up_ref, down_ref, links_ref, forward_ref, out_ref, edge_ref):
-    edge_ref[0:18] = links_ref[:, 0]
-    edge_ref[18:24] = forward_ref[:, 0]
-    edge_ref[24:30] = forward_ref[:, 1]
+def pack_kernel(block_z, block_x, up_ref, down_ref, out_ref):
     zh = block_z + 1
     slot_lanes = zh * XH
     width_x = block_x * G
@@ -90,6 +87,16 @@
             out_ref[zb * G + g] = value
 
 
+def phases(group, depth_z, block_z, block_x, scale):
+    row = iota((CROWS, LANES), 0)
+    angle = ((group * block_z + row // block_x) * PMOM % depth_z).astype(F32)
+    angle = angle * (2.0 * math.pi / depth_z)
+    inside = row < block_z * block_x
+    cos_z = jnp.where(inside, jnp.cos(angle) * scale, 0.0)[:, :1]
+    sin_z = jnp.where(inside, jnp.sin(angle) * scale, 0.0)[:, :1]
+    return cos_z, sin_z
+
+
 def chain_kernel(
     depth_z,
     scale,
@@ -101,30 +108,31 @@
     links_next_ref,
     forward_ref,
     forward_next_ref,
-    edge_ref,
     lengths_ref,
     separations_ref,
     owners_ref,
     chain_ref,
     corner_ref,
     picked_ref,
+    tail_ref,
     link_rows,
     field_rows,
+    tails,
 ):
     place = lax.axis_index("zs")
     rows_y = links_ref.shape[3]
     zh = block_z + 1
     slot_lanes = zh * XH
     count = block_z * block_x
-    link_rows[...] = jnp.zeros_like(link_rows)
-    field_rows[...] = jnp.zeros_like(field_rows)
+    no_plane = jnp.zeros((block_x, rows_y), F32)
 
     def fill_links(i, carry):
         for z in range(block_z):
             link_rows[i, block_x * z : block_x * (z + 1)] = links_ref[i, z].astype(F32)
             at = count + block_x * z
-            link_rows[i, at : at + block_x] = links_next_ref[i, z].astype(F32)
-        link_rows[i, 2 * count : 2 * count + block_x] = edge_ref[i].astype(F32)
+            last = z == block_z - 1
+            plane = no_plane if last else links_next_ref[i, z].astype(F32)
+            link_rows[i, at : at + block_x] = plane
         return carry
 
     def fill_field(i, carry):
@@ -132,20 +140,12 @@
             field_rows[i, block_x * z : block_x * (z + 1)] = forward_ref[i, z].astype(F32)
             at = count + block_x * z
             field_rows[i, at : at + block_x] = forward_next_ref[i, z].astype(F32)
-        field_rows[i, 2 * count : 2 * count + block_x] = edge_ref[18 + i].astype(F32)
-        at = 2 * count + block_x
-        field_rows[i, at : at + block_x] = edge_ref[24 + i].astype(F32)
         return carry
 
     lax.fori_loop(0, 18, fill_links, 0)
     lax.fori_loop(0, 6, fill_field, 0)
 
-    row = iota((CROWS, LANES), 0)
-    z_of_row = (place // G) * block_z + row // block_x
-    angle = (z_of_row * PMOM % depth_z).astype(F32) * (2.0 * math.pi / depth_z)
-    inside = row < count
-    cos_z = jnp.where(inside, jnp.cos(angle) * scale, 0.0)[:, :1]
-    sin_z = jnp.where(inside, jnp.sin(angle) * scale, 0.0)[:, :1]
+    cos_z, sin_z = phases(place // G, depth_z, block_z, block_x, scale)
     total_rows = link_rows.shape[1]
 
     def step(length, carry):
@@ -166,6 +166,9 @@
                     imag = term_imag if imag is None else imag + term_imag
                 field_rows[a, :, lanes] = real
                 field_rows[3 + a, :, lanes] = imag
+                kept = jnp.clip(length + 1 - block_z, 0, LMAX - block_z)
+                tails[kept, a, :, lanes] = real[:block_x]
+                tails[kept, 3 + a, :, lanes] = imag[:block_x]
                 top_real, top_imag = real[:CROWS], imag[:CROWS]
                 chain_ref[length, a * CROWS : (a + 1) * CROWS, lanes] = (
                     top_real * cos_z - top_imag * sin_z
@@ -176,6 +179,7 @@
         return carry
 
     lax.fori_loop(0, LMAX, step, 0)
+    tail_ref[...] = tails[: LMAX - block_z]
 
     shape = (6 * CROWS, LANES)
     row = iota(shape, 0)
@@ -214,7 +218,34 @@
     picked_ref[...] = jnp.where(picked[1:2] > 0.5, lane_of, -1)
 
 
-def meet_kernel(block_z, block_x, got_ref, corner_ref, chain_ref, seq_ref, table_ref):
+def tail_kernel(depth_z, scale, block_z, block_x, links_ref, tail_ref, extra_ref):
+    cos_z, sin_z = phases(lax.axis_index("zs") // G, depth_z, block_z, block_x, scale)
+    extra_ref[...] = jnp.zeros_like(extra_ref)
+    past = LMAX - block_z
+    vecs = [[tail_ref[k, c] for c in range(6)] for k in range(past)]
+    for z in range(block_z - 1, block_z - 1 - past, -1):
+        links = [links_ref[i, z].astype(F32) for i in range(18)]
+        at = z * block_x
+        cos_at, sin_at = cos_z[at : at + block_x], sin_z[at : at + block_x]
+        moved = []
+        for k in range(past - (block_z - 1 - z)):
+            vec = vecs[k]
+            real, imag = [], []
+            for a in range(3):
+                row = [(links[3 * a + b], links[9 + 3 * a + b]) for b in range(3)]
+                real.append(sum(row[b][0] * vec[b] - row[b][1] * vec[3 + b] for b in range(3)))
+                imag.append(sum(row[b][0] * vec[3 + b] + row[b][1] * vec[b] for b in range(3)))
+            moved.append(real + imag)
+            kept = k + block_z - 1 - z
+            for a in range(3):
+                first = a * CROWS + at
+                extra_ref[kept, first : first + block_x] = real[a] * cos_at - imag[a] * sin_at
+                first = (3 + a) * CROWS + at
+                extra_ref[kept, first : first + block_x] = real[a] * sin_at + imag[a] * cos_at
+        vecs = moved
+
+
+def meet_kernel(block_z, block_x, got_ref, corner_ref, chain_ref, extra_ref, seq_ref, table_ref):
     rows_y = got_ref.shape[0] * NT
     got = got_ref[...].reshape(rows_y, LANES)
     high, low = split_two(got)
@@ -232,6 +263,8 @@
     sums = []
     for length in range(LMAX):
         chain = chain_ref[length]
+        if length >= block_z:
+            chain = chain + extra_ref[length - block_z]
         for field in (seq, turned):
             prod = field * chain
             part = prod[:8]
@@ -249,8 +282,8 @@
     table_ref[...] = flat
 
 
-def final_kernel(total_ref, picked_ref, out_ref):
-    total = total_ref[...]
+def final_kernel(tables_ref, picked_ref, out_ref):
+    total = jnp.sum(tables_ref[...], axis=0, keepdims=True)
     picked = picked_ref[...]
     value = jnp.take_along_axis(
         jnp.broadcast_to(total, picked.shape), jnp.maximum(picked, 0), axis=1
@@ -292,46 +325,37 @@
 
     links_next = passed_along(links, "zs", -G)
     field_next = passed_along(field, "zs", -G)
-    payload, edge = pl.pallas_call(
+    payload = pl.pallas_call(
         functools.partial(pack_kernel, block_z, block_x),
-        out_shape=(
-            jax.ShapeDtypeStruct((devices, NT, LANES), F32),
-            jax.ShapeDtypeStruct((30, block_x, rows_y), BF16),
-        ),
+        out_shape=jax.ShapeDtypeStruct((devices, NT, LANES), F32),
         grid=(1,),
-        in_specs=[
-            pl.BlockSpec(quark_up.shape, lambda i: (0, 0, 0, 0)),
-            pl.BlockSpec(quark_down.shape, lambda i: (0, 0, 0, 0)),
-            pl.BlockSpec((18, 1, block_x, rows_y), lambda i: (0, 0, 0, 0)),
-            pl.BlockSpec((6, 2, block_x, rows_y), lambda i: (0, 0, 0, 0)),
-        ],
-        out_specs=(
-            pl.BlockSpec((devices, NT, LANES), lambda i: (0, 0, 0)),
-            pl.BlockSpec((30, block_x, rows_y), lambda i: (0, 0, 0)),
-        ),
+        in_specs=[pl.BlockSpec(quark_up.shape, lambda i: (0, 0, 0, 0))] * 2,
+        out_specs=pl.BlockSpec((devices, NT, LANES), lambda i: (0, 0, 0)),
         compiler_params=WIDE_PARAMS,
         cost_estimate=cost(2_000_000_000, 400_000),
         name="pack",
-    )(quark_up, quark_down, links, field)
-    edge_next = passed_along(edge, "zs", -2 * G)
+    )(quark_up, quark_down)
     got = lax.all_to_all(payload, "zs", split_axis=0, concat_axis=0, tiled=True)
 
     requests = (lengths.shape[0] // LANES, LANES)
-    chain, corner, picked = pl.pallas_call(
+    past = LMAX - block_z
+    chain, corner, picked, tail = pl.pallas_call(
         functools.partial(chain_kernel, depth_z, scale, block_z, block_x),
         out_shape=(
             jax.ShapeDtypeStruct((LMAX, 6 * CROWS, rows_y), F32),
             jax.ShapeDtypeStruct((2, 12 * CROWS, LANES), BF16),
             jax.ShapeDtypeStruct((8, LANES), jnp.int32),
+            jax.ShapeDtypeStruct((past, 6, block_x, rows_y), F32),
         ),
-        in_specs=[SMEM, SMEM] + [VMEM] * 8,
-        out_specs=(VMEM, VMEM, VMEM),
+        in_specs=[SMEM, SMEM] + [VMEM] * 7,
+        out_specs=(VMEM,) * 4,
         scratch_shapes=[
-            pltpu.VMEM((18, 32, rows_y), F32),
-            pltpu.VMEM((6, 32, rows_y), F32),
+            pltpu.VMEM((18, 2 * block_z * block_x, rows_y), F32),
+            pltpu.VMEM((6, 2 * block_z * block_x, rows_y), F32),
+            pltpu.VMEM((past + 1, 6, block_x, rows_y), F32),
         ],
         compiler_params=PARAMS,
-        cost_estimate=cost(3_000_000_000, 2_000_000),
+        cost_estimate=cost(3_000_000_000, 200_000),
         name="chain",
     )(
         corner_weight,
@@ -340,11 +364,20 @@
         links_next,
         field,
         field_next,
-        edge_next,
         lengths.reshape(requests),
         separations.reshape(requests),
         owner_map.reshape(requests),
     )
+
+    extra = pl.pallas_call(
+        functools.partial(tail_kernel, depth_z, scale, block_z, block_x),
+        out_shape=jax.ShapeDtypeStruct((past, 6 * CROWS, rows_y), F32),
+        in_specs=[VMEM] * 2,
+        out_specs=VMEM,
+        compiler_params=PARAMS,
+        cost_estimate=cost(100_000_000, 200_000),
+        name="tail",
+    )(links, passed_along(tail, "zs", -G))
 
     seq, table = pl.pallas_call(
         functools.partial(meet_kernel, block_z, block_x),
@@ -352,13 +385,13 @@
             jax.ShapeDtypeStruct((6, block_z, block_x, rows_y), F32),
             jax.ShapeDtypeStruct((1, LANES), F32),
         ),
-        in_specs=[VMEM] * 3,
+        in_specs=[VMEM] * 4,
         out_specs=(VMEM, VMEM),
         compiler_params=PARAMS,
         cost_estimate=cost(2_000_000_000, 1_000_000),
         name="meet",
-    )(got, corner, chain)
-    total = lax.psum(table, "zs")
+    )(got, corner, chain, extra)
+    tables = lax.all_gather(table, "zs", axis=0, tiled=True)
     owned = pl.pallas_call(
         final_kernel,
         out_shape=jax.ShapeDtypeStruct((2, MOST), F32),
@@ -366,7 +399,7 @@
         out_specs=VMEM,
         compiler_params=PARAMS,
         name="final",
-    )(total, picked)
+    )(tables, picked)
     return (seq.reshape(2, 3, 1, block_z, block_x, rows_y), owned.T)
 
 

time: 62.8 us -> 63.9 us (1.018)
  blocking collectives: 38.3 us -> 41.9 us
  waiting for transfers between devices: 5.2 us -> 1.71 us
  starting transfers between devices: 11.7 us -> 13 us
    all_gather x0 -> x1, blocking collectives: none -> 41.9 us  [shards(): tables = lax.all_gather(table, 'zs', axis=0, tiled=True)]
    psum x1 -> x0, blocking collectives: 38.3 us -> none  [shards(): total = lax.psum(table, 'zs')]
    all_to_all x1, waiting for transfers between devices: 5.19 us -> 0.19 us  [shards(): got = lax.all_to_all(payload, 'zs', split_axis=0, concat_axis=0, tiled=True)]
    ppermute x3, starting transfers between devices: 5.55 us -> 9.19 us  [passed_along(): return lax.ppermute(block, axis, route)]
    all_to_all x1, starting transfers between devices: 6.16 us -> 3.83 us  [shards(): got = lax.all_to_all(payload, 'zs', split_axis=0, concat_axis=0, tiled=True)]
    ppermute x3, waiting for transfers between devices: 0.01 us -> 1.53 us  [passed_along(): return lax.ppermute(block, axis, route)]
  transfers between devices with their start and end apart: 4 -> 4, of which waited for: 1 -> 2; matrix products, arithmetic and copies ran while one was open for 0% -> 0% of each run, Pallas kernels for 7% -> 6%
where the time goes in v4:
time: 63.9 us; the launch traced here: 63.6 us
  blocking collectives  41.9 us (66%)
  starting transfers between devices  13 us (20%)
  Pallas kernels  5.62 us (9%)
  waiting for transfers between devices  1.71 us (3%)
  between operations  0.72 us (1%)
  local copies, waits for them, and re-layouts  0.65 us (1%)
    all_gather x1, blocking collectives, shards(): tables = lax.all_gather(table, 'zs', axis=0, tiled=True)  41.9 us
    ppermute x3, starting transfers between devices, passed_along(): return lax.ppermute(block, axis, route)  9.19 us
    all_to_all x1, starting transfers between devices, shards(): got = lax.all_to_all(payload, 'zs', split_axis=0, concat_axis=0, tiled=True)  3.83 us
    pallas_call x1, Pallas kernels, shards(): pl.pallas_call(functools.partial(chain_kernel, depth_z, scale, block_z, b...  2.06 us
    pallas_call x1, Pallas kernels, shards(): pl.pallas_call(functools.partial(pack_kernel, block_z, block_x), out_shap...  1.75 us
    ppermute x3, waiting for transfers between devices, passed_along(): return lax.ppermute(block, axis, route)  1.53 us
  transfers between devices with their start and end apart: 4, of which 2 were waited for; matrix products, arithmetic and copies ran while one was open for 0% of the time, Pallas kernels for 6%

profile of v4, /device:TPU:0, one launch (start us, length us, event | category | flops | bytes accessed | tf_op | source)
XLA Modules:
  0.0 63.6 jit_solution(3035255692500948382)
XLA Ops:
  0.6 5.1 %collective-permute-start.1 = (bf16[6,6,2,256]{3,2,1,0:T(2,128)(2,1)}, bf16[6,6,2,256]{3,2,1,0:T(2,128)(2,1)S(1)}, u32[]{:S(2)}, u32[]{:S(2)}) collective-permute-start(bf16[6,6,2,256]{3,2,1,0:T(2,128)(2,1)} %bitcast.17), channel_id=1, source_target_pairs={{8,0},{9,1},{10,2},{11,3},{12,4},{13,5},{14,6},{15,7},{16,8},{17,9... | collective-permute-start | bytes 110600 | tf_op jit(solution)/shard_map/ppermute | solution.py:28
  5.7 0.4 collective-permute-start
  6.2 1.7 %pack.1 = f32[32,8,128]{2,1,0:T(8,128)} custom-call(bf16[2,3,8,384]{3,2,1,0:T(8,128)(2,1)} %up_ref.1, bf16[2,3,8,384]{3,2,1,0:T(8,128)(2,1)} %down_ref.1), custom_call_target="tpu_custom_call" | custom-call | flops 2000000000 | bytes 400000 | tf_op jit(solution)/shard_map/pack/pallas_call | solution.py:328
  7.9 0.0 copy-start
  7.9 0.0 copy-start.1
  7.9 0.0 copy-start.3
  7.9 0.0 copy-start.4
  7.9 3.8 %all-to-all-start = ((f32[32,8,128]{2,1,0:T(8,128)}), f32[32,8,128]{2,1,0:T(8,128)S(1)}, u32[]{:S(2)}, u32[]{:S(2)}) async-start(f32[32,8,128]{2,1,0:T(8,128)} %pack.1), calls=%async_computation | async-start | bytes 262144 | tf_op jit(solution)/shard_map/all_to_all | solution.py:338
  11.8 0.0 copy-start.2
  11.8 0.0 collective-permute-done.1.forward_next_ref
  11.8 0.0 collective-permute-done.links_next_ref
  11.8 0.0 copy-start.5
  11.8 0.0 copy-start.6
  11.8 0.0 copy-done
  11.8 0.0 copy-done.1
  11.9 0.0 copy-done.3
  11.9 0.0 copy-done.4
  11.9 0.6 copy-done.2
  12.5 0.0 copy-done.5
  12.5 0.0 copy-done.6
  12.5 2.1 %chain.1 = (f32[8,96,256]{2,1,0:T(8,128)S(1)}, bf16[2,192,128]{2,1,0:T(8,128)(2,1)S(1)}, s32[8,128]{1,0:T(8,128)S(1)}, f32[2,6,2,256]{3,2,1,0:T(2,128)S(1)}) custom-call(f32[8]{0:T(128)S(1)} %copy-done.6, s32[3,8]{1,0:T(4,128)S(1)} %bitcast.22, bf16[18,6,2,256]{3,2,1,0:T(2,128)(2,1)S(1)} %bitcast.15, ...), custom_call_target="tpu_custom_call" | custom-call | flops 3000000000 | bytes 200000 | tf_op jit(solution)/shard_map/chain/pallas_call | solution.py:342
  14.6 3.6 %collective-permute-start.2 = (f32[2,6,2,256]{3,2,1,0:T(2,128)S(1)}, f32[2,6,2,256]{3,2,1,0:T(2,128)S(1)}, u32[]{:S(2)}, u32[]{:S(2)}) collective-permute-start(f32[2,6,2,256]{3,2,1,0:T(2,128)S(1)} %get-tuple-element.10), channel_id=1, source_target_pairs={{8,0},{9,1},{10,2},{11,3},{12,4},{13,5},{14,6},{15,7},{16,8},{17,9... | collective-permute-start | bytes 73736 | tf_op jit(solution)/shard_map/ppermute | solution.py:28
  18.2 1.5 %collective-permute-done.2.tail_ref = f32[2,6,2,256]{3,2,1,0:T(2,128)S(1)} collective-permute-done((f32[2,6,2,256]{3,2,1,0:T(2,128)S(1)}, f32[2,6,2,256]{3,2,1,0:T(2,128)S(1)}, u32[]{:S(2)}, u32[]{:S(2)}) %collective-permute-start.2) | collective-permute-done | bytes 24608 | tf_op jit(solution)/shard_map/ppermute | solution.py:28
  19.7 0.1 tail.1.extra_ref
  19.8 0.2 all-to-all-done.got_ref
  20.0 1.1 %meet.1 = (f32[6,6,2,256]{3,2,1,0:T(2,128)}, f32[1,128]{1,0:T(1,128)S(1)}) custom-call(f32[32,8,128]{2,1,0:T(8,128)S(1)} %all-to-all-done.got_ref, bf16[2,192,128]{2,1,0:T(8,128)(2,1)S(1)} %get-tuple-element.8.corner_ref, f32[8,96,256]{2,1,0:T(8,128)S(1)} %get-tuple-element.9.chain_ref, f32[2,96,256]{2,1,0:T(8,128)S(1)} %tail.1.extra_ref), custom_call_target="tpu_custom_call" | custom-call | flops 2000000000 | bytes 1000000 | tf_op jit(solution)/shard_map/meet/pallas_call | solution.py:382
  21.1 41.9 %all-gather = f32[32,1,128]{2,1,0:T(1,128)S(1)} all-gather(f32[1,1,128]{2,1,0:T(1,128)S(1)} %bitcast.13), channel_id=1, replica_groups=mesh['grp'=1,'zs'=32] {'zs'}, dimensions={0}, use_global_device_ids=true | all-gather | bytes 16896 | tf_op jit(solution)/shard_map/all_gather | solution.py:394
  62.9 0.6 %final.1 = f32[2,96]{1,0:T(2,128)} custom-call(f32[32,128]{1,0:T(8,128)S(1)} %bitcast.12, s32[8,128]{1,0:T(8,128)S(1)} %get-tuple-element.13.picked_ref), custom_call_target="tpu_custom_call" | custom-call | tf_op jit(solution)/shard_map/final/pallas_call | solution.py:395
Async XLA Ops:
  0.6 11.2 %collective-permute-start.1 = (bf16[6,6,2,256]{3,2,1,0:T(2,128)(2,1)}, bf16[6,6,2,256]{3,2,1,0:T(2,128)(2,1)S(1)}, u32[]{:S(2)}, u32[]{:S(2)}) collective-permute-start(bf16[6,6,2,256]{3,2,1,0:T(2,128)(2,1)} %bitcast.17), channel_id=1, source_target_pairs={{8,0},{9,1},{10,2},{11,3},{12,4},{13,5},{14,6},{15,7},{16,8},{17,9... | collective-permute-start | bytes 110600 | tf_op jit(solution)/shard_map/ppermute | solution.py:28
  5.7 6.1 %collective-permute-start = (bf16[18,6,2,256]{3,2,1,0:T(2,128)(2,1)}, bf16[18,6,2,256]{3,2,1,0:T(2,128)(2,1)S(1)}, u32[]{:S(2)}, u32[]{:S(2)}) collective-permute-start(bf16[18,6,2,256]{3,2,1,0:T(2,128)(2,1)} %bitcast.14), channel_id=1, source_target_pairs={{8,0},{9,1},{10,2},{11,3},{12,4},{13,5},{14,6},{15,7},{16,8},{17,9... | collective-permute-start | bytes 331784 | tf_op jit(solution)/shard_map/ppermute | solution.py:28
  7.9 3.9 %copy-start = (bf16[2,3,3,1,6,2,256]{6,5,4,3,2,1,0:T(2,128)(2,1)S(1)}, bf16[2,3,3,1,6,2,256]{6,5,4,3,2,1,0:T(2,128)(2,1)}, u32[]{:S(2)}) copy-start(bf16[2,3,3,1,6,2,256]{6,5,4,3,2,1,0:T(2,128)(2,1)} %param.12) | copy-start | bytes 331780
  7.9 3.9 %copy-start.1 = (bf16[2,3,1,6,2,256]{5,4,3,2,1,0:T(2,128)(2,1)S(1)}, bf16[2,3,1,6,2,256]{5,4,3,2,1,0:T(2,128)(2,1)}, u32[]{:S(2)}) copy-start(bf16[2,3,1,6,2,256]{5,4,3,2,1,0:T(2,128)(2,1)} %param.11) | copy-start | bytes 110596
  7.9 3.9 %copy-start.3 = (s32[1024]{0:T(1024)S(1)}, s32[1024]{0:T(1024)}, u32[]{:S(2)}) copy-start(s32[1024]{0:T(1024)} %param.16) | copy-start | bytes 12292
  7.9 3.9 %copy-start.4 = (s32[1024,1]{0,1:T(1,128)S(1)}, s32[1024,1]{0,1:T(1,128)}, u32[]{:S(2)}) copy-start(s32[1024,1]{0,1:T(1,128)} %param.17) | copy-start | bytes 12292
  7.9 12.1 %all-to-all-start = ((f32[32,8,128]{2,1,0:T(8,128)}), f32[32,8,128]{2,1,0:T(8,128)S(1)}, u32[]{:S(2)}, u32[]{:S(2)}) async-start(f32[32,8,128]{2,1,0:T(8,128)} %pack.1), calls=%async_computation | async-start | bytes 262144 | tf_op jit(solution)/shard_map/all_to_all | solution.py:338
  11.8 0.7 %copy-start.2 = (s32[1024]{0:T(1024)S(1)}, s32[1024]{0:T(1024)}, u32[]{:S(2)}) copy-start(s32[1024]{0:T(1024)} %param.15) | copy-start | bytes 12292
  11.8 0.7 %copy-start.5 = (s32[8,3]{0,1:T(4,128)S(1)}, s32[8,3]{0,1:T(4,128)}, u32[]{:S(2)}) copy-start(s32[8,3]{0,1:T(4,128)} %param.14) | copy-start | bytes 292
  11.8 0.7 %copy-start.6 = (f32[8]{0:T(128)S(1)}, f32[8]{0:T(128)}, u32[]{:S(2)}) copy-start(f32[8]{0:T(128)} %weight_ref.1) | copy-start | bytes 100
  14.6 5.2 %collective-permute-start.2 = (f32[2,6,2,256]{3,2,1,0:T(2,128)S(1)}, f32[2,6,2,256]{3,2,1,0:T(2,128)S(1)}, u32[]{:S(2)}, u32[]{:S(2)}) collective-permute-start(f32[2,6,2,256]{3,2,1,0:T(2,128)S(1)} %get-tuple-element.10), channel_id=1, source_target_pairs={{8,0},{9,1},{10,2},{11,3},{12,4},{13,5},{14,6},{15,7},{16,8},{17,9... | collective-permute-start | bytes 73736 | tf_op jit(solution)/shard_map/ppermute | solution.py:28

commit v5 on v1

--- a/solution.py
+++ b/solution.py
@@ -90,6 +90,16 @@
             out_ref[zb * G + g] = value
 
 
+def phases(group, depth_z, block_z, block_x, scale):
+    row = iota((CROWS, LANES), 0)
+    angle = ((group * block_z + row // block_x) * PMOM % depth_z).astype(F32)
+    angle = angle * (2.0 * math.pi / depth_z)
+    inside = row < block_z * block_x
+    cos_z = jnp.where(inside, jnp.cos(angle) * scale, 0.0)[:, :1]
+    sin_z = jnp.where(inside, jnp.sin(angle) * scale, 0.0)[:, :1]
+    return cos_z, sin_z
+
+
 def chain_kernel(
     depth_z,
     scale,
@@ -101,7 +111,6 @@
     links_next_ref,
     forward_ref,
     forward_next_ref,
-    edge_ref,
     lengths_ref,
     separations_ref,
     owners_ref,
@@ -110,21 +119,29 @@
     picked_ref,
     link_rows,
     field_rows,
+    index_rows,
+    index_done,
 ):
+    sources = (lengths_ref, separations_ref, owners_ref)
+    copies = [
+        pltpu.make_async_copy(sources[i], index_rows.at[i], index_done.at[i]) for i in range(3)
+    ]
+    for copy in copies:
+        copy.start()
     place = lax.axis_index("zs")
     rows_y = links_ref.shape[3]
     zh = block_z + 1
     slot_lanes = zh * XH
     count = block_z * block_x
-    link_rows[...] = jnp.zeros_like(link_rows)
-    field_rows[...] = jnp.zeros_like(field_rows)
+    no_plane = jnp.zeros((block_x, rows_y), F32)
 
     def fill_links(i, carry):
         for z in range(block_z):
             link_rows[i, block_x * z : block_x * (z + 1)] = links_ref[i, z].astype(F32)
             at = count + block_x * z
-            link_rows[i, at : at + block_x] = links_next_ref[i, z].astype(F32)
-        link_rows[i, 2 * count : 2 * count + block_x] = edge_ref[i].astype(F32)
+            last = z == block_z - 1
+            plane = no_plane if last else links_next_ref[i, z].astype(F32)
+            link_rows[i, at : at + block_x] = plane
         return carry
 
     def fill_field(i, carry):
@@ -132,20 +149,12 @@
             field_rows[i, block_x * z : block_x * (z + 1)] = forward_ref[i, z].astype(F32)
             at = count + block_x * z
             field_rows[i, at : at + block_x] = forward_next_ref[i, z].astype(F32)
-        field_rows[i, 2 * count : 2 * count + block_x] = edge_ref[18 + i].astype(F32)
-        at = 2 * count + block_x
-        field_rows[i, at : at + block_x] = edge_ref[24 + i].astype(F32)
         return carry
 
     lax.fori_loop(0, 18, fill_links, 0)
     lax.fori_loop(0, 6, fill_field, 0)
 
-    row = iota((CROWS, LANES), 0)
-    z_of_row = (place // G) * block_z + row // block_x
-    angle = (z_of_row * PMOM % depth_z).astype(F32) * (2.0 * math.pi / depth_z)
-    inside = row < count
-    cos_z = jnp.where(inside, jnp.cos(angle) * scale, 0.0)[:, :1]
-    sin_z = jnp.where(inside, jnp.sin(angle) * scale, 0.0)[:, :1]
+    cos_z, sin_z = phases(place // G, depth_z, block_z, block_x, scale)
     total_rows = link_rows.shape[1]
 
     def step(length, carry):
@@ -195,8 +204,10 @@
         corner_ref[0, y_step * 6 * CROWS : (y_step + 1) * 6 * CROWS] = high
         corner_ref[1, y_step * 6 * CROWS : (y_step + 1) * 6 * CROWS] = low
 
-    mine = owners_ref[...] == place
-    codes = (lengths_ref[...] * (2 * NT) + separations_ref[...]).astype(F32)
+    for copy in copies:
+        copy.wait()
+    mine = index_rows[2] == place
+    codes = (index_rows[0] * (2 * NT) + index_rows[1]).astype(F32)
     member = jnp.where(mine, 1.0, 0.0)
     below = jnp.where(iota((LANES, LANES), 0) < iota((LANES, LANES), 1), 1.0, 0.0)
     earlier = jnp.dot(member.astype(BF16), below.astype(BF16), preferred_element_type=F32)
@@ -214,7 +225,43 @@
     picked_ref[...] = jnp.where(picked[1:2] > 0.5, lane_of, -1)
 
 
-def meet_kernel(block_z, block_x, got_ref, corner_ref, chain_ref, seq_ref, table_ref):
+def link_times(links, vec):
+    real, imag = [], []
+    for a in range(3):
+        row = [(links[3 * a + b], links[9 + 3 * a + b]) for b in range(3)]
+        real.append(sum(row[b][0] * vec[b] - row[b][1] * vec[3 + b] for b in range(3)))
+        imag.append(sum(row[b][0] * vec[3 + b] + row[b][1] * vec[b] for b in range(3)))
+    return real + imag
+
+
+def tail_kernel(
+    depth_z, scale, block_z, block_x, links_ref, links_next_ref, edge_ref, corner_ref, extra_ref
+):
+    cos_z, sin_z = phases(lax.axis_index("zs") // G, depth_z, block_z, block_x, scale)
+    extra_ref[...] = jnp.zeros_like(extra_ref)
+    planes = edge_ref[...].astype(F32)
+    near = [planes[18 + c] for c in range(6)]
+    far = link_times([planes[i] for i in range(18)], [planes[24 + c] for c in range(6)])
+    vecs = [near, far]
+    for z in range(2 * block_z - 1, block_z - 3, -1):
+        ref = links_ref if z < block_z else links_next_ref
+        links = [ref[i, z % block_z].astype(F32) for i in range(18)]
+        vecs = [link_times(links, vec) for vec in vecs]
+        if z < block_z:
+            at = z * block_x
+            cos_at, sin_at = cos_z[at : at + block_x], sin_z[at : at + block_x]
+            for k, vec in enumerate(vecs):
+                kept = k + block_z - 1 - z
+                for a in range(3):
+                    real, imag = vec[a], vec[3 + a]
+                    first = a * CROWS + at
+                    extra_ref[kept, first : first + block_x] = real * cos_at - imag * sin_at
+                    first = (3 + a) * CROWS + at
+                    extra_ref[kept, first : first + block_x] = real * sin_at + imag * cos_at
+            vecs = vecs[:-1]
+
+
+def meet_kernel(block_z, block_x, got_ref, corner_ref, chain_ref, extra_ref, seq_ref, table_ref):
     rows_y = got_ref.shape[0] * NT
     got = got_ref[...].reshape(rows_y, LANES)
     high, low = split_two(got)
@@ -232,6 +279,8 @@
     sums = []
     for length in range(LMAX):
         chain = chain_ref[length]
+        if length >= block_z:
+            chain = chain + extra_ref[length - block_z]
         for field in (seq, turned):
             prod = field * chain
             part = prod[:8]
@@ -246,11 +295,11 @@
         table = table + pltpu.roll(table, shift, 1)
     mine = iota((2 * LMAX, LANES), 1) // NT == iota((2 * LMAX, LANES), 0)
     flat = jnp.sum(jnp.where(mine, table, 0.0), axis=0, keepdims=True)
-    table_ref[...] = flat
-
-
-def final_kernel(total_ref, picked_ref, out_ref):
-    total = total_ref[...]
+    table_ref[...] = jnp.broadcast_to(flat, table_ref.shape)
+
+
+def final_kernel(tables_ref, picked_ref, out_ref):
+    total = jnp.sum(tables_ref[...], axis=0, keepdims=True)
     picked = picked_ref[...]
     value = jnp.take_along_axis(
         jnp.broadcast_to(total, picked.shape), jnp.maximum(picked, 0), axis=1
@@ -313,10 +362,12 @@
         cost_estimate=cost(2_000_000_000, 400_000),
         name="pack",
     )(quark_up, quark_down, links, field)
+    got = lax.all_to_all(payload, "zs", split_axis=0, concat_axis=0, tiled=True)
+
+    requests = (lengths.shape[0] // LANES, LANES)
+    past = LMAX - block_z
+    edge, links_next = lax.optimization_barrier((edge, links_next))
     edge_next = passed_along(edge, "zs", -2 * G)
-    got = lax.all_to_all(payload, "zs", split_axis=0, concat_axis=0, tiled=True)
-
-    requests = (lengths.shape[0] // LANES, LANES)
     chain, corner, picked = pl.pallas_call(
         functools.partial(chain_kernel, depth_z, scale, block_z, block_x),
         out_shape=(
@@ -324,14 +375,16 @@
             jax.ShapeDtypeStruct((2, 12 * CROWS, LANES), BF16),
             jax.ShapeDtypeStruct((8, LANES), jnp.int32),
         ),
-        in_specs=[SMEM, SMEM] + [VMEM] * 8,
-        out_specs=(VMEM, VMEM, VMEM),
+        in_specs=[SMEM, SMEM] + [VMEM] * 4 + [pl.BlockSpec(memory_space=pl.ANY)] * 3,
+        out_specs=(VMEM,) * 3,
         scratch_shapes=[
-            pltpu.VMEM((18, 32, rows_y), F32),
-            pltpu.VMEM((6, 32, rows_y), F32),
+            pltpu.VMEM((18, 2 * block_z * block_x, rows_y), F32),
+            pltpu.VMEM((6, 2 * block_z * block_x, rows_y), F32),
+            pltpu.VMEM((3,) + requests, jnp.int32),
+            pltpu.SemaphoreType.DMA((3,)),
         ],
         compiler_params=PARAMS,
-        cost_estimate=cost(3_000_000_000, 2_000_000),
+        cost_estimate=cost(3_000_000_000, 200_000),
         name="chain",
     )(
         corner_weight,
@@ -340,25 +393,36 @@
         links_next,
         field,
         field_next,
-        edge_next,
         lengths.reshape(requests),
         separations.reshape(requests),
         owner_map.reshape(requests),
     )
 
+    extra = pl.pallas_call(
+        functools.partial(tail_kernel, depth_z, scale, block_z, block_x),
+        out_shape=jax.ShapeDtypeStruct((past, 6 * CROWS, rows_y), F32),
+        in_specs=[VMEM] * 3 + [pl.BlockSpec(memory_space=pl.ANY)],
+        out_specs=VMEM,
+        compiler_params=PARAMS,
+        cost_estimate=cost(400_000_000, 200_000),
+        name="tail",
+    )(links, links_next, edge_next, corner)
+
     seq, table = pl.pallas_call(
         functools.partial(meet_kernel, block_z, block_x),
         out_shape=(
             jax.ShapeDtypeStruct((6, block_z, block_x, rows_y), F32),
-            jax.ShapeDtypeStruct((1, LANES), F32),
+            jax.ShapeDtypeStruct((devices, LANES), F32),
         ),
-        in_specs=[VMEM] * 3,
+        in_specs=[VMEM] * 4,
         out_specs=(VMEM, VMEM),
         compiler_params=PARAMS,
         cost_estimate=cost(2_000_000_000, 1_000_000),
         name="meet",
-    )(got, corner, chain)
-    total = lax.psum(table, "zs")
+    )(got, corner, chain, extra)
+    tables = lax.all_to_all(
+        table.reshape(devices, 1, LANES), "zs", split_axis=0, concat_axis=0, tiled=True
+    ).reshape(devices, LANES)
     owned = pl.pallas_call(
         final_kernel,
         out_shape=jax.ShapeDtypeStruct((2, MOST), F32),
@@ -366,7 +430,7 @@
         out_specs=VMEM,
         compiler_params=PARAMS,
         name="final",
-    )(total, picked)
+    )(tables, picked)
     return (seq.reshape(2, 3, 1, block_z, block_x, rows_y), owned.T)
 
 

time: 62.8 us -> 32.5 us (0.52)
  blocking collectives: 38.3 us -> 10.4 us
  waiting for transfers between devices: 5.2 us -> 2.39 us
    psum x1 -> x0, blocking collectives: 38.3 us -> none  [shards(): total = lax.psum(table, 'zs')]
    all_to_all x0 -> x1, blocking collectives: none -> 10.4 us  [shards(): lax.all_to_all(table.reshape(devices, 1, LANES), 'zs', split_axis=0, conc...]
    all_to_all x1, waiting for transfers between devices: 5.19 us -> 0.16 us  [shards(): got = lax.all_to_all(payload, 'zs', split_axis=0, concat_axis=0, tiled=True)]
    ppermute x3, starting transfers between devices: 5.55 us -> 8.29 us  [passed_along(): return lax.ppermute(block, axis, route)]
    all_to_all x1, starting transfers between devices: 6.16 us -> 3.83 us  [shards(): got = lax.all_to_all(payload, 'zs', split_axis=0, concat_axis=0, tiled=True)]
    ppermute x3, waiting for transfers between devices: 0.01 us -> 2.23 us  [passed_along(): return lax.ppermute(block, axis, route)]
  transfers between devices with their start and end apart: 4 -> 4, of which waited for: 1 -> 2; matrix products, arithmetic and copies ran while one was open for 0% -> 0% of each run, Pallas kernels for 7% -> 13%
where the time goes in v5:
time: 32.5 us; the launch traced here: 32.2 us
  starting transfers between devices  12.1 us (37%)
  blocking collectives  10.4 us (32%)
  Pallas kernels  5.92 us (18%)
  waiting for transfers between devices  2.39 us (7%)
  between operations  0.74 us (2%)
  local copies, waits for them, and re-layouts  0.64 us (2%)
    all_to_all x1, blocking collectives, shards(): lax.all_to_all(table.reshape(devices, 1, LANES), 'zs', split_axis=0, conc...  10.4 us
    ppermute x3, starting transfers between devices, passed_along(): return lax.ppermute(block, axis, route)  8.29 us
    all_to_all x1, starting transfers between devices, shards(): got = lax.all_to_all(payload, 'zs', split_axis=0, concat_axis=0, tiled=True)  3.83 us
    ppermute x3, waiting for transfers between devices, passed_along(): return lax.ppermute(block, axis, route)  2.23 us
    pallas_call x1, Pallas kernels, shards(): pl.pallas_call(functools.partial(chain_kernel, depth_z, scale, block_z, b...  2.22 us
    pallas_call x1, Pallas kernels, shards(): pl.pallas_call(functools.partial(pack_kernel, block_z, block_x), out_shap...  1.78 us
    pallas_call x1, Pallas kernels, shards(): pl.pallas_call(functools.partial(meet_kernel, block_z, block_x), out_shap...  1.07 us
  transfers between devices with their start and end apart: 4, of which 2 were waited for; matrix products, arithmetic and copies ran while one was open for 0% of the time, Pallas kernels for 13%

profile of v5, /device:TPU:0, one launch (start us, length us, event | category | flops | bytes accessed | tf_op | source)
XLA Modules:
  0.0 32.2 jit_solution(17018809354580181875)
XLA Ops:
  0.6 5.1 %collective-permute-start.1 = (bf16[6,6,2,256]{3,2,1,0:T(2,128)(2,1)}, bf16[6,6,2,256]{3,2,1,0:T(2,128)(2,1)S(1)}, u32[]{:S(2)}, u32[]{:S(2)}) collective-permute-start(bf16[6,6,2,256]{3,2,1,0:T(2,128)(2,1)} %bitcast.20), channel_id=1, source_target_pairs={{8,0},{9,1},{10,2},{11,3},{12,4},{13,5},{14,6},{15,7},{16,8},{17,9... | collective-permute-start | bytes 110600 | tf_op jit(solution)/shard_map/ppermute | solution.py:28
  5.7 0.4 %collective-permute-start = (bf16[18,6,2,256]{3,2,1,0:T(2,128)(2,1)}, bf16[18,6,2,256]{3,2,1,0:T(2,128)(2,1)S(1)}, u32[]{:S(2)}, u32[]{:S(2)}) collective-permute-start(bf16[18,6,2,256]{3,2,1,0:T(2,128)(2,1)} %bitcast.16), channel_id=1, source_target_pairs={{8,0},{9,1},{10,2},{11,3},{12,4},{13,5},{14,6},{15,7},{16,8},{17,9... | collective-permute-start | bytes 331784 | tf_op jit(solution)/shard_map/ppermute | solution.py:28
  6.2 1.8 %pack.1 = (f32[32,8,128]{2,1,0:T(8,128)}, bf16[30,2,256]{2,1,0:T(2,128)(2,1)}) custom-call(bf16[2,3,8,384]{3,2,1,0:T(8,128)(2,1)} %up_ref.1, bf16[2,3,8,384]{3,2,1,0:T(8,128)(2,1)} %down_ref.1, bf16[18,6,2,256]{3,2,1,0:T(2,128)(2,1)} %bitcast.17, bf16[6,6,2,256]{3,2,1,0:T(2,128)(2,1)} %bitcast.21), custom_call_target="tpu_custom_call" | custom-call | flops 2000000000 | bytes 400000 | tf_op jit(solution)/shard_map/pack/pallas_call | solution.py:344
  8.0 0.0 copy-start.7
  8.0 0.0 copy-start
  8.0 0.0 copy-start.1
  8.0 0.0 copy-start.4
  8.0 0.0 copy-start.5
  8.0 3.8 %all-to-all-start = ((f32[32,8,128]{2,1,0:T(8,128)}), f32[32,8,128]{2,1,0:T(8,128)S(1)}, u32[]{:S(2)}, u32[]{:S(2)}) async-start(f32[32,8,128]{2,1,0:T(8,128)} %get-tuple-element.11), calls=%async_computation | async-start | bytes 262144 | tf_op jit(solution)/shard_map/all_to_all | solution.py:365
  11.8 0.0 collective-permute-done.links_next_ref
  11.8 0.0 copy-start.3
  11.9 0.0 copy-done.7
  11.9 0.0 copy-start.2
  11.9 2.7 %collective-permute-start.2 = (bf16[30,2,256]{2,1,0:T(2,128)(2,1)S(1)}, bf16[30,2,256]{2,1,0:T(2,128)(2,1)S(1)}, u32[]{:S(2)}, u32[]{:S(2)}) collective-permute-start(bf16[30,2,256]{2,1,0:T(2,128)(2,1)S(1)} %copy-done.7), channel_id=1, source_target_pairs={{16,0},{17,1},{18,2},{19,3},{20,4},{21,5},{22,6},{23,7},{24,8},{25... | collective-permute-start | bytes 92168 | tf_op jit(solution)/shard_map/ppermute | solution.py:28
  14.6 0.0 collective-permute-done.1.forward_next_ref
  14.6 0.0 copy-start.6
  14.6 0.0 copy-done
  14.6 0.0 copy-done.1
  14.6 0.0 copy-done.4
  14.6 0.0 copy-done.5
  14.7 0.0 copy-done.3
  14.7 0.0 copy-done.2
  14.7 0.6 %copy-done.6 = f32[8]{0:T(128)S(1)} copy-done((f32[8]{0:T(128)S(1)}, f32[8]{0:T(128)}, u32[]{:S(2)}) %copy-start.6) | copy-done | bytes 56
  15.3 2.2 %chain.1 = (f32[8,96,256]{2,1,0:T(8,128)S(1)}, bf16[2,192,128]{2,1,0:T(8,128)(2,1)S(1)}, s32[8,128]{1,0:T(8,128)S(1)}) custom-call(f32[8]{0:T(128)S(1)} %copy-done.6, s32[3,8]{1,0:T(4,128)S(1)} %bitcast.26, bf16[18,6,2,256]{3,2,1,0:T(2,128)(2,1)S(1)} %bitcast.18, bf16[18,6,2,256]{3,2,1,0:T(2,128)(2,1)S(1)} %collective-permute-done.links_next_ref, ...), custom_call_target="tpu_custom_call" | custom-call | flops 3000000000 | bytes 200000 | tf_op jit(solution)/shard_map/chain/pallas_call | solution.py:371
  17.5 2.2 %collective-permute-done.2.edge_ref = bf16[30,2,256]{2,1,0:T(2,128)(2,1)S(1)} collective-permute-done((bf16[30,2,256]{2,1,0:T(2,128)(2,1)S(1)}, bf16[30,2,256]{2,1,0:T(2,128)(2,1)S(1)}, u32[]{:S(2)}, u32[]{:S(2)}) %collective-permute-start.2) | collective-permute-done | bytes 30752 | tf_op jit(solution)/shard_map/ppermute | solution.py:28
  19.7 0.2 tail.1.extra_ref
  19.9 0.2 all-to-all-done.got_ref
  20.1 1.1 %meet.1 = (f32[6,6,2,256]{3,2,1,0:T(2,128)}, f32[32,128]{1,0:T(8,128)S(1)}) custom-call(f32[32,8,128]{2,1,0:T(8,128)S(1)} %all-to-all-done.got_ref, bf16[2,192,128]{2,1,0:T(8,128)(2,1)S(1)} %get-tuple-element.14.corner_ref, f32[8,96,256]{2,1,0:T(8,128)S(1)} %get-tuple-element.15.chain_ref, f32[2,96,256]{2,1,0:T(8,128)S(1)} %tail.1.extra_ref), custom_call_target="tpu_custom_call" | custom-call | flops 2000000000 | bytes 1000000 | tf_op jit(solution)/shard_map/meet/pallas_call | solution.py:411
  21.2 10.4 %all_to_all.10 = f32[32,1,128]{2,1,0:T(1,128)S(1)} all-to-all(f32[32,1,128]{2,1,0:T(1,128)S(1)} %bitcast.15), channel_id=1, replica_groups=mesh['grp'=1,'zs'=32] {'zs'}, dimensions={0} | all-to-all | bytes 32768 | tf_op jit(solution)/shard_map/all_to_all | solution.py:423
  31.6 0.6 %final.1 = f32[2,96]{1,0:T(2,128)} custom-call(f32[32,128]{1,0:T(8,128)S(1)} %bitcast.14, s32[8,128]{1,0:T(8,128)S(1)} %get-tuple-element.19.picked_ref), custom_call_target="tpu_custom_call" | custom-call | tf_op jit(solution)/shard_map/final/pallas_call | solution.py:426
Async XLA Ops:
  0.6 14.0 %collective-permute-start.1 = (bf16[6,6,2,256]{3,2,1,0:T(2,128)(2,1)}, bf16[6,6,2,256]{3,2,1,0:T(2,128)(2,1)S(1)}, u32[]{:S(2)}, u32[]{:S(2)}) collective-permute-start(bf16[6,6,2,256]{3,2,1,0:T(2,128)(2,1)} %bitcast.20), channel_id=1, source_target_pairs={{8,0},{9,1},{10,2},{11,3},{12,4},{13,5},{14,6},{15,7},{16,8},{17,9... | collective-permute-start | bytes 110600 | tf_op jit(solution)/shard_map/ppermute | solution.py:28
  5.7 6.1 %collective-permute-start = (bf16[18,6,2,256]{3,2,1,0:T(2,128)(2,1)}, bf16[18,6,2,256]{3,2,1,0:T(2,128)(2,1)S(1)}, u32[]{:S(2)}, u32[]{:S(2)}) collective-permute-start(bf16[18,6,2,256]{3,2,1,0:T(2,128)(2,1)} %bitcast.16), channel_id=1, source_target_pairs={{8,0},{9,1},{10,2},{11,3},{12,4},{13,5},{14,6},{15,7},{16,8},{17,9... | collective-permute-start | bytes 331784 | tf_op jit(solution)/shard_map/ppermute | solution.py:28
  8.0 3.9 %copy-start.7 = (bf16[30,2,256]{2,1,0:T(2,128)(2,1)S(1)}, bf16[30,2,256]{2,1,0:T(2,128)(2,1)}, u32[]{:S(2)}) copy-start(bf16[30,2,256]{2,1,0:T(2,128)(2,1)} %get-tuple-element.16) | copy-start | bytes 92164
  8.0 6.7 %copy-start = (bf16[2,3,3,1,6,2,256]{6,5,4,3,2,1,0:T(2,128)(2,1)S(1)}, bf16[2,3,3,1,6,2,256]{6,5,4,3,2,1,0:T(2,128)(2,1)}, u32[]{:S(2)}) copy-start(bf16[2,3,3,1,6,2,256]{6,5,4,3,2,1,0:T(2,128)(2,1)} %param.12) | copy-start | bytes 331780
  8.0 6.7 %copy-start.1 = (bf16[2,3,1,6,2,256]{5,4,3,2,1,0:T(2,128)(2,1)S(1)}, bf16[2,3,1,6,2,256]{5,4,3,2,1,0:T(2,128)(2,1)}, u32[]{:S(2)}) copy-start(bf16[2,3,1,6,2,256]{5,4,3,2,1,0:T(2,128)(2,1)} %param.11) | copy-start | bytes 110596
  8.0 6.7 %copy-start.4 = (s32[1024,1]{0,1:T(1,128)S(1)}, s32[1024,1]{0,1:T(1,128)}, u32[]{:S(2)}) copy-start(s32[1024,1]{0,1:T(1,128)} %param.17) | copy-start | bytes 12292
  8.0 6.7 %copy-start.5 = (s32[8,3]{0,1:T(4,128)S(1)}, s32[8,3]{0,1:T(4,128)}, u32[]{:S(2)}) copy-start(s32[8,3]{0,1:T(4,128)} %param.14) | copy-start | bytes 292
  8.0 12.1 %all-to-all-start = ((f32[32,8,128]{2,1,0:T(8,128)}), f32[32,8,128]{2,1,0:T(8,128)S(1)}, u32[]{:S(2)}, u32[]{:S(2)}) async-start(f32[32,8,128]{2,1,0:T(8,128)} %get-tuple-element.11), calls=%async_computation | async-start | bytes 262144 | tf_op jit(solution)/shard_map/all_to_all | solution.py:365
  11.8 2.8 %copy-start.3 = (s32[1024]{0:T(1024)S(1)}, s32[1024]{0:T(1024)}, u32[]{:S(2)}) copy-start(s32[1024]{0:T(1024)} %param.16) | copy-start | bytes 12292
  11.9 2.8 %copy-start.2 = (s32[1024]{0:T(1024)S(1)}, s32[1024]{0:T(1024)}, u32[]{:S(2)}) copy-start(s32[1024]{0:T(1024)} %param.15) | copy-start | bytes 12292
  11.9 7.8 %collective-permute-start.2 = (bf16[30,2,256]{2,1,0:T(2,128)(2,1)S(1)}, bf16[30,2,256]{2,1,0:T(2,128)(2,1)S(1)}, u32[]{:S(2)}, u32[]{:S(2)}) collective-permute-start(bf16[30,2,256]{2,1,0:T(2,128)(2,1)S(1)} %copy-done.7), channel_id=1, source_target_pairs={{16,0},{17,1},{18,2},{19,3},{20,4},{21,5},{22,6},{23,7},{24,8},{25... | collective-permute-start | bytes 92168 | tf_op jit(solution)/shard_map/ppermute | solution.py:28
  14.6 0.7 %copy-start.6 = (f32[8]{0:T(128)S(1)}, f32[8]{0:T(128)}, u32[]{:S(2)}) copy-start(f32[8]{0:T(128)} %weight_ref.1) | copy-start | bytes 100

commit v6 on v5

--- a/solution.py
+++ b/solution.py
@@ -37,10 +37,28 @@
     return lax.broadcasted_iota(jnp.int32, shape, axis)
 
 
-def pack_kernel(block_z, block_x, up_ref, down_ref, links_ref, forward_ref, out_ref, edge_ref):
-    edge_ref[0:18] = links_ref[:, 0]
-    edge_ref[18:24] = forward_ref[:, 0]
-    edge_ref[24:30] = forward_ref[:, 1]
+def pack_kernel(
+    block_z,
+    block_x,
+    weight_ref,
+    offset_ref,
+    up_ref,
+    down_ref,
+    lengths_ref,
+    separations_ref,
+    owners_ref,
+    out_ref,
+    request_ref,
+    table_ref,
+):
+    codes = lengths_ref[...] * (2 * NT) + separations_ref[...]
+    request_ref[...] = owners_ref[...] * LANES + codes
+    lane = iota((8, LANES), 1)
+    table = jnp.zeros((8, LANES), F32)
+    for k in range(8):
+        corner = offset_ref[0, k] * 4 + offset_ref[1, k] * 2 + offset_ref[2, k]
+        table = jnp.where(lane == corner, weight_ref[k], table)
+    table_ref[...] = table
     zh = block_z + 1
     slot_lanes = zh * XH
     width_x = block_x * G
@@ -90,6 +108,12 @@
             out_ref[zb * G + g] = value
 
 
+def edge_kernel(links_ref, forward_ref, ready_ref, edge_ref):
+    edge_ref[0:18] = links_ref[:, 0]
+    edge_ref[18:24] = forward_ref[:, 0]
+    edge_ref[24:30] = forward_ref[:, 1]
+
+
 def phases(group, depth_z, block_z, block_x, scale):
     row = iota((CROWS, LANES), 0)
     angle = ((group * block_z + row // block_x) * PMOM % depth_z).astype(F32)
@@ -105,29 +129,18 @@
     scale,
     block_z,
     block_x,
-    weight_ref,
-    offset_ref,
+    table_ref,
+    request_ref,
     links_ref,
     links_next_ref,
     forward_ref,
     forward_next_ref,
-    lengths_ref,
-    separations_ref,
-    owners_ref,
     chain_ref,
     corner_ref,
     picked_ref,
     link_rows,
     field_rows,
-    index_rows,
-    index_done,
 ):
-    sources = (lengths_ref, separations_ref, owners_ref)
-    copies = [
-        pltpu.make_async_copy(sources[i], index_rows.at[i], index_done.at[i]) for i in range(3)
-    ]
-    for copy in copies:
-        copy.start()
     place = lax.axis_index("zs")
     rows_y = links_ref.shape[3]
     zh = block_z + 1
@@ -193,21 +206,18 @@
     z_step = lane % slot_lanes % zh - row % CROWS // block_x
     x_step = lane % slot_lanes // zh - row % block_x
     here = (lane // slot_lanes == (comp + place % G) % 6) & (row % CROWS < count)
-    sums = [jnp.zeros(shape, F32), jnp.zeros(shape, F32)]
-    for k in range(8):
-        match = here & (x_step == offset_ref[0, k]) & (z_step == offset_ref[2, k])
-        for y_step in range(2):
-            taken = jnp.where(offset_ref[1, k] == y_step, weight_ref[k], 0.0)
-            sums[y_step] = sums[y_step] + jnp.where(match, taken, 0.0)
+    here = here & (x_step >= 0) & (x_step < 2) & (z_step >= 0) & (z_step < 2)
+    table = jnp.broadcast_to(table_ref[0:1], shape)
     for y_step in range(2):
-        high, low = split_two(sums[y_step])
+        corner = jnp.where(here, 4 * x_step + 2 * y_step + z_step, 0)
+        weights = jnp.where(here, jnp.take_along_axis(table, corner, axis=1), 0.0)
+        high, low = split_two(weights)
         corner_ref[0, y_step * 6 * CROWS : (y_step + 1) * 6 * CROWS] = high
         corner_ref[1, y_step * 6 * CROWS : (y_step + 1) * 6 * CROWS] = low
 
-    for copy in copies:
-        copy.wait()
-    mine = index_rows[2] == place
-    codes = (index_rows[0] * (2 * NT) + index_rows[1]).astype(F32)
+    request = request_ref[...]
+    mine = request // LANES == place
+    codes = (request % LANES).astype(F32)
     member = jnp.where(mine, 1.0, 0.0)
     below = jnp.where(iota((LANES, LANES), 0) < iota((LANES, LANES), 1), 1.0, 0.0)
     earlier = jnp.dot(member.astype(BF16), below.astype(BF16), preferred_element_type=F32)
@@ -341,32 +351,47 @@
 
     links_next = passed_along(links, "zs", -G)
     field_next = passed_along(field, "zs", -G)
-    payload, edge = pl.pallas_call(
+    requests = (lengths.shape[0] // LANES, LANES)
+    payload, request, table = pl.pallas_call(
         functools.partial(pack_kernel, block_z, block_x),
         out_shape=(
             jax.ShapeDtypeStruct((devices, NT, LANES), F32),
-            jax.ShapeDtypeStruct((30, block_x, rows_y), BF16),
+            jax.ShapeDtypeStruct(requests, jnp.int32),
+            jax.ShapeDtypeStruct((8, LANES), F32),
         ),
         grid=(1,),
-        in_specs=[
-            pl.BlockSpec(quark_up.shape, lambda i: (0, 0, 0, 0)),
-            pl.BlockSpec(quark_down.shape, lambda i: (0, 0, 0, 0)),
-            pl.BlockSpec((18, 1, block_x, rows_y), lambda i: (0, 0, 0, 0)),
-            pl.BlockSpec((6, 2, block_x, rows_y), lambda i: (0, 0, 0, 0)),
-        ],
+        in_specs=[SMEM] * 2
+        + [pl.BlockSpec(quark_up.shape, lambda i: (0, 0, 0, 0))] * 2
+        + [pl.BlockSpec(requests, lambda i: (0, 0))] * 3,
         out_specs=(
             pl.BlockSpec((devices, NT, LANES), lambda i: (0, 0, 0)),
-            pl.BlockSpec((30, block_x, rows_y), lambda i: (0, 0, 0)),
+            pl.BlockSpec(requests, lambda i: (0, 0)),
+            pl.BlockSpec((8, LANES), lambda i: (0, 0)),
         ),
         compiler_params=WIDE_PARAMS,
         cost_estimate=cost(2_000_000_000, 400_000),
         name="pack",
-    )(quark_up, quark_down, links, field)
+    )(
+        corner_weight,
+        corner_offset.T,
+        quark_up,
+        quark_down,
+        lengths.reshape(requests),
+        separations.reshape(requests),
+        owner_map.reshape(requests),
+    )
     got = lax.all_to_all(payload, "zs", split_axis=0, concat_axis=0, tiled=True)
 
-    requests = (lengths.shape[0] // LANES, LANES)
     past = LMAX - block_z
-    edge, links_next = lax.optimization_barrier((edge, links_next))
+    edge = pl.pallas_call(
+        edge_kernel,
+        out_shape=jax.ShapeDtypeStruct((30, block_x, rows_y), BF16),
+        in_specs=[VMEM] * 2 + [pl.BlockSpec(memory_space=pl.ANY)],
+        out_specs=VMEM,
+        compiler_params=PARAMS,
+        cost_estimate=cost(50_000_000, 60_000),
+        name="edge",
+    )(links, field, links_next)
     edge_next = passed_along(edge, "zs", -2 * G)
     chain, corner, picked = pl.pallas_call(
         functools.partial(chain_kernel, depth_z, scale, block_z, block_x),
@@ -375,28 +400,16 @@
             jax.ShapeDtypeStruct((2, 12 * CROWS, LANES), BF16),
             jax.ShapeDtypeStruct((8, LANES), jnp.int32),
         ),
-        in_specs=[SMEM, SMEM] + [VMEM] * 4 + [pl.BlockSpec(memory_space=pl.ANY)] * 3,
+        in_specs=[VMEM] * 6,
         out_specs=(VMEM,) * 3,
         scratch_shapes=[
             pltpu.VMEM((18, 2 * block_z * block_x, rows_y), F32),
             pltpu.VMEM((6, 2 * block_z * block_x, rows_y), F32),
-            pltpu.VMEM((3,) + requests, jnp.int32),
-            pltpu.SemaphoreType.DMA((3,)),
         ],
         compiler_params=PARAMS,
         cost_estimate=cost(3_000_000_000, 200_000),
         name="chain",
-    )(
-        corner_weight,
-        corner_offset.T,
-        links,
-        links_next,
-        field,
-        field_next,
-        lengths.reshape(requests),
-        separations.reshape(requests),
-        owner_map.reshape(requests),
-    )
+    )(table, request, links, links_next, field, field_next)
 
     extra = pl.pallas_call(
         functools.partial(tail_kernel, depth_z, scale, block_z, block_x),
@@ -408,7 +421,7 @@
         name="tail",
     )(links, links_next, edge_next, corner)
 
-    seq, table = pl.pallas_call(
+    seq, partial = pl.pallas_call(
         functools.partial(meet_kernel, block_z, block_x),
         out_shape=(
             jax.ShapeDtypeStruct((6, block_z, block_x, rows_y), F32),
@@ -421,7 +434,7 @@
         name="meet",
     )(got, corner, chain, extra)
     tables = lax.all_to_all(
-        table.reshape(devices, 1, LANES), "zs", split_axis=0, concat_axis=0, tiled=True
+        partial.reshape(devices, 1, LANES), "zs", split_axis=0, concat_axis=0, tiled=True
     ).reshape(devices, LANES)
     owned = pl.pallas_call(
         final_kernel,

time: 32.5 us -> 32.5 us (level)
  waiting for transfers between devices: 2.39 us -> 3.81 us
  Pallas kernels: 5.92 us -> 5.16 us
  local copies, waits for them, and re-layouts: 0.64 us -> 0.02 us
    ppermute x3, waiting for transfers between devices: 2.23 us -> 3.65 us  [passed_along(): return lax.ppermute(block, axis, route)]
    pallas_call x1, Pallas kernels: 2.22 us -> 1.42 us  [shards(): pl.pallas_call(functools.partial(chain_kernel, depth_z, scale, block_z, b...]
    unnamed x16 -> x8, local copies, waits for them, and re-layouts: 0.64 us -> 0.02 us
  transfers between devices with their start and end apart: 4 -> 4, of which waited for: 2 -> 2; matrix products, arithmetic and copies ran while one was open for 0% -> 0% of each run, Pallas kernels for 13% -> 11%
where the time goes in v6:
time: 32.5 us; the launch traced here: 32.2 us
  starting transfers between devices  12.1 us (37%)
  blocking collectives  10.4 us (32%)
  Pallas kernels  5.16 us (16%)
  waiting for transfers between devices  3.81 us (12%)
  between operations  0.7 us (2%)
    all_to_all x1, blocking collectives, shards(): lax.all_to_all(partial.reshape(devices, 1, LANES), 'zs', split_axis=0, co...  10.4 us
    ppermute x3, starting transfers between devices, passed_along(): return lax.ppermute(block, axis, route)  8.29 us
    all_to_all x1, starting transfers between devices, shards(): got = lax.all_to_all(payload, 'zs', split_axis=0, concat_axis=0, tiled=True)  3.83 us
    ppermute x3, waiting for transfers between devices, passed_along(): return lax.ppermute(block, axis, route)  3.65 us
    pallas_call x1, Pallas kernels, shards(): pl.pallas_call(functools.partial(pack_kernel, block_z, block_x), out_shap...  1.8 us
    pallas_call x1, Pallas kernels, shards(): pl.pallas_call(functools.partial(chain_kernel, depth_z, scale, block_z, b...  1.42 us
    pallas_call x1, Pallas kernels, shards(): pl.pallas_call(functools.partial(meet_kernel, block_z, block_x), out_shap...  1.07 us
  transfers between devices with their start and end apart: 4, of which 2 were waited for; matrix products, arithmetic and copies ran while one was open for 0% of the time, Pallas kernels for 11%

profile of v6, /device:TPU:0, one launch (start us, length us, event | category | flops | bytes accessed | tf_op | source)
XLA Modules:
  0.0 32.2 jit_solution(9448339248119583163)
XLA Ops:
  0.6 5.1 %collective-permute-start.1 = (bf16[6,6,2,256]{3,2,1,0:T(2,128)(2,1)}, bf16[6,6,2,256]{3,2,1,0:T(2,128)(2,1)S(1)}, u32[]{:S(2)}, u32[]{:S(2)}) collective-permute-start(bf16[6,6,2,256]{3,2,1,0:T(2,128)(2,1)} %bitcast.19), channel_id=1, source_target_pairs={{8,0},{9,1},{10,2},{11,3},{12,4},{13,5},{14,6},{15,7},{16,8},{17,9... | collective-permute-start | bytes 110600 | tf_op jit(solution)/shard_map/ppermute | solution.py:28
  5.7 0.4 %collective-permute-start = (bf16[18,6,2,256]{3,2,1,0:T(2,128)(2,1)}, bf16[18,6,2,256]{3,2,1,0:T(2,128)(2,1)S(1)}, u32[]{:S(2)}, u32[]{:S(2)}) collective-permute-start(bf16[18,6,2,256]{3,2,1,0:T(2,128)(2,1)} %bitcast.14), channel_id=1, source_target_pairs={{8,0},{9,1},{10,2},{11,3},{12,4},{13,5},{14,6},{15,7},{16,8},{17,9... | collective-permute-start | bytes 331784 | tf_op jit(solution)/shard_map/ppermute | solution.py:28
  6.2 1.8 %pack.1 = (f32[32,8,128]{2,1,0:T(8,128)}, s32[8,128]{1,0:T(8,128)}, f32[8,128]{1,0:T(8,128)}) custom-call(f32[8]{0:T(128)} %weight_ref.1, s32[3,8]{1,0:T(4,128)} %bitcast.27, bf16[2,3,8,384]{3,2,1,0:T(8,128)(2,1)} %up_ref.1, bf16[2,3,8,384]{3,2,1,0:T(8,128)(2,1)} %down_ref.1, s32[8,128]{1,0:T(8,128)} %bitcast.24, s32[8,128]{1,0:T(8,128)} %bitcast.25, ...), custom_call_target="tpu_custom_call" | custom-call | flops 2000000000 | bytes 400000 | tf_op jit(solution)/shard_map/pack/pallas_call | solution.py:355
  8.0 0.0 copy-start
  8.0 0.0 copy-start.1
  8.0 3.8 %all-to-all-start = ((f32[32,8,128]{2,1,0:T(8,128)}), f32[32,8,128]{2,1,0:T(8,128)S(1)}, u32[]{:S(2)}, u32[]{:S(2)}) async-start(f32[32,8,128]{2,1,0:T(8,128)} %get-tuple-element.10), calls=%async_computation | async-start | bytes 262144 | tf_op jit(solution)/shard_map/all_to_all | solution.py:383
  11.8 0.0 copy-start.2
  11.8 0.0 copy-start.3
  11.9 0.0 collective-permute-done.links_next_ref.ready_ref
  11.9 0.0 copy-done
  11.9 0.0 copy-done.1
  11.9 2.7 %collective-permute-start.2 = (bf16[30,2,256]{2,1,0:T(2,128)(2,1)S(1)}, bf16[30,2,256]{2,1,0:T(2,128)(2,1)S(1)}, u32[]{:S(2)}, u32[]{:S(2)}) collective-permute-start(bf16[30,2,256]{2,1,0:T(2,128)(2,1)S(1)} %edge.1), channel_id=1, source_target_pairs={{16,0},{17,1},{18,2},{19,3},{20,4},{21,5},{22,6},{23,7},{24,8},{25... | collective-permute-start | bytes 92168 | tf_op jit(solution)/shard_map/ppermute | solution.py:28
  14.6 0.0 collective-permute-done.1.forward_next_ref
  14.6 0.0 copy-done.2
  14.6 0.0 copy-done.3
  14.7 1.4 %chain.1 = (f32[8,96,256]{2,1,0:T(8,128)S(1)}, bf16[2,192,128]{2,1,0:T(8,128)(2,1)S(1)}, s32[8,128]{1,0:T(8,128)S(1)}) custom-call(f32[8,128]{1,0:T(8,128)S(1)} %copy-done.3, s32[8,128]{1,0:T(8,128)S(1)} %copy-done.2, bf16[18,6,2,256]{3,2,1,0:T(2,128)(2,1)S(1)} %bitcast.16, bf16[18,6,2,256]{3,2,1,0:T(2,128)(2,1)S(1)} %collective-permute-done.links_next_ref.ready_ref, ...), custom_call_target="tpu_custom_call" | custom-call | flops 3000000000 | bytes 200000 | tf_op jit(solution)/shard_map/chain/pallas_call | solution.py:396
  16.1 3.6 %collective-permute-done.2.edge_ref = bf16[30,2,256]{2,1,0:T(2,128)(2,1)S(1)} collective-permute-done((bf16[30,2,256]{2,1,0:T(2,128)(2,1)S(1)}, bf16[30,2,256]{2,1,0:T(2,128)(2,1)S(1)}, u32[]{:S(2)}, u32[]{:S(2)}) %collective-permute-start.2) | collective-permute-done | bytes 30752 | tf_op jit(solution)/shard_map/ppermute | solution.py:28
  19.7 0.2 tail.1.extra_ref
  19.9 0.2 all-to-all-done.got_ref
  20.1 1.1 %meet.1 = (f32[6,6,2,256]{3,2,1,0:T(2,128)}, f32[32,128]{1,0:T(8,128)S(1)}) custom-call(f32[32,8,128]{2,1,0:T(8,128)S(1)} %all-to-all-done.got_ref, bf16[2,192,128]{2,1,0:T(8,128)(2,1)S(1)} %get-tuple-element.13.corner_ref, f32[8,96,256]{2,1,0:T(8,128)S(1)} %get-tuple-element.14.chain_ref, f32[2,96,256]{2,1,0:T(8,128)S(1)} %tail.1.extra_ref), custom_call_target="tpu_custom_call" | custom-call | flops 2000000000 | bytes 1000000 | tf_op jit(solution)/shard_map/meet/pallas_call | solution.py:424
  21.2 10.4 %all_to_all.10 = f32[32,1,128]{2,1,0:T(1,128)S(1)} all-to-all(f32[32,1,128]{2,1,0:T(1,128)S(1)} %bitcast.22), channel_id=1, replica_groups=mesh['grp'=1,'zs'=32] {'zs'}, dimensions={0} | all-to-all | bytes 32768 | tf_op jit(solution)/shard_map/all_to_all | solution.py:436
  31.6 0.6 %final.1 = f32[2,96]{1,0:T(2,128)} custom-call(f32[32,128]{1,0:T(8,128)S(1)} %bitcast.18, s32[8,128]{1,0:T(8,128)S(1)} %get-tuple-element.17.picked_ref), custom_call_target="tpu_custom_call" | custom-call | tf_op jit(solution)/shard_map/final/pallas_call | solution.py:439
  (1 shorter events, 0.0 us)
Async XLA Ops:
  0.6 14.0 %collective-permute-start.1 = (bf16[6,6,2,256]{3,2,1,0:T(2,128)(2,1)}, bf16[6,6,2,256]{3,2,1,0:T(2,128)(2,1)S(1)}, u32[]{:S(2)}, u32[]{:S(2)}) collective-permute-start(bf16[6,6,2,256]{3,2,1,0:T(2,128)(2,1)} %bitcast.19), channel_id=1, source_target_pairs={{8,0},{9,1},{10,2},{11,3},{12,4},{13,5},{14,6},{15,7},{16,8},{17,9... | collective-permute-start | bytes 110600 | tf_op jit(solution)/shard_map/ppermute | solution.py:28
  5.7 6.1 %collective-permute-start = (bf16[18,6,2,256]{3,2,1,0:T(2,128)(2,1)}, bf16[18,6,2,256]{3,2,1,0:T(2,128)(2,1)S(1)}, u32[]{:S(2)}, u32[]{:S(2)}) collective-permute-start(bf16[18,6,2,256]{3,2,1,0:T(2,128)(2,1)} %bitcast.14), channel_id=1, source_target_pairs={{8,0},{9,1},{10,2},{11,3},{12,4},{13,5},{14,6},{15,7},{16,8},{17,9... | collective-permute-start | bytes 331784 | tf_op jit(solution)/shard_map/ppermute | solution.py:28
  8.0 3.9 %copy-start = (bf16[2,3,3,1,6,2,256]{6,5,4,3,2,1,0:T(2,128)(2,1)S(1)}, bf16[2,3,3,1,6,2,256]{6,5,4,3,2,1,0:T(2,128)(2,1)}, u32[]{:S(2)}) copy-start(bf16[2,3,3,1,6,2,256]{6,5,4,3,2,1,0:T(2,128)(2,1)} %param.12) | copy-start | bytes 331780
  8.0 3.9 %copy-start.1 = (bf16[2,3,1,6,2,256]{5,4,3,2,1,0:T(2,128)(2,1)S(1)}, bf16[2,3,1,6,2,256]{5,4,3,2,1,0:T(2,128)(2,1)}, u32[]{:S(2)}) copy-start(bf16[2,3,1,6,2,256]{5,4,3,2,1,0:T(2,128)(2,1)} %param.11) | copy-start | bytes 110596
  8.0 12.1 %all-to-all-start = ((f32[32,8,128]{2,1,0:T(8,128)}), f32[32,8,128]{2,1,0:T(8,128)S(1)}, u32[]{:S(2)}, u32[]{:S(2)}) async-start(f32[32,8,128]{2,1,0:T(8,128)} %get-tuple-element.10), calls=%async_computation | async-start | bytes 262144 | tf_op jit(solution)/shard_map/all_to_all | solution.py:383
  11.8 2.8 %copy-start.2 = (s32[8,128]{1,0:T(8,128)S(1)}, s32[8,128]{1,0:T(8,128)}, u32[]{:S(2)}) copy-start(s32[8,128]{1,0:T(8,128)} %get-tuple-element.12.request_ref) | copy-start | bytes 12292
  11.8 2.8 %copy-start.3 = (f32[8,128]{1,0:T(8,128)S(1)}, f32[8,128]{1,0:T(8,128)}, u32[]{:S(2)}) copy-start(f32[8,128]{1,0:T(8,128)} %get-tuple-element.11.table_ref) | copy-start | bytes 12292
  11.9 7.8 %collective-permute-start.2 = (bf16[30,2,256]{2,1,0:T(2,128)(2,1)S(1)}, bf16[30,2,256]{2,1,0:T(2,128)(2,1)S(1)}, u32[]{:S(2)}, u32[]{:S(2)}) collective-permute-start(bf16[30,2,256]{2,1,0:T(2,128)(2,1)S(1)} %edge.1), channel_id=1, source_target_pairs={{16,0},{17,1},{18,2},{19,3},{20,4},{21,5},{22,6},{23,7},{24,8},{25... | collective-permute-start | bytes 92168 | tf_op jit(solution)/shard_map/ppermute | solution.py:28

commit v7 on v6

--- a/solution.py
+++ b/solution.py
@@ -108,10 +108,23 @@
             out_ref[zb * G + g] = value
 
 
+def link_times(links, vec):
+    real, imag = [], []
+    for a in range(3):
+        row = [(links[3 * a + b], links[9 + 3 * a + b]) for b in range(3)]
+        real.append(sum(row[b][0] * vec[b] - row[b][1] * vec[3 + b] for b in range(3)))
+        imag.append(sum(row[b][0] * vec[3 + b] + row[b][1] * vec[b] for b in range(3)))
+    return real + imag
+
+
 def edge_kernel(links_ref, forward_ref, ready_ref, edge_ref):
-    edge_ref[0:18] = links_ref[:, 0]
-    edge_ref[18:24] = forward_ref[:, 0]
-    edge_ref[24:30] = forward_ref[:, 1]
+    edge_ref[0:6] = forward_ref[:, 0]
+    links = [links_ref[i, 0].astype(F32) for i in range(18)]
+    after = [forward_ref[c, 1].astype(F32) for c in range(6)]
+    for c, value in enumerate(link_times(links, after)):
+        high, low = split_two(value)
+        edge_ref[6 + c] = high
+        edge_ref[12 + c] = low
 
 
 def phases(group, depth_z, block_z, block_x, scale):
@@ -235,23 +248,14 @@
     picked_ref[...] = jnp.where(picked[1:2] > 0.5, lane_of, -1)
 
 
-def link_times(links, vec):
-    real, imag = [], []
-    for a in range(3):
-        row = [(links[3 * a + b], links[9 + 3 * a + b]) for b in range(3)]
-        real.append(sum(row[b][0] * vec[b] - row[b][1] * vec[3 + b] for b in range(3)))
-        imag.append(sum(row[b][0] * vec[3 + b] + row[b][1] * vec[b] for b in range(3)))
-    return real + imag
-
-
 def tail_kernel(
     depth_z, scale, block_z, block_x, links_ref, links_next_ref, edge_ref, corner_ref, extra_ref
 ):
     cos_z, sin_z = phases(lax.axis_index("zs") // G, depth_z, block_z, block_x, scale)
     extra_ref[...] = jnp.zeros_like(extra_ref)
     planes = edge_ref[...].astype(F32)
-    near = [planes[18 + c] for c in range(6)]
-    far = link_times([planes[i] for i in range(18)], [planes[24 + c] for c in range(6)])
+    near = [planes[c] for c in range(6)]
+    far = [planes[6 + c] + planes[12 + c] for c in range(6)]
     vecs = [near, far]
     for z in range(2 * block_z - 1, block_z - 3, -1):
         ref = links_ref if z < block_z else links_next_ref
@@ -385,7 +389,7 @@
     past = LMAX - block_z
     edge = pl.pallas_call(
         edge_kernel,
-        out_shape=jax.ShapeDtypeStruct((30, block_x, rows_y), BF16),
+        out_shape=jax.ShapeDtypeStruct((18, block_x, rows_y), BF16),
         in_specs=[VMEM] * 2 + [pl.BlockSpec(memory_space=pl.ANY)],
         out_specs=VMEM,
         compiler_params=PARAMS,

time: 32.5 us -> 31.9 us (0.982)
  blocking collectives: 10.4 us -> 9.88 us
    ppermute x3, waiting for transfers between devices: 3.65 us -> 3.1 us  [passed_along(): return lax.ppermute(block, axis, route)]
    all_to_all x1, blocking collectives: 10.4 us -> 9.88 us  [shards(): lax.all_to_all(partial.reshape(devices, 1, LANES), 'zs', split_axis=0, co...]
    all_to_all x1, waiting for transfers between devices: 0.16 us -> 0.7 us  [shards(): got = lax.all_to_all(payload, 'zs', split_axis=0, concat_axis=0, tiled=True)]
where the time goes in v7:
time: 31.9 us; the launch traced here: 31.7 us
  starting transfers between devices  12.1 us (38%)
  blocking collectives  9.88 us (31%)
  Pallas kernels  5.17 us (16%)
  waiting for transfers between devices  3.8 us (12%)
  between operations  0.7 us (2%)
    all_to_all x1, blocking collectives, shards(): lax.all_to_all(partial.reshape(devices, 1, LANES), 'zs', split_axis=0, co...  9.88 us
    ppermute x3, starting transfers between devices, passed_along(): return lax.ppermute(block, axis, route)  8.29 us
    all_to_all x1, starting transfers between devices, shards(): got = lax.all_to_all(payload, 'zs', split_axis=0, concat_axis=0, tiled=True)  3.83 us
    ppermute x3, waiting for transfers between devices, passed_along(): return lax.ppermute(block, axis, route)  3.1 us
    pallas_call x1, Pallas kernels, shards(): pl.pallas_call(functools.partial(pack_kernel, block_z, block_x), out_shap...  1.8 us
    pallas_call x1, Pallas kernels, shards(): pl.pallas_call(functools.partial(chain_kernel, depth_z, scale, block_z, b...  1.42 us
    pallas_call x1, Pallas kernels, shards(): pl.pallas_call(functools.partial(meet_kernel, block_z, block_x), out_shap...  1.07 us
    all_to_all x1, waiting for transfers between devices, shards(): got = lax.all_to_all(payload, 'zs', split_axis=0, concat_axis=0, tiled=True)  0.7 us
  transfers between devices with their start and end apart: 4, of which 2 were waited for; matrix products, arithmetic and copies ran while one was open for 0% of the time, Pallas kernels for 11%

profile of v7, /device:TPU:0, one launch (start us, length us, event | category | flops | bytes accessed | tf_op | source)
XLA Modules:
  0.0 31.7 jit_solution(2133458960225604878)
XLA Ops:
  0.6 5.1 %collective-permute-start.1 = (bf16[6,6,2,256]{3,2,1,0:T(2,128)(2,1)}, bf16[6,6,2,256]{3,2,1,0:T(2,128)(2,1)S(1)}, u32[]{:S(2)}, u32[]{:S(2)}) collective-permute-start(bf16[6,6,2,256]{3,2,1,0:T(2,128)(2,1)} %bitcast.19), channel_id=1, source_target_pairs={{8,0},{9,1},{10,2},{11,3},{12,4},{13,5},{14,6},{15,7},{16,8},{17,9... | collective-permute-start | bytes 110600 | tf_op jit(solution)/shard_map/ppermute | solution.py:28
  5.7 0.4 %collective-permute-start = (bf16[18,6,2,256]{3,2,1,0:T(2,128)(2,1)}, bf16[18,6,2,256]{3,2,1,0:T(2,128)(2,1)S(1)}, u32[]{:S(2)}, u32[]{:S(2)}) collective-permute-start(bf16[18,6,2,256]{3,2,1,0:T(2,128)(2,1)} %bitcast.14), channel_id=1, source_target_pairs={{8,0},{9,1},{10,2},{11,3},{12,4},{13,5},{14,6},{15,7},{16,8},{17,9... | collective-permute-start | bytes 331784 | tf_op jit(solution)/shard_map/ppermute | solution.py:28
  6.2 1.8 %pack.1 = (f32[32,8,128]{2,1,0:T(8,128)}, s32[8,128]{1,0:T(8,128)}, f32[8,128]{1,0:T(8,128)}) custom-call(f32[8]{0:T(128)} %weight_ref.1, s32[3,8]{1,0:T(4,128)} %bitcast.27, bf16[2,3,8,384]{3,2,1,0:T(8,128)(2,1)} %up_ref.1, bf16[2,3,8,384]{3,2,1,0:T(8,128)(2,1)} %down_ref.1, s32[8,128]{1,0:T(8,128)} %bitcast.24, s32[8,128]{1,0:T(8,128)} %bitcast.25, ...), custom_call_target="tpu_custom_call" | custom-call | flops 2000000000 | bytes 400000 | tf_op jit(solution)/shard_map/pack/pallas_call | solution.py:359
  8.0 0.0 copy-start
  8.0 0.0 copy-start.1
  8.0 3.8 %all-to-all-start = ((f32[32,8,128]{2,1,0:T(8,128)}), f32[32,8,128]{2,1,0:T(8,128)S(1)}, u32[]{:S(2)}, u32[]{:S(2)}) async-start(f32[32,8,128]{2,1,0:T(8,128)} %get-tuple-element.10), calls=%async_computation | async-start | bytes 262144 | tf_op jit(solution)/shard_map/all_to_all | solution.py:387
  11.8 0.0 copy-start.2
  11.8 0.0 copy-start.3
  11.9 0.0 collective-permute-done.links_next_ref.ready_ref
  11.9 0.0 copy-done
  11.9 0.0 copy-done.1
  11.9 2.7 %collective-permute-start.2 = (bf16[18,2,256]{2,1,0:T(2,128)(2,1)S(1)}, bf16[18,2,256]{2,1,0:T(2,128)(2,1)S(1)}, u32[]{:S(2)}, u32[]{:S(2)}) collective-permute-start(bf16[18,2,256]{2,1,0:T(2,128)(2,1)S(1)} %edge.1), channel_id=1, source_target_pairs={{16,0},{17,1},{18,2},{19,3},{20,4},{21,5},{22,6},{23,7},{24,8},{25... | collective-permute-start | bytes 55304 | tf_op jit(solution)/shard_map/ppermute | solution.py:28
  14.7 0.0 collective-permute-done.1.forward_next_ref
  14.7 0.0 copy-done.2
  14.7 0.0 copy-done.3
  14.7 1.4 %chain.1 = (f32[8,96,256]{2,1,0:T(8,128)S(1)}, bf16[2,192,128]{2,1,0:T(8,128)(2,1)S(1)}, s32[8,128]{1,0:T(8,128)S(1)}) custom-call(f32[8,128]{1,0:T(8,128)S(1)} %copy-done.3, s32[8,128]{1,0:T(8,128)S(1)} %copy-done.2, bf16[18,6,2,256]{3,2,1,0:T(2,128)(2,1)S(1)} %bitcast.16, bf16[18,6,2,256]{3,2,1,0:T(2,128)(2,1)S(1)} %collective-permute-done.links_next_ref.ready_ref, ...), custom_call_target="tpu_custom_call" | custom-call | flops 3000000000 | bytes 200000 | tf_op jit(solution)/shard_map/chain/pallas_call | solution.py:400
  16.1 3.1 %collective-permute-done.2.edge_ref = bf16[18,2,256]{2,1,0:T(2,128)(2,1)S(1)} collective-permute-done((bf16[18,2,256]{2,1,0:T(2,128)(2,1)S(1)}, bf16[18,2,256]{2,1,0:T(2,128)(2,1)S(1)}, u32[]{:S(2)}, u32[]{:S(2)}) %collective-permute-start.2) | collective-permute-done | bytes 18464 | tf_op jit(solution)/shard_map/ppermute | solution.py:28
  19.2 0.2 tail.1.extra_ref
  19.4 0.7 %all-to-all-done.got_ref = f32[32,8,128]{2,1,0:T(8,128)S(1)} async-done(((f32[32,8,128]{2,1,0:T(8,128)}), f32[32,8,128]{2,1,0:T(8,128)S(1)}, u32[]{:S(2)}, u32[]{:S(2)}) %all-to-all-start) | async-done | bytes 131104 | tf_op jit(solution)/shard_map/all_to_all | solution.py:387
  20.1 1.1 %meet.1 = (f32[6,6,2,256]{3,2,1,0:T(2,128)}, f32[32,128]{1,0:T(8,128)S(1)}) custom-call(f32[32,8,128]{2,1,0:T(8,128)S(1)} %all-to-all-done.got_ref, bf16[2,192,128]{2,1,0:T(8,128)(2,1)S(1)} %get-tuple-element.13.corner_ref, f32[8,96,256]{2,1,0:T(8,128)S(1)} %get-tuple-element.14.chain_ref, f32[2,96,256]{2,1,0:T(8,128)S(1)} %tail.1.extra_ref), custom_call_target="tpu_custom_call" | custom-call | flops 2000000000 | bytes 1000000 | tf_op jit(solution)/shard_map/meet/pallas_call | solution.py:428
  21.2 9.9 %all_to_all.10 = f32[32,1,128]{2,1,0:T(1,128)S(1)} all-to-all(f32[32,1,128]{2,1,0:T(1,128)S(1)} %bitcast.22), channel_id=1, replica_groups=mesh['grp'=1,'zs'=32] {'zs'}, dimensions={0} | all-to-all | bytes 32768 | tf_op jit(solution)/shard_map/all_to_all | solution.py:440
  31.0 0.6 %final.1 = f32[2,96]{1,0:T(2,128)} custom-call(f32[32,128]{1,0:T(8,128)S(1)} %bitcast.18, s32[8,128]{1,0:T(8,128)S(1)} %get-tuple-element.17.picked_ref), custom_call_target="tpu_custom_call" | custom-call | tf_op jit(solution)/shard_map/final/pallas_call | solution.py:443
  (1 shorter events, 0.0 us)
Async XLA Ops:
  0.6 14.0 %collective-permute-start.1 = (bf16[6,6,2,256]{3,2,1,0:T(2,128)(2,1)}, bf16[6,6,2,256]{3,2,1,0:T(2,128)(2,1)S(1)}, u32[]{:S(2)}, u32[]{:S(2)}) collective-permute-start(bf16[6,6,2,256]{3,2,1,0:T(2,128)(2,1)} %bitcast.19), channel_id=1, source_target_pairs={{8,0},{9,1},{10,2},{11,3},{12,4},{13,5},{14,6},{15,7},{16,8},{17,9... | collective-permute-start | bytes 110600 | tf_op jit(solution)/shard_map/ppermute | solution.py:28
  5.7 6.1 %collective-permute-start = (bf16[18,6,2,256]{3,2,1,0:T(2,128)(2,1)}, bf16[18,6,2,256]{3,2,1,0:T(2,128)(2,1)S(1)}, u32[]{:S(2)}, u32[]{:S(2)}) collective-permute-start(bf16[18,6,2,256]{3,2,1,0:T(2,128)(2,1)} %bitcast.14), channel_id=1, source_target_pairs={{8,0},{9,1},{10,2},{11,3},{12,4},{13,5},{14,6},{15,7},{16,8},{17,9... | collective-permute-start | bytes 331784 | tf_op jit(solution)/shard_map/ppermute | solution.py:28
  8.0 3.9 %copy-start = (bf16[2,3,3,1,6,2,256]{6,5,4,3,2,1,0:T(2,128)(2,1)S(1)}, bf16[2,3,3,1,6,2,256]{6,5,4,3,2,1,0:T(2,128)(2,1)}, u32[]{:S(2)}) copy-start(bf16[2,3,3,1,6,2,256]{6,5,4,3,2,1,0:T(2,128)(2,1)} %param.12) | copy-start | bytes 331780
  8.0 3.9 %copy-start.1 = (bf16[2,3,1,6,2,256]{5,4,3,2,1,0:T(2,128)(2,1)S(1)}, bf16[2,3,1,6,2,256]{5,4,3,2,1,0:T(2,128)(2,1)}, u32[]{:S(2)}) copy-start(bf16[2,3,1,6,2,256]{5,4,3,2,1,0:T(2,128)(2,1)} %param.11) | copy-start | bytes 110596
  8.0 12.1 %all-to-all-start = ((f32[32,8,128]{2,1,0:T(8,128)}), f32[32,8,128]{2,1,0:T(8,128)S(1)}, u32[]{:S(2)}, u32[]{:S(2)}) async-start(f32[32,8,128]{2,1,0:T(8,128)} %get-tuple-element.10), calls=%async_computation | async-start | bytes 262144 | tf_op jit(solution)/shard_map/all_to_all | solution.py:387
  11.8 2.8 %copy-start.2 = (s32[8,128]{1,0:T(8,128)S(1)}, s32[8,128]{1,0:T(8,128)}, u32[]{:S(2)}) copy-start(s32[8,128]{1,0:T(8,128)} %get-tuple-element.12.request_ref) | copy-start | bytes 12292
  11.8 2.8 %copy-start.3 = (f32[8,128]{1,0:T(8,128)S(1)}, f32[8,128]{1,0:T(8,128)}, u32[]{:S(2)}) copy-start(f32[8,128]{1,0:T(8,128)} %get-tuple-element.11.table_ref) | copy-start | bytes 12292
  11.9 7.3 %collective-permute-start.2 = (bf16[18,2,256]{2,1,0:T(2,128)(2,1)S(1)}, bf16[18,2,256]{2,1,0:T(2,128)(2,1)S(1)}, u32[]{:S(2)}, u32[]{:S(2)}) collective-permute-start(bf16[18,2,256]{2,1,0:T(2,128)(2,1)S(1)} %edge.1), channel_id=1, source_target_pairs={{16,0},{17,1},{18,2},{19,3},{20,4},{21,5},{22,6},{23,7},{24,8},{25... | collective-permute-start | bytes 55304 | tf_op jit(solution)/shard_map/ppermute | solution.py:28

commit v8 on v7

--- a/solution.py
+++ b/solution.py
@@ -275,7 +275,18 @@
             vecs = vecs[:-1]
 
 
-def meet_kernel(block_z, block_x, got_ref, corner_ref, chain_ref, extra_ref, seq_ref, table_ref):
+def meet_kernel(
+    block_z,
+    block_x,
+    got_ref,
+    corner_ref,
+    chain_ref,
+    extra_ref,
+    seq_ref,
+    table_ref,
+    seq_rows,
+    seq_done,
+):
     rows_y = got_ref.shape[0] * NT
     got = got_ref[...].reshape(rows_y, LANES)
     high, low = split_two(got)
@@ -288,7 +299,9 @@
     for comp in range(6):
         for z in range(block_z):
             at = comp * CROWS + z * block_x
-            seq_ref[comp, z] = seq[at : at + block_x]
+            seq_rows[comp, z] = seq[at : at + block_x]
+    copy = pltpu.make_async_copy(seq_rows, seq_ref, seq_done)
+    copy.start()
     turned = jnp.concatenate([-seq[3 * CROWS :], seq[: 3 * CROWS]], axis=0)
     sums = []
     for length in range(LMAX):
@@ -309,11 +322,16 @@
         table = table + pltpu.roll(table, shift, 1)
     mine = iota((2 * LMAX, LANES), 1) // NT == iota((2 * LMAX, LANES), 0)
     flat = jnp.sum(jnp.where(mine, table, 0.0), axis=0, keepdims=True)
-    table_ref[...] = jnp.broadcast_to(flat, table_ref.shape)
-
-
-def final_kernel(tables_ref, picked_ref, out_ref):
-    total = jnp.sum(tables_ref[...], axis=0, keepdims=True)
+    table_ref[...] = flat
+    copy.wait()
+
+
+def sum_kernel(mine_ref, other_ref, out_ref):
+    out_ref[...] = mine_ref[...] + other_ref[...]
+
+
+def final_kernel(mine_ref, other_ref, picked_ref, out_ref):
+    total = mine_ref[...] + other_ref[...]
     picked = picked_ref[...]
     value = jnp.take_along_axis(
         jnp.broadcast_to(total, picked.shape), jnp.maximum(picked, 0), axis=1
@@ -429,25 +447,39 @@
         functools.partial(meet_kernel, block_z, block_x),
         out_shape=(
             jax.ShapeDtypeStruct((6, block_z, block_x, rows_y), F32),
-            jax.ShapeDtypeStruct((devices, LANES), F32),
+            jax.ShapeDtypeStruct((1, LANES), F32),
         ),
         in_specs=[VMEM] * 4,
-        out_specs=(VMEM, VMEM),
+        out_specs=(pl.BlockSpec(memory_space=pl.ANY), VMEM),
+        scratch_shapes=[
+            pltpu.VMEM((6, block_z, block_x, rows_y), F32),
+            pltpu.SemaphoreType.DMA,
+        ],
         compiler_params=PARAMS,
         cost_estimate=cost(2_000_000_000, 1_000_000),
         name="meet",
     )(got, corner, chain, extra)
-    tables = lax.all_to_all(
-        partial.reshape(devices, 1, LANES), "zs", split_axis=0, concat_axis=0, tiled=True
-    ).reshape(devices, LANES)
+    bit = 1
+    while bit < devices:
+        other = lax.ppermute(partial, "zs", [(i, i ^ bit) for i in range(devices)])
+        bit *= 2
+        if bit < devices:
+            partial = pl.pallas_call(
+                sum_kernel,
+                out_shape=jax.ShapeDtypeStruct((1, LANES), F32),
+                in_specs=[VMEM] * 2,
+                out_specs=VMEM,
+                compiler_params=PARAMS,
+                name="sum",
+            )(partial, other)
     owned = pl.pallas_call(
         final_kernel,
         out_shape=jax.ShapeDtypeStruct((2, MOST), F32),
-        in_specs=[VMEM] * 2,
+        in_specs=[VMEM] * 3,
         out_specs=VMEM,
         compiler_params=PARAMS,
         name="final",
-    )(tables, picked)
+    )(partial, other, picked)
     return (seq.reshape(2, 3, 1, block_z, block_x, rows_y), owned.T)
 
 

time: 31.9 us -> 38.4 us (1.20)
  waiting for transfers between devices: 3.8 us -> 16.7 us
  blocking collectives: 9.88 us -> 0 us
  starting transfers between devices: 12.1 us -> 15.5 us
    ppermute x0 -> x5, waiting for transfers between devices: none -> 12.9 us  [shards(): other = lax.ppermute(partial, 'zs', [(i, i ^ bit) for i in range(devices)])]
    all_to_all x1 -> x0, blocking collectives: 9.88 us -> none  [shards(): lax.all_to_all(partial.reshape(devices, 1, LANES), 'zs', split_axis=0, co...]
    ppermute x0 -> x5, starting transfers between devices: none -> 3.4 us  [shards(): other = lax.ppermute(partial, 'zs', [(i, i ^ bit) for i in range(devices)])]
  transfers between devices with their start and end apart: 4 -> 9, of which waited for: 2 -> 7; matrix products, arithmetic and copies ran while one was open for 0% -> 0% of each run, Pallas kernels for 11% -> 9%
where the time goes in v8:
time: 38.4 us; the launch traced here: 38.2 us
  waiting for transfers between devices  16.7 us (43%)
  starting transfers between devices  15.5 us (40%)
  Pallas kernels  5.21 us (14%)
  between operations  0.71 us (2%)
    ppermute x5, waiting for transfers between devices, shards(): other = lax.ppermute(partial, 'zs', [(i, i ^ bit) for i in range(devices)])  12.9 us
    ppermute x3, starting transfers between devices, passed_along(): return lax.ppermute(block, axis, route)  8.29 us
    all_to_all x1, starting transfers between devices, shards(): got = lax.all_to_all(payload, 'zs', split_axis=0, concat_axis=0, tiled=True)  3.84 us
    ppermute x5, starting transfers between devices, shards(): other = lax.ppermute(partial, 'zs', [(i, i ^ bit) for i in range(devices)])  3.4 us
    ppermute x3, waiting for transfers between devices, passed_along(): return lax.ppermute(block, axis, route)  3.1 us
    pallas_call x1, Pallas kernels, shards(): pl.pallas_call(functools.partial(pack_kernel, block_z, block_x), out_shap...  1.81 us
    pallas_call x1, Pallas kernels, shards(): pl.pallas_call(functools.partial(chain_kernel, depth_z, scale, block_z, b...  1.42 us
    pallas_call x1, Pallas kernels, shards(): pl.pallas_call(functools.partial(meet_kernel, block_z, block_x), out_shap...  1.08 us
  transfers between devices with their start and end apart: 9, of which 7 were waited for; matrix products, arithmetic and copies ran while one was open for 0% of the time, Pallas kernels for 9%

profile of v8, /device:TPU:0, one launch (start us, length us, event | category | flops | bytes accessed | tf_op | source)
XLA Modules:
  0.0 38.2 jit_solution(9218098348460563126)
XLA Ops:
  0.6 5.1 %collective-permute-start.1 = (bf16[6,6,2,256]{3,2,1,0:T(2,128)(2,1)}, bf16[6,6,2,256]{3,2,1,0:T(2,128)(2,1)S(1)}, u32[]{:S(2)}, u32[]{:S(2)}) collective-permute-start(bf16[6,6,2,256]{3,2,1,0:T(2,128)(2,1)} %bitcast.14), channel_id=1, source_target_pairs={{8,0},{9,1},{10,2},{11,3},{12,4},{13,5},{14,6},{15,7},{16,8},{17,9... | collective-permute-start | bytes 110600 | tf_op jit(solution)/shard_map/ppermute | solution.py:28
  5.7 0.4 %collective-permute-start = (bf16[18,6,2,256]{3,2,1,0:T(2,128)(2,1)}, bf16[18,6,2,256]{3,2,1,0:T(2,128)(2,1)S(1)}, u32[]{:S(2)}, u32[]{:S(2)}) collective-permute-start(bf16[18,6,2,256]{3,2,1,0:T(2,128)(2,1)} %bitcast.10), channel_id=1, source_target_pairs={{8,0},{9,1},{10,2},{11,3},{12,4},{13,5},{14,6},{15,7},{16,8},{17,9... | collective-permute-start | bytes 331784 | tf_op jit(solution)/shard_map/ppermute | solution.py:28
  6.2 1.8 %pack.1 = (f32[32,8,128]{2,1,0:T(8,128)}, s32[8,128]{1,0:T(8,128)}, f32[8,128]{1,0:T(8,128)}) custom-call(f32[8]{0:T(128)} %weight_ref.1, s32[3,8]{1,0:T(4,128)} %bitcast.21, bf16[2,3,8,384]{3,2,1,0:T(8,128)(2,1)} %up_ref.1, bf16[2,3,8,384]{3,2,1,0:T(8,128)(2,1)} %down_ref.1, s32[8,128]{1,0:T(8,128)} %bitcast.18, s32[8,128]{1,0:T(8,128)} %bitcast.19, ...), custom_call_target="tpu_custom_call" | custom-call | flops 2000000000 | bytes 400000 | tf_op jit(solution)/shard_map/pack/pallas_call | solution.py:377
  8.0 0.0 copy-start
  8.0 0.0 copy-start.1
  8.0 3.8 %all-to-all-start = ((f32[32,8,128]{2,1,0:T(8,128)}), f32[32,8,128]{2,1,0:T(8,128)S(1)}, u32[]{:S(2)}, u32[]{:S(2)}) async-start(f32[32,8,128]{2,1,0:T(8,128)} %get-tuple-element.10), calls=%async_computation | async-start | bytes 262144 | tf_op jit(solution)/shard_map/all_to_all | solution.py:405
  11.8 0.0 copy-start.2
  11.9 0.0 copy-start.3
  11.9 0.0 collective-permute-done.links_next_ref.ready_ref
  11.9 0.0 copy-done
  11.9 0.0 copy-done.1
  11.9 2.7 %collective-permute-start.2 = (bf16[18,2,256]{2,1,0:T(2,128)(2,1)S(1)}, bf16[18,2,256]{2,1,0:T(2,128)(2,1)S(1)}, u32[]{:S(2)}, u32[]{:S(2)}) collective-permute-start(bf16[18,2,256]{2,1,0:T(2,128)(2,1)S(1)} %edge.1), channel_id=1, source_target_pairs={{16,0},{17,1},{18,2},{19,3},{20,4},{21,5},{22,6},{23,7},{24,8},{25... | collective-permute-start | bytes 55304 | tf_op jit(solution)/shard_map/ppermute | solution.py:28
  14.7 0.0 collective-permute-done.1.forward_next_ref
  14.7 0.0 copy-done.2
  14.7 0.0 copy-done.3
  14.7 1.4 %chain.1 = (f32[8,96,256]{2,1,0:T(8,128)S(1)}, bf16[2,192,128]{2,1,0:T(8,128)(2,1)S(1)}, s32[8,128]{1,0:T(8,128)S(1)}) custom-call(f32[8,128]{1,0:T(8,128)S(1)} %copy-done.3, s32[8,128]{1,0:T(8,128)S(1)} %copy-done.2, bf16[18,6,2,256]{3,2,1,0:T(2,128)(2,1)S(1)} %bitcast.12, bf16[18,6,2,256]{3,2,1,0:T(2,128)(2,1)S(1)} %collective-permute-done.links_next_ref.ready_ref, ...), custom_call_target="tpu_custom_call" | custom-call | flops 3000000000 | bytes 200000 | tf_op jit(solution)/shard_map/chain/pallas_call | solution.py:418
  16.1 3.1 %collective-permute-done.2.edge_ref = bf16[18,2,256]{2,1,0:T(2,128)(2,1)S(1)} collective-permute-done((bf16[18,2,256]{2,1,0:T(2,128)(2,1)S(1)}, bf16[18,2,256]{2,1,0:T(2,128)(2,1)S(1)}, u32[]{:S(2)}, u32[]{:S(2)}) %collective-permute-start.2) | collective-permute-done | bytes 18464 | tf_op jit(solution)/shard_map/ppermute | solution.py:28
  19.2 0.2 tail.1.extra_ref
  19.4 0.7 %all-to-all-done.got_ref = f32[32,8,128]{2,1,0:T(8,128)S(1)} async-done(((f32[32,8,128]{2,1,0:T(8,128)}), f32[32,8,128]{2,1,0:T(8,128)S(1)}, u32[]{:S(2)}, u32[]{:S(2)}) %all-to-all-start) | async-done | bytes 131104 | tf_op jit(solution)/shard_map/all_to_all | solution.py:405
  20.1 1.1 %meet.1 = (f32[6,6,2,256]{3,2,1,0:T(2,128)}, f32[1,128]{1,0:T(1,128)S(1)}) custom-call(f32[32,8,128]{2,1,0:T(8,128)S(1)} %all-to-all-done.got_ref, bf16[2,192,128]{2,1,0:T(8,128)(2,1)S(1)} %get-tuple-element.13.corner_ref, f32[8,96,256]{2,1,0:T(8,128)S(1)} %get-tuple-element.14.chain_ref, f32[2,96,256]{2,1,0:T(8,128)S(1)} %tail.1.extra_ref), custom_call_target="tpu_custom_call" | custom-call | flops 2000000000 | bytes 1000000 | tf_op jit(solution)/shard_map/meet/pallas_call | solution.py:446
  21.2 0.4 %collective-permute-start.3 = (f32[1,128]{1,0:T(1,128)S(1)}, f32[1,128]{1,0:T(1,128)S(1)}, u32[]{:S(2)}, u32[]{:S(2)}) collective-permute-start(f32[1,128]{1,0:T(1,128)S(1)} %get-tuple-element.16.mine_ref), channel_id=1, source_target_pairs={{0,1},{1,0},{2,3},{3,2},{4,5},{5,4},{6,7},{7,6},{8,9},{9,8},{10,11... | collective-permute-start | bytes 1544 | tf_op jit(solution)/shard_map/ppermute | solution.py:464
  21.7 0.8 %collective-permute-done.3.other_ref = f32[1,128]{1,0:T(1,128)S(1)} collective-permute-done((f32[1,128]{1,0:T(1,128)S(1)}, f32[1,128]{1,0:T(1,128)S(1)}, u32[]{:S(2)}, u32[]{:S(2)}) %collective-permute-start.3) | collective-permute-done | bytes 544 | tf_op jit(solution)/shard_map/ppermute | solution.py:464
  22.5 0.7 %collective-permute-start.4 = (f32[1,128]{1,0:T(1,128)S(1)}, f32[1,128]{1,0:T(1,128)S(1)}, u32[]{:S(2)}, u32[]{:S(2)}) collective-permute-start(f32[1,128]{1,0:T(1,128)S(1)} %sum.4.mine_ref), channel_id=1, source_target_pairs={{0,2},{1,3},{2,0},{3,1},{4,6},{5,7},{6,4},{7,5},{8,10},{9,11},{10,... | collective-permute-start | bytes 1544 | tf_op jit(solution)/shard_map/ppermute | solution.py:464
  23.2 2.8 %collective-permute-done.4.other_ref = f32[1,128]{1,0:T(1,128)S(1)} collective-permute-done((f32[1,128]{1,0:T(1,128)S(1)}, f32[1,128]{1,0:T(1,128)S(1)}, u32[]{:S(2)}, u32[]{:S(2)}) %collective-permute-start.4) | collective-permute-done | bytes 544 | tf_op jit(solution)/shard_map/ppermute | solution.py:464
  26.0 0.7 %collective-permute-start.5 = (f32[1,128]{1,0:T(1,128)S(1)}, f32[1,128]{1,0:T(1,128)S(1)}, u32[]{:S(2)}, u32[]{:S(2)}) collective-permute-start(f32[1,128]{1,0:T(1,128)S(1)} %sum.5.mine_ref), channel_id=1, source_target_pairs={{0,4},{1,5},{2,6},{3,7},{4,0},{5,1},{6,2},{7,3},{8,12},{9,13},{10,... | collective-permute-start | bytes 1544 | tf_op jit(solution)/shard_map/ppermute | solution.py:464
  26.7 2.8 %collective-permute-done.5.other_ref = f32[1,128]{1,0:T(1,128)S(1)} collective-permute-done((f32[1,128]{1,0:T(1,128)S(1)}, f32[1,128]{1,0:T(1,128)S(1)}, u32[]{:S(2)}, u32[]{:S(2)}) %collective-permute-start.5) | collective-permute-done | bytes 544 | tf_op jit(solution)/shard_map/ppermute | solution.py:464
  29.6 0.7 %collective-permute-start.6 = (f32[1,128]{1,0:T(1,128)S(1)}, f32[1,128]{1,0:T(1,128)S(1)}, u32[]{:S(2)}, u32[]{:S(2)}) collective-permute-start(f32[1,128]{1,0:T(1,128)S(1)} %sum.6.mine_ref), channel_id=1, source_target_pairs={{0,8},{1,9},{2,10},{3,11},{4,12},{5,13},{6,14},{7,15},{8,0},{9,1},... | collective-permute-start | bytes 1544 | tf_op jit(solution)/shard_map/ppermute | solution.py:464
  30.2 2.9 %collective-permute-done.6.other_ref = f32[1,128]{1,0:T(1,128)S(1)} collective-permute-done((f32[1,128]{1,0:T(1,128)S(1)}, f32[1,128]{1,0:T(1,128)S(1)}, u32[]{:S(2)}, u32[]{:S(2)}) %collective-permute-start.6) | collective-permute-done | bytes 544 | tf_op jit(solution)/shard_map/ppermute | solution.py:464
  33.1 0.9 %collective-permute-start.7 = (f32[1,128]{1,0:T(1,128)S(1)}, f32[1,128]{1,0:T(1,128)S(1)}, u32[]{:S(2)}, u32[]{:S(2)}) collective-permute-start(f32[1,128]{1,0:T(1,128)S(1)} %sum.7.mine_ref), channel_id=1, source_target_pairs={{0,16},{1,17},{2,18},{3,19},{4,20},{5,21},{6,22},{7,23},{8,24},{9,... | collective-permute-start | bytes 1544 | tf_op jit(solution)/shard_map/ppermute | solution.py:464
  34.0 3.6 %collective-permute-done.7.other_ref = f32[1,128]{1,0:T(1,128)S(1)} collective-permute-done((f32[1,128]{1,0:T(1,128)S(1)}, f32[1,128]{1,0:T(1,128)S(1)}, u32[]{:S(2)}, u32[]{:S(2)}) %collective-permute-start.7) | collective-permute-done | bytes 544 | tf_op jit(solution)/shard_map/ppermute | solution.py:464
  37.6 0.6 %final.1 = f32[2,96]{1,0:T(2,128)} custom-call(f32[1,128]{1,0:T(1,128)S(1)} %sum.7.mine_ref, f32[1,128]{1,0:T(1,128)S(1)} %collective-permute-done.7.other_ref, s32[8,128]{1,0:T(8,128)S(1)} %get-tuple-element.17.picked_ref), custom_call_target="tpu_custom_call" | custom-call | tf_op jit(solution)/shard_map/final/pallas_call | solution.py:475
  (5 shorter events, 0.1 us)
Async XLA Ops:
  0.6 14.1 %collective-permute-start.1 = (bf16[6,6,2,256]{3,2,1,0:T(2,128)(2,1)}, bf16[6,6,2,256]{3,2,1,0:T(2,128)(2,1)S(1)}, u32[]{:S(2)}, u32[]{:S(2)}) collective-permute-start(bf16[6,6,2,256]{3,2,1,0:T(2,128)(2,1)} %bitcast.14), channel_id=1, source_target_pairs={{8,0},{9,1},{10,2},{11,3},{12,4},{13,5},{14,6},{15,7},{16,8},{17,9... | collective-permute-start | bytes 110600 | tf_op jit(solution)/shard_map/ppermute | solution.py:28
  5.7 6.1 %collective-permute-start = (bf16[18,6,2,256]{3,2,1,0:T(2,128)(2,1)}, bf16[18,6,2,256]{3,2,1,0:T(2,128)(2,1)S(1)}, u32[]{:S(2)}, u32[]{:S(2)}) collective-permute-start(bf16[18,6,2,256]{3,2,1,0:T(2,128)(2,1)} %bitcast.10), channel_id=1, source_target_pairs={{8,0},{9,1},{10,2},{11,3},{12,4},{13,5},{14,6},{15,7},{16,8},{17,9... | collective-permute-start | bytes 331784 | tf_op jit(solution)/shard_map/ppermute | solution.py:28
  8.0 3.9 %copy-start = (bf16[2,3,3,1,6,2,256]{6,5,4,3,2,1,0:T(2,128)(2,1)S(1)}, bf16[2,3,3,1,6,2,256]{6,5,4,3,2,1,0:T(2,128)(2,1)}, u32[]{:S(2)}) copy-start(bf16[2,3,3,1,6,2,256]{6,5,4,3,2,1,0:T(2,128)(2,1)} %param.12) | copy-start | bytes 331780
  8.0 3.9 %copy-start.1 = (bf16[2,3,1,6,2,256]{5,4,3,2,1,0:T(2,128)(2,1)S(1)}, bf16[2,3,1,6,2,256]{5,4,3,2,1,0:T(2,128)(2,1)}, u32[]{:S(2)}) copy-start(bf16[2,3,1,6,2,256]{5,4,3,2,1,0:T(2,128)(2,1)} %param.11) | copy-start | bytes 110596
  8.0 12.1 %all-to-all-start = ((f32[32,8,128]{2,1,0:T(8,128)}), f32[32,8,128]{2,1,0:T(8,128)S(1)}, u32[]{:S(2)}, u32[]{:S(2)}) async-start(f32[32,8,128]{2,1,0:T(8,128)} %get-tuple-element.10), calls=%async_computation | async-start | bytes 262144 | tf_op jit(solution)/shard_map/all_to_all | solution.py:405
  11.8 2.8 %copy-start.2 = (s32[8,128]{1,0:T(8,128)S(1)}, s32[8,128]{1,0:T(8,128)}, u32[]{:S(2)}) copy-start(s32[8,128]{1,0:T(8,128)} %get-tuple-element.12.request_ref) | copy-start | bytes 12292
  11.9 2.8 %copy-start.3 = (f32[8,128]{1,0:T(8,128)S(1)}, f32[8,128]{1,0:T(8,128)}, u32[]{:S(2)}) copy-start(f32[8,128]{1,0:T(8,128)} %get-tuple-element.11.table_ref) | copy-start | bytes 12292
  11.9 7.3 %collective-permute-start.2 = (bf16[18,2,256]{2,1,0:T(2,128)(2,1)S(1)}, bf16[18,2,256]{2,1,0:T(2,128)(2,1)S(1)}, u32[]{:S(2)}, u32[]{:S(2)}) collective-permute-start(bf16[18,2,256]{2,1,0:T(2,128)(2,1)S(1)} %edge.1), channel_id=1, source_target_pairs={{16,0},{17,1},{18,2},{19,3},{20,4},{21,5},{22,6},{23,7},{24,8},{25... | collective-permute-start | bytes 55304 | tf_op jit(solution)/shard_map/ppermute | solution.py:28
  21.2 1.3 %collective-permute-start.3 = (f32[1,128]{1,0:T(1,128)S(1)}, f32[1,128]{1,0:T(1,128)S(1)}, u32[]{:S(2)}, u32[]{:S(2)}) collective-permute-start(f32[1,128]{1,0:T(1,128)S(1)} %get-tuple-element.16.mine_ref), channel_id=1, source_target_pairs={{0,1},{1,0},{2,3},{3,2},{4,5},{5,4},{6,7},{7,6},{8,9},{9,8},{10,11... | collective-permute-start | bytes 1544 | tf_op jit(solution)/shard_map/ppermute | solution.py:464
  22.5 3.5 %collective-permute-start.4 = (f32[1,128]{1,0:T(1,128)S(1)}, f32[1,128]{1,0:T(1,128)S(1)}, u32[]{:S(2)}, u32[]{:S(2)}) collective-permute-start(f32[1,128]{1,0:T(1,128)S(1)} %sum.4.mine_ref), channel_id=1, source_target_pairs={{0,2},{1,3},{2,0},{3,1},{4,6},{5,7},{6,4},{7,5},{8,10},{9,11},{10,... | collective-permute-start | bytes 1544 | tf_op jit(solution)/shard_map/ppermute | solution.py:464
  26.0 3.5 %collective-permute-start.5 = (f32[1,128]{1,0:T(1,128)S(1)}, f32[1,128]{1,0:T(1,128)S(1)}, u32[]{:S(2)}, u32[]{:S(2)}) collective-permute-start(f32[1,128]{1,0:T(1,128)S(1)} %sum.5.mine_ref), channel_id=1, source_target_pairs={{0,4},{1,5},{2,6},{3,7},{4,0},{5,1},{6,2},{7,3},{8,12},{9,13},{10,... | collective-permute-start | bytes 1544 | tf_op jit(solution)/shard_map/ppermute | solution.py:464
  29.6 3.5 %collective-permute-start.6 = (f32[1,128]{1,0:T(1,128)S(1)}, f32[1,128]{1,0:T(1,128)S(1)}, u32[]{:S(2)}, u32[]{:S(2)}) collective-permute-start(f32[1,128]{1,0:T(1,128)S(1)} %sum.6.mine_ref), channel_id=1, source_target_pairs={{0,8},{1,9},{2,10},{3,11},{4,12},{5,13},{6,14},{7,15},{8,0},{9,1},... | collective-permute-start | bytes 1544 | tf_op jit(solution)/shard_map/ppermute | solution.py:464
  33.1 4.4 %collective-permute-start.7 = (f32[1,128]{1,0:T(1,128)S(1)}, f32[1,128]{1,0:T(1,128)S(1)}, u32[]{:S(2)}, u32[]{:S(2)}) collective-permute-start(f32[1,128]{1,0:T(1,128)S(1)} %sum.7.mine_ref), channel_id=1, source_target_pairs={{0,16},{1,17},{2,18},{3,19},{4,20},{5,21},{6,22},{7,23},{8,24},{9,... | collective-permute-start | bytes 1544 | tf_op jit(solution)/shard_map/ppermute | solution.py:464

commit v9 on v7

--- a/solution.py
+++ b/solution.py
@@ -285,10 +285,7 @@
     both = dot(corner_ref[0], high) + dot(corner_ref[0], low) + dot(corner_ref[1], high)
     size = 6 * CROWS
     seq = both[:size] + pltpu.roll(both[size:], rows_y - NT, 1)
-    for comp in range(6):
-        for z in range(block_z):
-            at = comp * CROWS + z * block_x
-            seq_ref[comp, z] = seq[at : at + block_x]
+    seq_ref[...] = seq
     turned = jnp.concatenate([-seq[3 * CROWS :], seq[: 3 * CROWS]], axis=0)
     sums = []
     for length in range(LMAX):
@@ -310,6 +307,14 @@
     mine = iota((2 * LMAX, LANES), 1) // NT == iota((2 * LMAX, LANES), 0)
     flat = jnp.sum(jnp.where(mine, table, 0.0), axis=0, keepdims=True)
     table_ref[...] = jnp.broadcast_to(flat, table_ref.shape)
+
+
+def store_kernel(rows_ref, seq_ref):
+    block_z, block_x = seq_ref.shape[1:3]
+    for comp in range(6):
+        for z in range(block_z):
+            at = comp * CROWS + z * block_x
+            seq_ref[comp, z] = rows_ref[at : at + block_x]
 
 
 def final_kernel(tables_ref, picked_ref, out_ref):
@@ -425,10 +430,10 @@
         name="tail",
     )(links, links_next, edge_next, corner)
 
-    seq, partial = pl.pallas_call(
+    seq_rows, partial = pl.pallas_call(
         functools.partial(meet_kernel, block_z, block_x),
         out_shape=(
-            jax.ShapeDtypeStruct((6, block_z, block_x, rows_y), F32),
+            jax.ShapeDtypeStruct((6 * CROWS, rows_y), F32),
             jax.ShapeDtypeStruct((devices, LANES), F32),
         ),
         in_specs=[VMEM] * 4,
@@ -440,6 +445,15 @@
     tables = lax.all_to_all(
         partial.reshape(devices, 1, LANES), "zs", split_axis=0, concat_axis=0, tiled=True
     ).reshape(devices, LANES)
+    seq = pl.pallas_call(
+        store_kernel,
+        out_shape=jax.ShapeDtypeStruct((6, block_z, block_x, rows_y), F32),
+        in_specs=[VMEM],
+        out_specs=VMEM,
+        compiler_params=PARAMS,
+        cost_estimate=cost(2_000_000_000, 200_000),
+        name="store",
+    )(seq_rows)
     owned = pl.pallas_call(
         final_kernel,
         out_shape=jax.ShapeDtypeStruct((2, MOST), F32),

time: 31.9 us -> 32.4 us (1.016)
  blocking collectives: 9.88 us -> 0 us
  waiting for transfers between devices: 3.8 us -> 10.3 us
  starting transfers between devices: 12.1 us -> 15.1 us
  Pallas kernels: 5.17 us -> 6.09 us
    all_to_all x1 -> x0, blocking collectives: 9.88 us -> none  [shards(): lax.all_to_all(partial.reshape(devices, 1, LANES), 'zs', split_axis=0, co...]
    all_to_all x0 -> x1, waiting for transfers between devices: none -> 6.48 us  [shards(): lax.all_to_all(partial.reshape(devices, 1, LANES), 'zs', split_axis=0, co...]
    all_to_all x0 -> x1, starting transfers between devices: none -> 2.93 us  [shards(): lax.all_to_all(partial.reshape(devices, 1, LANES), 'zs', split_axis=0, co...]
    pallas_call x0 -> x1, Pallas kernels: none -> 0.66 us  [shards(): pl.pallas_call(store_kernel, out_shape=jax.ShapeDtypeStruct((6, block_z,...]
  transfers between devices with their start and end apart: 4 -> 5, of which waited for: 2 -> 3; matrix products, arithmetic and copies ran while one was open for 0% -> 0% of each run, Pallas kernels for 11% -> 13%
where the time goes in v9:
time: 32.4 us; the launch traced here: 32.1 us
  starting transfers between devices  15.1 us (47%)
  waiting for transfers between devices  10.3 us (32%)
  Pallas kernels  6.09 us (19%)
  between operations  0.71 us (2%)
    ppermute x3, starting transfers between devices, passed_along(): return lax.ppermute(block, axis, route)  8.29 us
    all_to_all x1, waiting for transfers between devices, shards(): lax.all_to_all(partial.reshape(devices, 1, LANES), 'zs', split_axis=0, co...  6.48 us
    all_to_all x1, starting transfers between devices, shards(): got = lax.all_to_all(payload, 'zs', split_axis=0, concat_axis=0, tiled=True)  3.83 us
    ppermute x3, waiting for transfers between devices, passed_along(): return lax.ppermute(block, axis, route)  3.1 us
    all_to_all x1, starting transfers between devices, shards(): lax.all_to_all(partial.reshape(devices, 1, LANES), 'zs', split_axis=0, co...  2.93 us
    pallas_call x1, Pallas kernels, shards(): pl.pallas_call(functools.partial(pack_kernel, block_z, block_x), out_shap...  1.81 us
    pallas_call x1, Pallas kernels, shards(): pl.pallas_call(functools.partial(chain_kernel, depth_z, scale, block_z, b...  1.42 us
    pallas_call x1, Pallas kernels, shards(): pl.pallas_call(functools.partial(meet_kernel, block_z, block_x), out_shap...  1.32 us
  transfers between devices with their start and end apart: 5, of which 3 were waited for; matrix products, arithmetic and copies ran while one was open for 0% of the time, Pallas kernels for 13%

profile of v9, /device:TPU:0, one launch (start us, length us, event | category | flops | bytes accessed | tf_op | source)
XLA Modules:
  0.0 32.1 jit_solution(4712226560391665029)
XLA Ops:
  0.6 5.1 %collective-permute-start.1 = (bf16[6,6,2,256]{3,2,1,0:T(2,128)(2,1)}, bf16[6,6,2,256]{3,2,1,0:T(2,128)(2,1)S(1)}, u32[]{:S(2)}, u32[]{:S(2)}) collective-permute-start(bf16[6,6,2,256]{3,2,1,0:T(2,128)(2,1)} %bitcast.19), channel_id=1, source_target_pairs={{8,0},{9,1},{10,2},{11,3},{12,4},{13,5},{14,6},{15,7},{16,8},{17,9... | collective-permute-start | bytes 110600 | tf_op jit(solution)/shard_map/ppermute | solution.py:28
  5.7 0.4 %collective-permute-start = (bf16[18,6,2,256]{3,2,1,0:T(2,128)(2,1)}, bf16[18,6,2,256]{3,2,1,0:T(2,128)(2,1)S(1)}, u32[]{:S(2)}, u32[]{:S(2)}) collective-permute-start(bf16[18,6,2,256]{3,2,1,0:T(2,128)(2,1)} %bitcast.14), channel_id=1, source_target_pairs={{8,0},{9,1},{10,2},{11,3},{12,4},{13,5},{14,6},{15,7},{16,8},{17,9... | collective-permute-start | bytes 331784 | tf_op jit(solution)/shard_map/ppermute | solution.py:28
  6.2 1.8 %pack.1 = (f32[32,8,128]{2,1,0:T(8,128)}, s32[8,128]{1,0:T(8,128)}, f32[8,128]{1,0:T(8,128)}) custom-call(f32[8]{0:T(128)} %weight_ref.1, s32[3,8]{1,0:T(4,128)} %bitcast.26, bf16[2,3,8,384]{3,2,1,0:T(8,128)(2,1)} %up_ref.1, bf16[2,3,8,384]{3,2,1,0:T(8,128)(2,1)} %down_ref.1, s32[8,128]{1,0:T(8,128)} %bitcast.23, s32[8,128]{1,0:T(8,128)} %bitcast.24, ...), custom_call_target="tpu_custom_call" | custom-call | flops 2000000000 | bytes 400000 | tf_op jit(solution)/shard_map/pack/pallas_call | solution.py:364
  8.0 0.0 copy-start
  8.0 0.0 copy-start.1
  8.0 3.8 %all-to-all-start = ((f32[32,8,128]{2,1,0:T(8,128)}), f32[32,8,128]{2,1,0:T(8,128)S(1)}, u32[]{:S(2)}, u32[]{:S(2)}) async-start(f32[32,8,128]{2,1,0:T(8,128)} %get-tuple-element.10), calls=%async_computation | async-start | bytes 262144 | tf_op jit(solution)/shard_map/all_to_all | solution.py:392
  11.8 0.0 copy-start.2
  11.9 0.0 copy-start.3
  11.9 0.0 collective-permute-done.links_next_ref.ready_ref
  11.9 0.0 copy-done
  11.9 0.0 copy-done.1
  11.9 2.7 %collective-permute-start.2 = (bf16[18,2,256]{2,1,0:T(2,128)(2,1)S(1)}, bf16[18,2,256]{2,1,0:T(2,128)(2,1)S(1)}, u32[]{:S(2)}, u32[]{:S(2)}) collective-permute-start(bf16[18,2,256]{2,1,0:T(2,128)(2,1)S(1)} %edge.1), channel_id=1, source_target_pairs={{16,0},{17,1},{18,2},{19,3},{20,4},{21,5},{22,6},{23,7},{24,8},{25... | collective-permute-start | bytes 55304 | tf_op jit(solution)/shard_map/ppermute | solution.py:28
  14.7 0.0 collective-permute-done.1.forward_next_ref
  14.7 0.0 copy-done.2
  14.7 0.0 copy-done.3
  14.7 1.4 %chain.1 = (f32[8,96,256]{2,1,0:T(8,128)S(1)}, bf16[2,192,128]{2,1,0:T(8,128)(2,1)S(1)}, s32[8,128]{1,0:T(8,128)S(1)}) custom-call(f32[8,128]{1,0:T(8,128)S(1)} %copy-done.3, s32[8,128]{1,0:T(8,128)S(1)} %copy-done.2, bf16[18,6,2,256]{3,2,1,0:T(2,128)(2,1)S(1)} %bitcast.16, bf16[18,6,2,256]{3,2,1,0:T(2,128)(2,1)S(1)} %collective-permute-done.links_next_ref.ready_ref, ...), custom_call_target="tpu_custom_call" | custom-call | flops 3000000000 | bytes 200000 | tf_op jit(solution)/shard_map/chain/pallas_call | solution.py:405
  16.1 3.1 %collective-permute-done.2.edge_ref = bf16[18,2,256]{2,1,0:T(2,128)(2,1)S(1)} collective-permute-done((bf16[18,2,256]{2,1,0:T(2,128)(2,1)S(1)}, bf16[18,2,256]{2,1,0:T(2,128)(2,1)S(1)}, u32[]{:S(2)}, u32[]{:S(2)}) %collective-permute-start.2) | collective-permute-done | bytes 18464 | tf_op jit(solution)/shard_map/ppermute | solution.py:28
  19.2 0.2 tail.1.extra_ref
  19.4 0.7 %all-to-all-done.got_ref = f32[32,8,128]{2,1,0:T(8,128)S(1)} async-done(((f32[32,8,128]{2,1,0:T(8,128)}), f32[32,8,128]{2,1,0:T(8,128)S(1)}, u32[]{:S(2)}, u32[]{:S(2)}) %all-to-all-start) | async-done | bytes 131104 | tf_op jit(solution)/shard_map/all_to_all | solution.py:392
  20.1 1.3 %meet.1 = (f32[96,256]{1,0:T(8,128)S(1)}, f32[32,128]{1,0:T(8,128)}) custom-call(f32[32,8,128]{2,1,0:T(8,128)S(1)} %all-to-all-done.got_ref, bf16[2,192,128]{2,1,0:T(8,128)(2,1)S(1)} %get-tuple-element.13.corner_ref, f32[8,96,256]{2,1,0:T(8,128)S(1)} %get-tuple-element.14.chain_ref, f32[2,96,256]{2,1,0:T(8,128)S(1)} %tail.1.extra_ref), custom_call_target="tpu_custom_call" | custom-call | flops 2000000000 | bytes 1000000 | tf_op jit(solution)/shard_map/meet/pallas_call | solution.py:433
  21.4 2.9 %all-to-all-start.1 = ((f32[32,1,128]{2,1,0:T(1,128)}), f32[32,1,128]{2,1,0:T(1,128)S(1)}, u32[]{:S(2)}, u32[]{:S(2)}) async-start(f32[32,1,128]{2,1,0:T(1,128)} %bitcast.9), calls=%async_computation.1 | async-start | bytes 32768 | tf_op jit(solution)/shard_map/all_to_all | solution.py:445
  24.4 0.7 %store.1 = f32[6,6,2,256]{3,2,1,0:T(2,128)} custom-call(f32[96,256]{1,0:T(8,128)S(1)} %get-tuple-element.15.rows_ref), custom_call_target="tpu_custom_call" | custom-call | flops 2000000000 | bytes 200000 | tf_op jit(solution)/shard_map/store/pallas_call | solution.py:448
  25.0 6.5 %all-to-all-done.1 = f32[32,1,128]{2,1,0:T(1,128)S(1)} async-done(((f32[32,1,128]{2,1,0:T(1,128)}), f32[32,1,128]{2,1,0:T(1,128)S(1)}, u32[]{:S(2)}, u32[]{:S(2)}) %all-to-all-start.1) | async-done | bytes 16416 | tf_op jit(solution)/shard_map/all_to_all | solution.py:445
  31.5 0.6 %final.1 = f32[2,96]{1,0:T(2,128)} custom-call(f32[32,128]{1,0:T(8,128)S(1)} %bitcast.18, s32[8,128]{1,0:T(8,128)S(1)} %get-tuple-element.17.picked_ref), custom_call_target="tpu_custom_call" | custom-call | tf_op jit(solution)/shard_map/final/pallas_call | solution.py:457
  (1 shorter events, 0.0 us)
Async XLA Ops:
  0.6 14.1 %collective-permute-start.1 = (bf16[6,6,2,256]{3,2,1,0:T(2,128)(2,1)}, bf16[6,6,2,256]{3,2,1,0:T(2,128)(2,1)S(1)}, u32[]{:S(2)}, u32[]{:S(2)}) collective-permute-start(bf16[6,6,2,256]{3,2,1,0:T(2,128)(2,1)} %bitcast.19), channel_id=1, source_target_pairs={{8,0},{9,1},{10,2},{11,3},{12,4},{13,5},{14,6},{15,7},{16,8},{17,9... | collective-permute-start | bytes 110600 | tf_op jit(solution)/shard_map/ppermute | solution.py:28
  5.7 6.1 %collective-permute-start = (bf16[18,6,2,256]{3,2,1,0:T(2,128)(2,1)}, bf16[18,6,2,256]{3,2,1,0:T(2,128)(2,1)S(1)}, u32[]{:S(2)}, u32[]{:S(2)}) collective-permute-start(bf16[18,6,2,256]{3,2,1,0:T(2,128)(2,1)} %bitcast.14), channel_id=1, source_target_pairs={{8,0},{9,1},{10,2},{11,3},{12,4},{13,5},{14,6},{15,7},{16,8},{17,9... | collective-permute-start | bytes 331784 | tf_op jit(solution)/shard_map/ppermute | solution.py:28
  8.0 3.9 %copy-start = (bf16[2,3,3,1,6,2,256]{6,5,4,3,2,1,0:T(2,128)(2,1)S(1)}, bf16[2,3,3,1,6,2,256]{6,5,4,3,2,1,0:T(2,128)(2,1)}, u32[]{:S(2)}) copy-start(bf16[2,3,3,1,6,2,256]{6,5,4,3,2,1,0:T(2,128)(2,1)} %param.12) | copy-start | bytes 331780
  8.0 3.9 %copy-start.1 = (bf16[2,3,1,6,2,256]{5,4,3,2,1,0:T(2,128)(2,1)S(1)}, bf16[2,3,1,6,2,256]{5,4,3,2,1,0:T(2,128)(2,1)}, u32[]{:S(2)}) copy-start(bf16[2,3,1,6,2,256]{5,4,3,2,1,0:T(2,128)(2,1)} %param.11) | copy-start | bytes 110596
  8.0 12.1 %all-to-all-start = ((f32[32,8,128]{2,1,0:T(8,128)}), f32[32,8,128]{2,1,0:T(8,128)S(1)}, u32[]{:S(2)}, u32[]{:S(2)}) async-start(f32[32,8,128]{2,1,0:T(8,128)} %get-tuple-element.10), calls=%async_computation | async-start | bytes 262144 | tf_op jit(solution)/shard_map/all_to_all | solution.py:392
  11.8 2.8 %copy-start.2 = (s32[8,128]{1,0:T(8,128)S(1)}, s32[8,128]{1,0:T(8,128)}, u32[]{:S(2)}) copy-start(s32[8,128]{1,0:T(8,128)} %get-tuple-element.12.request_ref) | copy-start | bytes 12292
  11.9 2.8 %copy-start.3 = (f32[8,128]{1,0:T(8,128)S(1)}, f32[8,128]{1,0:T(8,128)}, u32[]{:S(2)}) copy-start(f32[8,128]{1,0:T(8,128)} %get-tuple-element.11.table_ref) | copy-start | bytes 12292
  11.9 7.3 %collective-permute-start.2 = (bf16[18,2,256]{2,1,0:T(2,128)(2,1)S(1)}, bf16[18,2,256]{2,1,0:T(2,128)(2,1)S(1)}, u32[]{:S(2)}, u32[]{:S(2)}) collective-permute-start(bf16[18,2,256]{2,1,0:T(2,128)(2,1)S(1)} %edge.1), channel_id=1, source_target_pairs={{16,0},{17,1},{18,2},{19,3},{20,4},{21,5},{22,6},{23,7},{24,8},{25... | collective-permute-start | bytes 55304 | tf_op jit(solution)/shard_map/ppermute | solution.py:28
  21.4 10.1 %all-to-all-start.1 = ((f32[32,1,128]{2,1,0:T(1,128)}), f32[32,1,128]{2,1,0:T(1,128)S(1)}, u32[]{:S(2)}, u32[]{:S(2)}) async-start(f32[32,1,128]{2,1,0:T(1,128)} %bitcast.9), calls=%async_computation.1 | async-start | bytes 32768 | tf_op jit(solution)/shard_map/all_to_all | solution.py:445

commit v10 on v7

--- a/solution.py
+++ b/solution.py
@@ -37,28 +37,28 @@
     return lax.broadcasted_iota(jnp.int32, shape, axis)
 
 
-def pack_kernel(
-    block_z,
-    block_x,
-    weight_ref,
-    offset_ref,
-    up_ref,
-    down_ref,
-    lengths_ref,
-    separations_ref,
-    owners_ref,
-    out_ref,
-    request_ref,
-    table_ref,
-):
-    codes = lengths_ref[...] * (2 * NT) + separations_ref[...]
-    request_ref[...] = owners_ref[...] * LANES + codes
-    lane = iota((8, LANES), 1)
-    table = jnp.zeros((8, LANES), F32)
-    for k in range(8):
-        corner = offset_ref[0, k] * 4 + offset_ref[1, k] * 2 + offset_ref[2, k]
-        table = jnp.where(lane == corner, weight_ref[k], table)
-    table_ref[...] = table
+def pack_kernel(last_group, block_z, block_x, up_ref, down_ref, *refs):
+    *_, out_ref, up_rows, down_rows, out_rows, done = refs
+    groups = lax.axis_size("zs") // G
+    group = lax.axis_index("zs") // G
+
+    @pl.when((group == groups - 1) == last_group)
+    def _():
+        copies = [
+            pltpu.make_async_copy(up_ref, up_rows, done.at[0]),
+            pltpu.make_async_copy(down_ref, down_rows, done.at[1]),
+        ]
+        for copy in copies:
+            copy.start()
+        for copy in copies:
+            copy.wait()
+        pack_rows(block_z, block_x, up_rows, down_rows, out_rows)
+        copy = pltpu.make_async_copy(out_rows, out_ref, done.at[2])
+        copy.start()
+        copy.wait()
+
+
+def pack_rows(block_z, block_x, up_ref, down_ref, out_ref):
     zh = block_z + 1
     slot_lanes = zh * XH
     width_x = block_x * G
@@ -142,8 +142,11 @@
     scale,
     block_z,
     block_x,
-    table_ref,
-    request_ref,
+    weight_ref,
+    offset_ref,
+    lengths_ref,
+    separations_ref,
+    owners_ref,
     links_ref,
     links_next_ref,
     forward_ref,
@@ -220,7 +223,11 @@
     x_step = lane % slot_lanes // zh - row % block_x
     here = (lane // slot_lanes == (comp + place % G) % 6) & (row % CROWS < count)
     here = here & (x_step >= 0) & (x_step < 2) & (z_step >= 0) & (z_step < 2)
-    table = jnp.broadcast_to(table_ref[0:1], shape)
+    table = jnp.zeros((8, LANES), F32)
+    for k in range(8):
+        corner = offset_ref[0, k] * 4 + offset_ref[1, k] * 2 + offset_ref[2, k]
+        table = jnp.where(iota((8, LANES), 1) == corner, weight_ref[k], table)
+    table = jnp.broadcast_to(table[0:1], shape)
     for y_step in range(2):
         corner = jnp.where(here, 4 * x_step + 2 * y_step + z_step, 0)
         weights = jnp.where(here, jnp.take_along_axis(table, corner, axis=1), 0.0)
@@ -228,9 +235,8 @@
         corner_ref[0, y_step * 6 * CROWS : (y_step + 1) * 6 * CROWS] = high
         corner_ref[1, y_step * 6 * CROWS : (y_step + 1) * 6 * CROWS] = low
 
-    request = request_ref[...]
-    mine = request // LANES == place
-    codes = (request % LANES).astype(F32)
+    mine = owners_ref[...] == place
+    codes = (lengths_ref[...] * (2 * NT) + separations_ref[...]).astype(F32)
     member = jnp.where(mine, 1.0, 0.0)
     below = jnp.where(iota((LANES, LANES), 0) < iota((LANES, LANES), 1), 1.0, 0.0)
     earlier = jnp.dot(member.astype(BF16), below.astype(BF16), preferred_element_type=F32)
@@ -332,6 +338,7 @@
 
 PARAMS = pltpu.CompilerParams(vmem_limit_bytes=16 * 1024 * 1024)
 WIDE_PARAMS = pltpu.CompilerParams(vmem_limit_bytes=60 * 1024 * 1024)
+WHOLE_PARAMS = pltpu.CompilerParams(vmem_limit_bytes=67_100_000)
 
 
 def shards(
@@ -353,40 +360,34 @@
     links = gauge_links.reshape(18, block_z, block_x, rows_y)
     field = forward.reshape(6, block_z, block_x, rows_y)
 
-    links_next = passed_along(links, "zs", -G)
-    field_next = passed_along(field, "zs", -G)
+    def packed(last_group, *payload):
+        anywhere = pl.BlockSpec(memory_space=pl.ANY)
+        return pl.pallas_call(
+            functools.partial(pack_kernel, last_group, block_z, block_x),
+            out_shape=jax.ShapeDtypeStruct((devices, NT, LANES), F32),
+            in_specs=[anywhere] * (2 + len(payload)),
+            out_specs=anywhere,
+            input_output_aliases={2: 0} if payload else {},
+            scratch_shapes=[
+                pltpu.VMEM(quark_up.shape, BF16),
+                pltpu.VMEM(quark_up.shape, BF16),
+                pltpu.VMEM((devices, NT, LANES), F32),
+                pltpu.SemaphoreType.DMA((3,)),
+            ],
+            compiler_params=WIDE_PARAMS if last_group else WHOLE_PARAMS,
+            cost_estimate=cost(2_000_000_000, 400_000) if last_group else cost(1_000, 1_000),
+            name="pack",
+        )(quark_up, quark_down, *payload)
+
+    payload = packed(False)
+    payload, links_out, field_out = lax.optimization_barrier((payload, links, field))
+    links_next = passed_along(links_out, "zs", -G)
+    field_next = passed_along(field_out, "zs", -G)
+    payload = packed(True, payload)
+    got = lax.all_to_all(payload, "zs", split_axis=0, concat_axis=0, tiled=True)
+
+    past = LMAX - block_z
     requests = (lengths.shape[0] // LANES, LANES)
-    payload, request, table = pl.pallas_call(
-        functools.partial(pack_kernel, block_z, block_x),
-        out_shape=(
-            jax.ShapeDtypeStruct((devices, NT, LANES), F32),
-            jax.ShapeDtypeStruct(requests, jnp.int32),
-            jax.ShapeDtypeStruct((8, LANES), F32),
-        ),
-        grid=(1,),
-        in_specs=[SMEM] * 2
-        + [pl.BlockSpec(quark_up.shape, lambda i: (0, 0, 0, 0))] * 2
-        + [pl.BlockSpec(requests, lambda i: (0, 0))] * 3,
-        out_specs=(
-            pl.BlockSpec((devices, NT, LANES), lambda i: (0, 0, 0)),
-            pl.BlockSpec(requests, lambda i: (0, 0)),
-            pl.BlockSpec((8, LANES), lambda i: (0, 0)),
-        ),
-        compiler_params=WIDE_PARAMS,
-        cost_estimate=cost(2_000_000_000, 400_000),
-        name="pack",
-    )(
-        corner_weight,
-        corner_offset.T,
-        quark_up,
-        quark_down,
-        lengths.reshape(requests),
-        separations.reshape(requests),
-        owner_map.reshape(requests),
-    )
-    got = lax.all_to_all(payload, "zs", split_axis=0, concat_axis=0, tiled=True)
-
-    past = LMAX - block_z
     edge = pl.pallas_call(
         edge_kernel,
         out_shape=jax.ShapeDtypeStruct((18, block_x, rows_y), BF16),
@@ -404,7 +405,7 @@
             jax.ShapeDtypeStruct((2, 12 * CROWS, LANES), BF16),
             jax.ShapeDtypeStruct((8, LANES), jnp.int32),
         ),
-        in_specs=[VMEM] * 6,
+        in_specs=[SMEM] * 2 + [VMEM] * 7,
         out_specs=(VMEM,) * 3,
         scratch_shapes=[
             pltpu.VMEM((18, 2 * block_z * block_x, rows_y), F32),
@@ -413,7 +414,17 @@
         compiler_params=PARAMS,
         cost_estimate=cost(3_000_000_000, 200_000),
         name="chain",
-    )(table, request, links, links_next, field, field_next)
+    )(
+        corner_weight,
+        corner_offset.T,
+        lengths.reshape(requests),
+        separations.reshape(requests),
+        owner_map.reshape(requests),
+        links,
+        links_next,
+        field,
+        field_next,
+    )
 
     extra = pl.pallas_call(
         functools.partial(tail_kernel, depth_z, scale, block_z, block_x),

time: 31.9 us -> 32.6 us (1.022)
  waiting for transfers between devices: 3.8 us -> 2.55 us
  local copies, waits for them, and re-layouts: 0.02 us -> 0.69 us
  starting transfers between devices: 12.1 us -> 12.7 us
  Pallas kernels: 5.17 us -> 5.75 us
    ppermute x3, waiting for transfers between devices: 3.1 us -> 1.84 us  [passed_along(): return lax.ppermute(block, axis, route)]
    unnamed x8 -> x14, local copies, waits for them, and re-layouts: 0.02 us -> 0.69 us
    all_to_all x1, starting transfers between devices: 3.83 us -> 4.45 us  [shards(): got = lax.all_to_all(payload, 'zs', split_axis=0, concat_axis=0, tiled=True)]
    pallas_call x1, Pallas kernels: 1.42 us -> 1.99 us  [shards(): pl.pallas_call(functools.partial(chain_kernel, depth_z, scale, block_z, b...]
    pallas_call x1 -> x2, Pallas kernels: 1.8 us -> 1.82 us  [packed(): pl.pallas_call(functools.partial(pack_kernel, last_group, block_z, block_...]
  transfers between devices with their start and end apart: 4 -> 4, of which waited for: 2 -> 2; matrix products, arithmetic and copies ran while one was open for 0% -> 0% of each run, Pallas kernels for 11% -> 7%
where the time goes in v10:
time: 32.6 us; the launch traced here: 32.4 us
  starting transfers between devices  12.7 us (39%)
  blocking collectives  9.88 us (30%)
  Pallas kernels  5.75 us (18%)
  waiting for transfers between devices  2.55 us (8%)
  between operations  0.75 us (2%)
  local copies, waits for them, and re-layouts  0.69 us (2%)
    all_to_all x1, blocking collectives, shards(): lax.all_to_all(partial.reshape(devices, 1, LANES), 'zs', split_axis=0, co...  9.88 us
    ppermute x3, starting transfers between devices, passed_along(): return lax.ppermute(block, axis, route)  8.28 us
    all_to_all x1, starting transfers between devices, shards(): got = lax.all_to_all(payload, 'zs', split_axis=0, concat_axis=0, tiled=True)  4.45 us
    pallas_call x1, Pallas kernels, shards(): pl.pallas_call(functools.partial(chain_kernel, depth_z, scale, block_z, b...  1.99 us
    ppermute x3, waiting for transfers between devices, passed_along(): return lax.ppermute(block, axis, route)  1.84 us
    pallas_call x2, Pallas kernels, packed(): pl.pallas_call(functools.partial(pack_kernel, last_group, block_z, block_...  1.82 us
    pallas_call x1, Pallas kernels, shards(): pl.pallas_call(functools.partial(meet_kernel, block_z, block_x), out_shap...  1.07 us
    all_to_all x1, waiting for transfers between devices, shards(): got = lax.all_to_all(payload, 'zs', split_axis=0, concat_axis=0, tiled=True)  0.7 us
  transfers between devices with their start and end apart: 4, of which 2 were waited for; matrix products, arithmetic and copies ran while one was open for 0% of the time, Pallas kernels for 7%

profile of v10, /device:TPU:0, one launch (start us, length us, event | category | flops | bytes accessed | tf_op | source)
XLA Modules:
  0.0 32.4 jit_solution(1030146038844901700)
XLA Ops:
  0.6 1.8 %pack.2.refs_0_ = f32[32,8,128]{2,1,0:T(8,128)} custom-call(bf16[2,3,8,384]{3,2,1,0:T(8,128)(2,1)} %up_ref.3, bf16[2,3,8,384]{3,2,1,0:T(8,128)(2,1)} %down_ref.3), custom_call_target="tpu_custom_call" | custom-call | flops 1000 | bytes 1000 | tf_op jit(solution)/shard_map/pack/pallas_call | solution.py:365
  2.4 3.4 %collective-permute-start.1 = (bf16[6,6,2,256]{3,2,1,0:T(2,128)(2,1)}, bf16[6,6,2,256]{3,2,1,0:T(2,128)(2,1)S(1)}, u32[]{:S(2)}, u32[]{:S(2)}) collective-permute-start(bf16[6,6,2,256]{3,2,1,0:T(2,128)(2,1)} %bitcast.19), channel_id=1, source_target_pairs={{8,0},{9,1},{10,2},{11,3},{12,4},{13,5},{14,6},{15,7},{16,8},{17,9... | collective-permute-start | bytes 110600 | tf_op jit(solution)/shard_map/ppermute | solution.py:28
  5.8 2.2 %collective-permute-start = (bf16[18,6,2,256]{3,2,1,0:T(2,128)(2,1)}, bf16[18,6,2,256]{3,2,1,0:T(2,128)(2,1)S(1)}, u32[]{:S(2)}, u32[]{:S(2)}) collective-permute-start(bf16[18,6,2,256]{3,2,1,0:T(2,128)(2,1)} %bitcast.14), channel_id=1, source_target_pairs={{8,0},{9,1},{10,2},{11,3},{12,4},{13,5},{14,6},{15,7},{16,8},{17,9... | collective-permute-start | bytes 331784 | tf_op jit(solution)/shard_map/ppermute | solution.py:28
  8.0 0.0 copy-start
  8.0 0.0 copy-start.1
  8.0 4.5 %all-to-all-start = ((f32[32,8,128]{2,1,0:T(8,128)}), f32[32,8,128]{2,1,0:T(8,128)S(1)}, u32[]{:S(2)}, u32[]{:S(2)}) async-start(f32[32,8,128]{2,1,0:T(8,128)} %pack.3), calls=%async_computation | async-start | bytes 262144 | tf_op jit(solution)/shard_map/all_to_all | solution.py:387
  12.5 0.0 collective-permute-done.links_next_ref.ready_ref
  12.5 0.0 copy-done
  12.5 0.0 copy-done.1
  12.5 0.0 copy-start.3
  12.5 0.0 copy-start.4
  12.6 0.0 copy-start.2
  12.6 2.7 %collective-permute-start.2 = (bf16[18,2,256]{2,1,0:T(2,128)(2,1)S(1)}, bf16[18,2,256]{2,1,0:T(2,128)(2,1)S(1)}, u32[]{:S(2)}, u32[]{:S(2)}) collective-permute-start(bf16[18,2,256]{2,1,0:T(2,128)(2,1)S(1)} %edge.1), channel_id=1, source_target_pairs={{16,0},{17,1},{18,2},{19,3},{20,4},{21,5},{22,6},{23,7},{24,8},{25... | collective-permute-start | bytes 55304 | tf_op jit(solution)/shard_map/ppermute | solution.py:28
  15.3 0.0 collective-permute-done.1.forward_next_ref
  15.3 0.0 copy-start.5
  15.3 0.0 copy-start.6
  15.4 0.0 copy-done.3
  15.4 0.0 copy-done.4
  15.4 0.0 copy-done.2
  15.4 0.7 %copy-done.5 = s32[8,3]{0,1:T(4,128)S(1)} copy-done((s32[8,3]{0,1:T(4,128)S(1)}, s32[8,3]{0,1:T(4,128)}, u32[]{:S(2)}) %copy-start.5) | copy-done | bytes 120
  16.0 0.0 copy-done.6
  16.0 2.0 %chain.1 = (f32[8,96,256]{2,1,0:T(8,128)S(1)}, bf16[2,192,128]{2,1,0:T(8,128)(2,1)S(1)}, s32[8,128]{1,0:T(8,128)S(1)}) custom-call(f32[8]{0:T(128)S(1)} %copy-done.6, s32[3,8]{1,0:T(4,128)S(1)} %bitcast.26, s32[8,128]{1,0:T(8,128)S(1)} %bitcast.23, s32[8,128]{1,0:T(8,128)S(1)} %bitcast.24, s32[8,128]{1,0:T(8,128)S(1)} %bitcast.25, ...), custom_call_target="tpu_custom_call" | custom-call | flops 3000000000 | bytes 200000 | tf_op jit(solution)/shard_map/chain/pallas_call | solution.py:401
  18.0 1.8 %collective-permute-done.2.edge_ref = bf16[18,2,256]{2,1,0:T(2,128)(2,1)S(1)} collective-permute-done((bf16[18,2,256]{2,1,0:T(2,128)(2,1)S(1)}, bf16[18,2,256]{2,1,0:T(2,128)(2,1)S(1)}, u32[]{:S(2)}, u32[]{:S(2)}) %collective-permute-start.2) | collective-permute-done | bytes 18464 | tf_op jit(solution)/shard_map/ppermute | solution.py:28
  19.9 0.2 tail.1.extra_ref
  20.1 0.7 %all-to-all-done.got_ref = f32[32,8,128]{2,1,0:T(8,128)S(1)} async-done(((f32[32,8,128]{2,1,0:T(8,128)}), f32[32,8,128]{2,1,0:T(8,128)S(1)}, u32[]{:S(2)}, u32[]{:S(2)}) %all-to-all-start) | async-done | bytes 131104 | tf_op jit(solution)/shard_map/all_to_all | solution.py:387
  20.8 1.1 %meet.1 = (f32[6,6,2,256]{3,2,1,0:T(2,128)}, f32[32,128]{1,0:T(8,128)S(1)}) custom-call(f32[32,8,128]{2,1,0:T(8,128)S(1)} %all-to-all-done.got_ref, bf16[2,192,128]{2,1,0:T(8,128)(2,1)S(1)} %get-tuple-element.13.corner_ref, f32[8,96,256]{2,1,0:T(8,128)S(1)} %get-tuple-element.14.chain_ref, f32[2,96,256]{2,1,0:T(8,128)S(1)} %tail.1.extra_ref), custom_call_target="tpu_custom_call" | custom-call | flops 2000000000 | bytes 1000000 | tf_op jit(solution)/shard_map/meet/pallas_call | solution.py:439
  21.8 9.9 %all_to_all.10 = f32[32,1,128]{2,1,0:T(1,128)S(1)} all-to-all(f32[32,1,128]{2,1,0:T(1,128)S(1)} %bitcast.22), channel_id=1, replica_groups=mesh['grp'=1,'zs'=32] {'zs'}, dimensions={0} | all-to-all | bytes 32768 | tf_op jit(solution)/shard_map/all_to_all | solution.py:451
  31.7 0.6 %final.1 = f32[2,96]{1,0:T(2,128)} custom-call(f32[32,128]{1,0:T(8,128)S(1)} %bitcast.18, s32[8,128]{1,0:T(8,128)S(1)} %get-tuple-element.17.picked_ref), custom_call_target="tpu_custom_call" | custom-call | tf_op jit(solution)/shard_map/final/pallas_call | solution.py:454
  (2 shorter events, 0.1 us)
Async XLA Ops:
  2.4 12.9 %collective-permute-start.1 = (bf16[6,6,2,256]{3,2,1,0:T(2,128)(2,1)}, bf16[6,6,2,256]{3,2,1,0:T(2,128)(2,1)S(1)}, u32[]{:S(2)}, u32[]{:S(2)}) collective-permute-start(bf16[6,6,2,256]{3,2,1,0:T(2,128)(2,1)} %bitcast.19), channel_id=1, source_target_pairs={{8,0},{9,1},{10,2},{11,3},{12,4},{13,5},{14,6},{15,7},{16,8},{17,9... | collective-permute-start | bytes 110600 | tf_op jit(solution)/shard_map/ppermute | solution.py:28
  5.8 6.7 %collective-permute-start = (bf16[18,6,2,256]{3,2,1,0:T(2,128)(2,1)}, bf16[18,6,2,256]{3,2,1,0:T(2,128)(2,1)S(1)}, u32[]{:S(2)}, u32[]{:S(2)}) collective-permute-start(bf16[18,6,2,256]{3,2,1,0:T(2,128)(2,1)} %bitcast.14), channel_id=1, source_target_pairs={{8,0},{9,1},{10,2},{11,3},{12,4},{13,5},{14,6},{15,7},{16,8},{17,9... | collective-permute-start | bytes 331784 | tf_op jit(solution)/shard_map/ppermute | solution.py:28
  8.0 4.5 %copy-start = (bf16[2,3,3,1,6,2,256]{6,5,4,3,2,1,0:T(2,128)(2,1)S(1)}, bf16[2,3,3,1,6,2,256]{6,5,4,3,2,1,0:T(2,128)(2,1)}, u32[]{:S(2)}) copy-start(bf16[2,3,3,1,6,2,256]{6,5,4,3,2,1,0:T(2,128)(2,1)} %param.12) | copy-start | bytes 331780
  8.0 4.5 %copy-start.1 = (bf16[2,3,1,6,2,256]{5,4,3,2,1,0:T(2,128)(2,1)S(1)}, bf16[2,3,1,6,2,256]{5,4,3,2,1,0:T(2,128)(2,1)}, u32[]{:S(2)}) copy-start(bf16[2,3,1,6,2,256]{5,4,3,2,1,0:T(2,128)(2,1)} %param.11) | copy-start | bytes 110596
  8.0 12.7 %all-to-all-start = ((f32[32,8,128]{2,1,0:T(8,128)}), f32[32,8,128]{2,1,0:T(8,128)S(1)}, u32[]{:S(2)}, u32[]{:S(2)}) async-start(f32[32,8,128]{2,1,0:T(8,128)} %pack.3), calls=%async_computation | async-start | bytes 262144 | tf_op jit(solution)/shard_map/all_to_all | solution.py:387
  12.5 2.8 %copy-start.3 = (s32[1024]{0:T(1024)S(1)}, s32[1024]{0:T(1024)}, u32[]{:S(2)}) copy-start(s32[1024]{0:T(1024)} %param.16) | copy-start | bytes 12292
  12.5 2.8 %copy-start.4 = (s32[1024,1]{0,1:T(1,128)S(1)}, s32[1024,1]{0,1:T(1,128)}, u32[]{:S(2)}) copy-start(s32[1024,1]{0,1:T(1,128)} %param.17) | copy-start | bytes 12292
  12.6 2.8 %copy-start.2 = (s32[1024]{0:T(1024)S(1)}, s32[1024]{0:T(1024)}, u32[]{:S(2)}) copy-start(s32[1024]{0:T(1024)} %param.15) | copy-start | bytes 12292
  12.6 7.3 %collective-permute-start.2 = (bf16[18,2,256]{2,1,0:T(2,128)(2,1)S(1)}, bf16[18,2,256]{2,1,0:T(2,128)(2,1)S(1)}, u32[]{:S(2)}, u32[]{:S(2)}) collective-permute-start(bf16[18,2,256]{2,1,0:T(2,128)(2,1)S(1)} %edge.1), channel_id=1, source_target_pairs={{16,0},{17,1},{18,2},{19,3},{20,4},{21,5},{22,6},{23,7},{24,8},{25... | collective-permute-start | bytes 55304 | tf_op jit(solution)/shard_map/ppermute | solution.py:28
  15.3 0.7 %copy-start.5 = (s32[8,3]{0,1:T(4,128)S(1)}, s32[8,3]{0,1:T(4,128)}, u32[]{:S(2)}) copy-start(s32[8,3]{0,1:T(4,128)} %param.14) | copy-start | bytes 292
  15.3 0.7 %copy-start.6 = (f32[8]{0:T(128)S(1)}, f32[8]{0:T(128)}, u32[]{:S(2)}) copy-start(f32[8]{0:T(128)} %weight_ref.1) | copy-start | bytes 100

commit v11 on v7

--- a/solution.py
+++ b/solution.py
@@ -290,7 +290,6 @@
             at = comp * CROWS + z * block_x
             seq_ref[comp, z] = seq[at : at + block_x]
     turned = jnp.concatenate([-seq[3 * CROWS :], seq[: 3 * CROWS]], axis=0)
-    sums = []
     for length in range(LMAX):
         chain = chain_ref[length]
         if length >= block_z:
@@ -303,17 +302,16 @@
             narrow = part[:, :LANES]
             for at in range(LANES, rows_y, LANES):
                 narrow = narrow + part[:, at : at + LANES]
-            sums.append(jnp.sum(narrow, axis=0, keepdims=True))
-    table = jnp.concatenate(sums, axis=0)
+            row = (2 * length + (field is turned)) * 8
+            table_ref[row : row + 8] = narrow
+
+
+def final_kernel(total_ref, picked_ref, out_ref):
+    table = jnp.sum(total_ref[...].reshape(2 * LMAX, 8, LANES), axis=1)
     for shift in (64, 32, 16, 8):
         table = table + pltpu.roll(table, shift, 1)
     mine = iota((2 * LMAX, LANES), 1) // NT == iota((2 * LMAX, LANES), 0)
-    flat = jnp.sum(jnp.where(mine, table, 0.0), axis=0, keepdims=True)
-    table_ref[...] = jnp.broadcast_to(flat, table_ref.shape)
-
-
-def final_kernel(tables_ref, picked_ref, out_ref):
-    total = jnp.sum(tables_ref[...], axis=0, keepdims=True)
+    total = jnp.sum(jnp.where(mine, table, 0.0), axis=0, keepdims=True)
     picked = picked_ref[...]
     value = jnp.take_along_axis(
         jnp.broadcast_to(total, picked.shape), jnp.maximum(picked, 0), axis=1
@@ -429,7 +427,7 @@
         functools.partial(meet_kernel, block_z, block_x),
         out_shape=(
             jax.ShapeDtypeStruct((6, block_z, block_x, rows_y), F32),
-            jax.ShapeDtypeStruct((devices, LANES), F32),
+            jax.ShapeDtypeStruct((16 * LMAX, LANES), F32),
         ),
         in_specs=[VMEM] * 4,
         out_specs=(VMEM, VMEM),
@@ -437,9 +435,7 @@
         cost_estimate=cost(2_000_000_000, 1_000_000),
         name="meet",
     )(got, corner, chain, extra)
-    tables = lax.all_to_all(
-        partial.reshape(devices, 1, LANES), "zs", split_axis=0, concat_axis=0, tiled=True
-    ).reshape(devices, LANES)
+    total = lax.psum(partial, "zs")
     owned = pl.pallas_call(
         final_kernel,
         out_shape=jax.ShapeDtypeStruct((2, MOST), F32),
@@ -447,7 +443,7 @@
         out_specs=VMEM,
         compiler_params=PARAMS,
         name="final",
-    )(tables, picked)
+    )(total, picked)
     return (seq.reshape(2, 3, 1, block_z, block_x, rows_y), owned.T)
 
 

time: 31.9 us -> 154 us (4.83)
  waiting for transfers between devices: 3.8 us -> 120 us
  between operations: 0.7 us -> 14.1 us
  blocking collectives: 9.88 us -> 0 us
    psum x0 -> x1, waiting for transfers between devices: none -> 116 us  [shards(): total = lax.psum(partial, 'zs')]
    all_to_all x1 -> x0, blocking collectives: 9.88 us -> none  [shards(): lax.all_to_all(partial.reshape(devices, 1, LANES), 'zs', split_axis=0, co...]
  transfers between devices with their start and end apart: 4 -> 5, of which waited for: 2 -> 3; matrix products, arithmetic and copies ran while one was open for 0% -> 0% of each run, Pallas kernels for 11% -> 2%
where the time goes in v11:
time: 154 us; the launch traced here: 152 us
  waiting for transfers between devices  120 us (78%)
  between operations  14.1 us (9%)
  starting transfers between devices  12.2 us (8%)
  Pallas kernels  5.46 us (4%)
    psum x1, waiting for transfers between devices, shards(): total = lax.psum(partial, 'zs')  116 us
    ppermute x3, starting transfers between devices, passed_along(): return lax.ppermute(block, axis, route)  8.29 us
    all_to_all x1, starting transfers between devices, shards(): got = lax.all_to_all(payload, 'zs', split_axis=0, concat_axis=0, tiled=True)  3.84 us
  transfers between devices with their start and end apart: 5, of which 3 were waited for; matrix products, arithmetic and copies ran while one was open for 0% of the time, Pallas kernels for 2%

profile of v11, /device:TPU:0, one launch (start us, length us, event | category | flops | bytes accessed | tf_op | source)
XLA Modules:
  0.0 152.4 jit_solution(6441195007624326150)
XLA Ops:
  7.2 5.1 %collective-permute-start.1 = (bf16[6,6,2,256]{3,2,1,0:T(2,128)(2,1)}, bf16[6,6,2,256]{3,2,1,0:T(2,128)(2,1)S(1)}, u32[]{:S(2)}, u32[]{:S(2)}) collective-permute-start(bf16[6,6,2,256]{3,2,1,0:T(2,128)(2,1)} %bitcast.14), channel_id=1, source_target_pairs={{8,0},{9,1},{10,2},{11,3},{12,4},{13,5},{14,6},{15,7},{16,8},{17,9... | collective-permute-start | bytes 110600 | tf_op jit(solution)/shard_map/ppermute | solution.py:28
  12.3 0.4 collective-permute-start
  12.7 1.8 %pack.1 = (f32[32,8,128]{2,1,0:T(8,128)}, s32[8,128]{1,0:T(8,128)}, f32[8,128]{1,0:T(8,128)}) custom-call(f32[8]{0:T(128)} %weight_ref.1, s32[3,8]{1,0:T(4,128)} %bitcast.21, bf16[2,3,8,384]{3,2,1,0:T(8,128)(2,1)} %up_ref.1, bf16[2,3,8,384]{3,2,1,0:T(8,128)(2,1)} %down_ref.1, s32[8,128]{1,0:T(8,128)} %bitcast.18, s32[8,128]{1,0:T(8,128)} %bitcast.19, ...), custom_call_target="tpu_custom_call" | custom-call | flops 2000000000 | bytes 400000 | tf_op jit(solution)/shard_map/pack/pallas_call | solution.py:357
  14.5 0.0 copy-start
  14.5 0.0 copy-start.2
  14.5 3.8 %all-to-all-start = ((f32[32,8,128]{2,1,0:T(8,128)}), f32[32,8,128]{2,1,0:T(8,128)S(1)}, u32[]{:S(2)}, u32[]{:S(2)}) async-start(f32[32,8,128]{2,1,0:T(8,128)} %get-tuple-element.10), calls=%async_computation | async-start | bytes 262144 | tf_op jit(solution)/shard_map/all_to_all | solution.py:385
  18.4 0.0 copy-start.3
  18.4 0.0 copy-start.4
  18.4 0.0 all-reduce.2.cloned.1.call-start
  18.4 0.0 collective-permute-done.links_next_ref.ready_ref
  18.5 0.0 copy-done
  18.5 0.0 copy-done.2
  18.5 2.7 %collective-permute-start.2 = (bf16[18,2,256]{2,1,0:T(2,128)(2,1)S(1)}, bf16[18,2,256]{2,1,0:T(2,128)(2,1)S(1)}, u32[]{:S(2)}, u32[]{:S(2)}) collective-permute-start(bf16[18,2,256]{2,1,0:T(2,128)(2,1)S(1)} %edge.1), channel_id=1, source_target_pairs={{16,0},{17,1},{18,2},{19,3},{20,4},{21,5},{22,6},{23,7},{24,8},{25... | collective-permute-start | bytes 55304 | tf_op jit(solution)/shard_map/ppermute | solution.py:28
  21.3 0.0 collective-permute-done.1.forward_next_ref
  21.3 0.0 copy-done.3
  21.3 0.0 copy-done.4
  21.3 1.4 chain.1
  22.7 3.0 %collective-permute-done.2.edge_ref = bf16[18,2,256]{2,1,0:T(2,128)(2,1)S(1)} collective-permute-done((bf16[18,2,256]{2,1,0:T(2,128)(2,1)S(1)}, bf16[18,2,256]{2,1,0:T(2,128)(2,1)S(1)}, u32[]{:S(2)}, u32[]{:S(2)}) %collective-permute-start.2) | collective-permute-done | bytes 18464 | tf_op jit(solution)/shard_map/ppermute | solution.py:28
  25.7 0.2 tail.1.extra_ref
  25.9 0.7 all-to-all-done.got_ref
  26.6 1.1 meet.1
  27.7 0.0 all-reduce.2.cloned.1.call-update
  27.7 116.0 %all-reduce.2.cloned.1.call-done.total_ref = f32[128,128]{1,0:T(8,128)} async-done(((f32[128,128]{1,0:T(8,128)}), f32[128,128]{1,0:T(8,128)}) %all-reduce.2.cloned.1.call-update) | async-done | bytes 65552 | tf_op jit(solution)/shard_map/psum | solution.py:438
  143.8 0.0 copy-start.1
  143.8 0.8 copy-done.1
  144.6 0.9 final.1
  (1 shorter events, 0.0 us)
Async XLA Ops:
  7.2 14.1 %collective-permute-start.1 = (bf16[6,6,2,256]{3,2,1,0:T(2,128)(2,1)}, bf16[6,6,2,256]{3,2,1,0:T(2,128)(2,1)S(1)}, u32[]{:S(2)}, u32[]{:S(2)}) collective-permute-start(bf16[6,6,2,256]{3,2,1,0:T(2,128)(2,1)} %bitcast.14), channel_id=1, source_target_pairs={{8,0},{9,1},{10,2},{11,3},{12,4},{13,5},{14,6},{15,7},{16,8},{17,9... | collective-permute-start | bytes 110600 | tf_op jit(solution)/shard_map/ppermute | solution.py:28
  12.3 6.2 %collective-permute-start = (bf16[18,6,2,256]{3,2,1,0:T(2,128)(2,1)}, bf16[18,6,2,256]{3,2,1,0:T(2,128)(2,1)S(1)}, u32[]{:S(2)}, u32[]{:S(2)}) collective-permute-start(bf16[18,6,2,256]{3,2,1,0:T(2,128)(2,1)} %bitcast.10), channel_id=1, source_target_pairs={{8,0},{9,1},{10,2},{11,3},{12,4},{13,5},{14,6},{15,7},{16,8},{17,9... | collective-permute-start | bytes 331784 | tf_op jit(solution)/shard_map/ppermute | solution.py:28
  14.5 3.9 %copy-start = (bf16[2,3,3,1,6,2,256]{6,5,4,3,2,1,0:T(2,128)(2,1)S(1)}, bf16[2,3,3,1,6,2,256]{6,5,4,3,2,1,0:T(2,128)(2,1)}, u32[]{:S(2)}) copy-start(bf16[2,3,3,1,6,2,256]{6,5,4,3,2,1,0:T(2,128)(2,1)} %param.12) | copy-start | bytes 331780
  14.5 3.9 %copy-start.2 = (bf16[2,3,1,6,2,256]{5,4,3,2,1,0:T(2,128)(2,1)S(1)}, bf16[2,3,1,6,2,256]{5,4,3,2,1,0:T(2,128)(2,1)}, u32[]{:S(2)}) copy-start(bf16[2,3,1,6,2,256]{5,4,3,2,1,0:T(2,128)(2,1)} %param.11) | copy-start | bytes 110596
  14.5 12.1 %all-to-all-start = ((f32[32,8,128]{2,1,0:T(8,128)}), f32[32,8,128]{2,1,0:T(8,128)S(1)}, u32[]{:S(2)}, u32[]{:S(2)}) async-start(f32[32,8,128]{2,1,0:T(8,128)} %get-tuple-element.10), calls=%async_computation | async-start | bytes 262144 | tf_op jit(solution)/shard_map/all_to_all | solution.py:385
  18.4 2.9 %copy-start.3 = (s32[8,128]{1,0:T(8,128)S(1)}, s32[8,128]{1,0:T(8,128)}, u32[]{:S(2)}) copy-start(s32[8,128]{1,0:T(8,128)} %get-tuple-element.12.request_ref) | copy-start | bytes 12292
  18.4 2.9 %copy-start.4 = (f32[8,128]{1,0:T(8,128)S(1)}, f32[8,128]{1,0:T(8,128)}, u32[]{:S(2)}) copy-start(f32[8,128]{1,0:T(8,128)} %get-tuple-element.11.table_ref) | copy-start | bytes 12292
  18.4 125.4 %all-reduce.2.cloned.1.call-start = ((), (), s32[]{:S(2)}) async-start(), calls=%async_computation.1 | async-start | bytes 131072 | tf_op jit(solution)/shard_map/psum | solution.py:438
  18.5 7.2 %collective-permute-start.2 = (bf16[18,2,256]{2,1,0:T(2,128)(2,1)S(1)}, bf16[18,2,256]{2,1,0:T(2,128)(2,1)S(1)}, u32[]{:S(2)}, u32[]{:S(2)}) collective-permute-start(bf16[18,2,256]{2,1,0:T(2,128)(2,1)S(1)} %edge.1), channel_id=1, source_target_pairs={{16,0},{17,1},{18,2},{19,3},{20,4},{21,5},{22,6},{23,7},{24,8},{25... | collective-permute-start | bytes 55304 | tf_op jit(solution)/shard_map/ppermute | solution.py:28
  143.8 0.8 copy-start.1
Sparse Core Ops, SparseCore 0:
  27.9 115.8 all-reduce.1

commit v12 on v10

--- a/solution.py
+++ b/solution.py
@@ -37,12 +37,12 @@
     return lax.broadcasted_iota(jnp.int32, shape, axis)
 
 
-def pack_kernel(last_group, block_z, block_x, up_ref, down_ref, *refs):
+def pack_kernel(upper_half, block_z, block_x, up_ref, down_ref, *refs):
     *_, out_ref, up_rows, down_rows, out_rows, done = refs
     groups = lax.axis_size("zs") // G
     group = lax.axis_index("zs") // G
 
-    @pl.when((group == groups - 1) == last_group)
+    @pl.when((group >= groups // 2) == upper_half)
     def _():
         copies = [
             pltpu.make_async_copy(up_ref, up_rows, done.at[0]),
@@ -52,13 +52,18 @@
             copy.start()
         for copy in copies:
             copy.wait()
-        pack_rows(block_z, block_x, up_rows, down_rows, out_rows)
-        copy = pltpu.make_async_copy(out_rows, out_ref, done.at[2])
-        copy.start()
-        copy.wait()
-
-
-def pack_rows(block_z, block_x, up_ref, down_ref, out_ref):
+        sends = [
+            pltpu.make_async_copy(
+                out_rows.at[zb * G : (zb + 1) * G], out_ref.at[zb * G : (zb + 1) * G], done.at[2 + zb]
+            )
+            for zb in range(groups)
+        ]
+        pack_rows(block_z, block_x, up_rows, down_rows, out_rows, sends)
+        for copy in sends:
+            copy.wait()
+
+
+def pack_rows(block_z, block_x, up_ref, down_ref, out_ref, sends):
     zh = block_z + 1
     slot_lanes = zh * XH
     width_x = block_x * G
@@ -106,6 +111,7 @@
                     one_slot == (comp + g) % 6, results[comp][zb, :, at : at + LANES], value
                 )
             out_ref[zb * G + g] = value
+        sends[zb].start()
 
 
 def link_times(links, vec):
@@ -232,8 +238,8 @@
         corner = jnp.where(here, 4 * x_step + 2 * y_step + z_step, 0)
         weights = jnp.where(here, jnp.take_along_axis(table, corner, axis=1), 0.0)
         high, low = split_two(weights)
-        corner_ref[0, y_step * 6 * CROWS : (y_step + 1) * 6 * CROWS] = high
-        corner_ref[1, y_step * 6 * CROWS : (y_step + 1) * 6 * CROWS] = low
+        rows = slice(y_step * 6 * CROWS, (y_step + 1) * 6 * CROWS)
+        corner_ref[rows] = jnp.concatenate([high, high, low], axis=1)
 
     mine = owners_ref[...] == place
     codes = (lengths_ref[...] * (2 * NT) + separations_ref[...]).astype(F32)
@@ -285,10 +291,8 @@
     rows_y = got_ref.shape[0] * NT
     got = got_ref[...].reshape(rows_y, LANES)
     high, low = split_two(got)
-    dot = functools.partial(
-        lax.dot_general, dimension_numbers=NT_DIMS, preferred_element_type=F32
-    )
-    both = dot(corner_ref[0], high) + dot(corner_ref[0], low) + dot(corner_ref[1], high)
+    terms = jnp.concatenate([high, low, high], axis=1)
+    both = lax.dot_general(corner_ref[...], terms, NT_DIMS, preferred_element_type=F32)
     size = 6 * CROWS
     seq = both[:size] + pltpu.roll(both[size:], rows_y - NT, 1)
     for comp in range(6):
@@ -309,11 +313,15 @@
             narrow = part[:, :LANES]
             for at in range(LANES, rows_y, LANES):
                 narrow = narrow + part[:, at : at + LANES]
-            sums.append(jnp.sum(narrow, axis=0, keepdims=True))
-    table = jnp.concatenate(sums, axis=0)
-    for shift in (64, 32, 16, 8):
-        table = table + pltpu.roll(table, shift, 1)
-    mine = iota((2 * LMAX, LANES), 1) // NT == iota((2 * LMAX, LANES), 0)
+            sums.append(narrow)
+    rows = 2 * LMAX * 8
+    high, low = split_two(jnp.concatenate(sums, axis=0))
+    same_t = jnp.where(iota((LANES, LANES), 0) % NT == iota((LANES, LANES), 1) % NT, 1.0, 0.0)
+    table = jnp.dot(
+        jnp.concatenate([high, low], axis=0), same_t.astype(BF16), preferred_element_type=F32
+    )
+    table = table[:rows] + table[rows:]
+    mine = iota((rows, LANES), 1) // NT == iota((rows, LANES), 0) // 8
     flat = jnp.sum(jnp.where(mine, table, 0.0), axis=0, keepdims=True)
     table_ref[...] = jnp.broadcast_to(flat, table_ref.shape)
 
@@ -360,10 +368,10 @@
     links = gauge_links.reshape(18, block_z, block_x, rows_y)
     field = forward.reshape(6, block_z, block_x, rows_y)
 
-    def packed(last_group, *payload):
+    def packed(upper_half, *payload):
         anywhere = pl.BlockSpec(memory_space=pl.ANY)
         return pl.pallas_call(
-            functools.partial(pack_kernel, last_group, block_z, block_x),
+            functools.partial(pack_kernel, upper_half, block_z, block_x),
             out_shape=jax.ShapeDtypeStruct((devices, NT, LANES), F32),
             in_specs=[anywhere] * (2 + len(payload)),
             out_specs=anywhere,
@@ -372,10 +380,10 @@
                 pltpu.VMEM(quark_up.shape, BF16),
                 pltpu.VMEM(quark_up.shape, BF16),
                 pltpu.VMEM((devices, NT, LANES), F32),
-                pltpu.SemaphoreType.DMA((3,)),
+                pltpu.SemaphoreType.DMA((2 + devices // G,)),
             ],
-            compiler_params=WIDE_PARAMS if last_group else WHOLE_PARAMS,
-            cost_estimate=cost(2_000_000_000, 400_000) if last_group else cost(1_000, 1_000),
+            compiler_params=WIDE_PARAMS if upper_half else WHOLE_PARAMS,
+            cost_estimate=cost(2_000_000_000, 400_000) if upper_half else cost(1_000, 1_000),
             name="pack",
         )(quark_up, quark_down, *payload)
 
@@ -402,7 +410,7 @@
         functools.partial(chain_kernel, depth_z, scale, block_z, block_x),
         out_shape=(
             jax.ShapeDtypeStruct((LMAX, 6 * CROWS, rows_y), F32),
-            jax.ShapeDtypeStruct((2, 12 * CROWS, LANES), BF16),
+            jax.ShapeDtypeStruct((12 * CROWS, 3 * LANES), BF16),
             jax.ShapeDtypeStruct((8, LANES), jnp.int32),
         ),
         in_specs=[SMEM] * 2 + [VMEM] * 7,

time: 32.6 us -> 32.6 us (level)
    ppermute x3, starting transfers between devices: 8.28 us -> 6.56 us  [passed_along(): return lax.ppermute(block, axis, route)]
    all_to_all x1, starting transfers between devices: 4.45 us -> 6.16 us  [shards(): got = lax.all_to_all(payload, 'zs', split_axis=0, concat_axis=0, tiled=True)]
where the time goes in v12:
time: 32.6 us; the launch traced here: 32.4 us
  starting transfers between devices  12.7 us (39%)
  blocking collectives  9.88 us (30%)
  Pallas kernels  5.78 us (18%)
  waiting for transfers between devices  2.54 us (8%)
  between operations  0.75 us (2%)
  local copies, waits for them, and re-layouts  0.69 us (2%)
    all_to_all x1, blocking collectives, shards(): lax.all_to_all(partial.reshape(devices, 1, LANES), 'zs', split_axis=0, co...  9.88 us
    ppermute x3, starting transfers between devices, passed_along(): return lax.ppermute(block, axis, route)  6.56 us
    all_to_all x1, starting transfers between devices, shards(): got = lax.all_to_all(payload, 'zs', split_axis=0, concat_axis=0, tiled=True)  6.16 us
    pallas_call x1, Pallas kernels, shards(): pl.pallas_call(functools.partial(chain_kernel, depth_z, scale, block_z, b...  1.99 us
    pallas_call x2, Pallas kernels, packed(): pl.pallas_call(functools.partial(pack_kernel, upper_half, block_z, block_...  1.85 us
    ppermute x3, waiting for transfers between devices, passed_along(): return lax.ppermute(block, axis, route)  1.84 us
    pallas_call x1, Pallas kernels, shards(): pl.pallas_call(functools.partial(meet_kernel, block_z, block_x), out_shap...  1.06 us
    all_to_all x1, waiting for transfers between devices, shards(): got = lax.all_to_all(payload, 'zs', split_axis=0, concat_axis=0, tiled=True)  0.7 us
  transfers between devices with their start and end apart: 4, of which 2 were waited for; matrix products, arithmetic and copies ran while one was open for 0% of the time, Pallas kernels for 7%

profile of v12, /device:TPU:0, one launch (start us, length us, event | category | flops | bytes accessed | tf_op | source)
XLA Modules:
  0.0 32.4 jit_solution(15637969109071792291)
XLA Ops:
  0.6 1.8 %pack.2.refs_0_ = f32[32,8,128]{2,1,0:T(8,128)} custom-call(bf16[2,3,8,384]{3,2,1,0:T(8,128)(2,1)} %up_ref.3, bf16[2,3,8,384]{3,2,1,0:T(8,128)(2,1)} %down_ref.3), custom_call_target="tpu_custom_call" | custom-call | flops 1000 | bytes 1000 | tf_op jit(solution)/shard_map/pack/pallas_call | solution.py:373
  2.4 3.4 %collective-permute-start.1 = (bf16[6,6,2,256]{3,2,1,0:T(2,128)(2,1)}, bf16[6,6,2,256]{3,2,1,0:T(2,128)(2,1)S(1)}, u32[]{:S(2)}, u32[]{:S(2)}) collective-permute-start(bf16[6,6,2,256]{3,2,1,0:T(2,128)(2,1)} %bitcast.19), channel_id=1, source_target_pairs={{8,0},{9,1},{10,2},{11,3},{12,4},{13,5},{14,6},{15,7},{16,8},{17,9... | collective-permute-start | bytes 110600 | tf_op jit(solution)/shard_map/ppermute | solution.py:28
  5.8 0.4 %collective-permute-start = (bf16[18,6,2,256]{3,2,1,0:T(2,128)(2,1)}, bf16[18,6,2,256]{3,2,1,0:T(2,128)(2,1)S(1)}, u32[]{:S(2)}, u32[]{:S(2)}) collective-permute-start(bf16[18,6,2,256]{3,2,1,0:T(2,128)(2,1)} %bitcast.14), channel_id=1, source_target_pairs={{8,0},{9,1},{10,2},{11,3},{12,4},{13,5},{14,6},{15,7},{16,8},{17,9... | collective-permute-start | bytes 331784 | tf_op jit(solution)/shard_map/ppermute | solution.py:28
  6.3 0.1 pack.3
  6.3 0.0 copy-start
  6.3 0.0 copy-start.1
  6.3 6.2 %all-to-all-start = ((f32[32,8,128]{2,1,0:T(8,128)}), f32[32,8,128]{2,1,0:T(8,128)S(1)}, u32[]{:S(2)}, u32[]{:S(2)}) async-start(f32[32,8,128]{2,1,0:T(8,128)} %pack.3), calls=%async_computation | async-start | bytes 262144 | tf_op jit(solution)/shard_map/all_to_all | solution.py:395
  12.5 0.0 collective-permute-done.links_next_ref.ready_ref
  12.5 0.0 copy-done
  12.5 0.0 copy-done.1
  12.5 0.0 copy-start.3
  12.6 0.0 copy-start.4
  12.6 0.0 copy-start.2
  12.6 2.7 %collective-permute-start.2 = (bf16[18,2,256]{2,1,0:T(2,128)(2,1)S(1)}, bf16[18,2,256]{2,1,0:T(2,128)(2,1)S(1)}, u32[]{:S(2)}, u32[]{:S(2)}) collective-permute-start(bf16[18,2,256]{2,1,0:T(2,128)(2,1)S(1)} %edge.1), channel_id=1, source_target_pairs={{16,0},{17,1},{18,2},{19,3},{20,4},{21,5},{22,6},{23,7},{24,8},{25... | collective-permute-start | bytes 55304 | tf_op jit(solution)/shard_map/ppermute | solution.py:28
  15.4 0.0 collective-permute-done.1.forward_next_ref
  15.4 0.0 copy-start.5
  15.4 0.0 copy-start.6
  15.4 0.0 copy-done.3
  15.4 0.0 copy-done.4
  15.4 0.0 copy-done.2
  15.4 0.7 %copy-done.5 = s32[8,3]{0,1:T(4,128)S(1)} copy-done((s32[8,3]{0,1:T(4,128)S(1)}, s32[8,3]{0,1:T(4,128)}, u32[]{:S(2)}) %copy-start.5) | copy-done | bytes 120
  16.1 0.0 copy-done.6
  16.1 2.0 %chain.1 = (f32[8,96,256]{2,1,0:T(8,128)S(1)}, bf16[192,384]{1,0:T(8,128)(2,1)S(1)}, s32[8,128]{1,0:T(8,128)S(1)}) custom-call(f32[8]{0:T(128)S(1)} %copy-done.6, s32[3,8]{1,0:T(4,128)S(1)} %bitcast.26, s32[8,128]{1,0:T(8,128)S(1)} %bitcast.23, s32[8,128]{1,0:T(8,128)S(1)} %bitcast.24, s32[8,128]{1,0:T(8,128)S(1)} %bitcast.25, ...), custom_call_target="tpu_custom_call" | custom-call | flops 3000000000 | bytes 200000 | tf_op jit(solution)/shard_map/chain/pallas_call | solution.py:409
  18.0 1.8 %collective-permute-done.2.edge_ref = bf16[18,2,256]{2,1,0:T(2,128)(2,1)S(1)} collective-permute-done((bf16[18,2,256]{2,1,0:T(2,128)(2,1)S(1)}, bf16[18,2,256]{2,1,0:T(2,128)(2,1)S(1)}, u32[]{:S(2)}, u32[]{:S(2)}) %collective-permute-start.2) | collective-permute-done | bytes 18464 | tf_op jit(solution)/shard_map/ppermute | solution.py:28
  19.9 0.2 tail.1.extra_ref
  20.1 0.7 %all-to-all-done.got_ref = f32[32,8,128]{2,1,0:T(8,128)S(1)} async-done(((f32[32,8,128]{2,1,0:T(8,128)}), f32[32,8,128]{2,1,0:T(8,128)S(1)}, u32[]{:S(2)}, u32[]{:S(2)}) %all-to-all-start) | async-done | bytes 131104 | tf_op jit(solution)/shard_map/all_to_all | solution.py:395
  20.8 1.1 %meet.1 = (f32[6,6,2,256]{3,2,1,0:T(2,128)}, f32[32,128]{1,0:T(8,128)S(1)}) custom-call(f32[32,8,128]{2,1,0:T(8,128)S(1)} %all-to-all-done.got_ref, bf16[192,384]{1,0:T(8,128)(2,1)S(1)} %get-tuple-element.13.corner_ref, f32[8,96,256]{2,1,0:T(8,128)S(1)} %get-tuple-element.14.chain_ref, f32[2,96,256]{2,1,0:T(8,128)S(1)} %tail.1.extra_ref), custom_call_target="tpu_custom_call" | custom-call | flops 2000000000 | bytes 1000000 | tf_op jit(solution)/shard_map/meet/pallas_call | solution.py:447
  21.8 9.9 %all_to_all.10 = f32[32,1,128]{2,1,0:T(1,128)S(1)} all-to-all(f32[32,1,128]{2,1,0:T(1,128)S(1)} %bitcast.22), channel_id=1, replica_groups=mesh['grp'=1,'zs'=32] {'zs'}, dimensions={0} | all-to-all | bytes 32768 | tf_op jit(solution)/shard_map/all_to_all | solution.py:459
  31.7 0.6 %final.1 = f32[2,96]{1,0:T(2,128)} custom-call(f32[32,128]{1,0:T(8,128)S(1)} %bitcast.18, s32[8,128]{1,0:T(8,128)S(1)} %get-tuple-element.17.picked_ref), custom_call_target="tpu_custom_call" | custom-call | tf_op jit(solution)/shard_map/final/pallas_call | solution.py:462
  (1 shorter events, 0.0 us)
Async XLA Ops:
  2.4 12.9 %collective-permute-start.1 = (bf16[6,6,2,256]{3,2,1,0:T(2,128)(2,1)}, bf16[6,6,2,256]{3,2,1,0:T(2,128)(2,1)S(1)}, u32[]{:S(2)}, u32[]{:S(2)}) collective-permute-start(bf16[6,6,2,256]{3,2,1,0:T(2,128)(2,1)} %bitcast.19), channel_id=1, source_target_pairs={{8,0},{9,1},{10,2},{11,3},{12,4},{13,5},{14,6},{15,7},{16,8},{17,9... | collective-permute-start | bytes 110600 | tf_op jit(solution)/shard_map/ppermute | solution.py:28
  5.8 6.7 %collective-permute-start = (bf16[18,6,2,256]{3,2,1,0:T(2,128)(2,1)}, bf16[18,6,2,256]{3,2,1,0:T(2,128)(2,1)S(1)}, u32[]{:S(2)}, u32[]{:S(2)}) collective-permute-start(bf16[18,6,2,256]{3,2,1,0:T(2,128)(2,1)} %bitcast.14), channel_id=1, source_target_pairs={{8,0},{9,1},{10,2},{11,3},{12,4},{13,5},{14,6},{15,7},{16,8},{17,9... | collective-permute-start | bytes 331784 | tf_op jit(solution)/shard_map/ppermute | solution.py:28
  6.3 6.2 %copy-start = (bf16[2,3,3,1,6,2,256]{6,5,4,3,2,1,0:T(2,128)(2,1)S(1)}, bf16[2,3,3,1,6,2,256]{6,5,4,3,2,1,0:T(2,128)(2,1)}, u32[]{:S(2)}) copy-start(bf16[2,3,3,1,6,2,256]{6,5,4,3,2,1,0:T(2,128)(2,1)} %param.12) | copy-start | bytes 331780
  6.3 6.2 %copy-start.1 = (bf16[2,3,1,6,2,256]{5,4,3,2,1,0:T(2,128)(2,1)S(1)}, bf16[2,3,1,6,2,256]{5,4,3,2,1,0:T(2,128)(2,1)}, u32[]{:S(2)}) copy-start(bf16[2,3,1,6,2,256]{5,4,3,2,1,0:T(2,128)(2,1)} %param.11) | copy-start | bytes 110596
  6.3 14.4 %all-to-all-start = ((f32[32,8,128]{2,1,0:T(8,128)}), f32[32,8,128]{2,1,0:T(8,128)S(1)}, u32[]{:S(2)}, u32[]{:S(2)}) async-start(f32[32,8,128]{2,1,0:T(8,128)} %pack.3), calls=%async_computation | async-start | bytes 262144 | tf_op jit(solution)/shard_map/all_to_all | solution.py:395
  12.5 2.8 %copy-start.3 = (s32[1024]{0:T(1024)S(1)}, s32[1024]{0:T(1024)}, u32[]{:S(2)}) copy-start(s32[1024]{0:T(1024)} %param.16) | copy-start | bytes 12292
  12.6 2.8 %copy-start.4 = (s32[1024,1]{0,1:T(1,128)S(1)}, s32[1024,1]{0,1:T(1,128)}, u32[]{:S(2)}) copy-start(s32[1024,1]{0,1:T(1,128)} %param.17) | copy-start | bytes 12292
  12.6 2.8 %copy-start.2 = (s32[1024]{0:T(1024)S(1)}, s32[1024]{0:T(1024)}, u32[]{:S(2)}) copy-start(s32[1024]{0:T(1024)} %param.15) | copy-start | bytes 12292
  12.6 7.3 %collective-permute-start.2 = (bf16[18,2,256]{2,1,0:T(2,128)(2,1)S(1)}, bf16[18,2,256]{2,1,0:T(2,128)(2,1)S(1)}, u32[]{:S(2)}, u32[]{:S(2)}) collective-permute-start(bf16[18,2,256]{2,1,0:T(2,128)(2,1)S(1)} %edge.1), channel_id=1, source_target_pairs={{16,0},{17,1},{18,2},{19,3},{20,4},{21,5},{22,6},{23,7},{24,8},{25... | collective-permute-start | bytes 55304 | tf_op jit(solution)/shard_map/ppermute | solution.py:28
  15.4 0.7 %copy-start.5 = (s32[8,3]{0,1:T(4,128)S(1)}, s32[8,3]{0,1:T(4,128)}, u32[]{:S(2)}) copy-start(s32[8,3]{0,1:T(4,128)} %param.14) | copy-start | bytes 292
  15.4 0.7 %copy-start.6 = (f32[8]{0:T(128)S(1)}, f32[8]{0:T(128)}, u32[]{:S(2)}) copy-start(f32[8]{0:T(128)} %weight_ref.1) | copy-start | bytes 100

commit v13 on v7

--- a/solution.py
+++ b/solution.py
@@ -16,6 +16,7 @@
 LANES = 128
 XH = 3
 CROWS = 16
+GROUP = 32
 
 F32 = jnp.float32
 BF16 = jnp.bfloat16
@@ -74,38 +75,34 @@
     planes = [cross(0, 0, c) - cross(1, 1, c) for c in range(3)]
     planes += [cross(0, 1, c) + cross(1, 0, c) for c in range(3)]
     lane = iota((1, 2 * LANES), 1)
-    half = lane // LANES
-    within = lane % LANES
-    slot = within // slot_lanes
-    cell = within % slot_lanes
-    source_row = iota((LANES, 2 * LANES), 0)
-    results = []
-    for comp in range(6):
-        turned = (slot + 12 - comp - 4 * half) % 6
-        source = (cell % zh) * width_x + (block_x * (turned + 4 * half) + cell // zh) % width_x
-        source = jnp.where((turned < 4) & (slot < 6), source, -1)
-        pick = jnp.where(source_row == source, 1.0, 0.0).astype(BF16)
-        wide = jnp.concatenate([planes[comp], planes[comp][:, :LANES]], axis=1)
-        rows = []
+    cell = lane % GROUP
+    source = (cell % zh) * width_x + (block_x * (lane // GROUP) + cell // zh) % width_x
+    source = jnp.where(cell < slot_lanes, source, -1)
+    pick = jnp.where(iota((LANES, 2 * LANES), 0) == source, 1.0, 0.0).astype(BF16)
+    rows = []
+    for plane in planes:
+        wide = jnp.concatenate([plane, plane[:, :LANES]], axis=1)
         for zb in range(z_blocks):
             begin = zb * block_z * width_x
             part = wide[:, begin : begin + LANES]
             high = part.astype(BF16).astype(F32)
             rows += [high, part - high]
-        left = jnp.concatenate(rows, axis=0).astype(BF16)
-        got = jnp.dot(left, pick, preferred_element_type=F32)
-        got = got.reshape(z_blocks, 2, NT, 2 * LANES)
-        results.append(got[:, 0] + got[:, 1])
-    one_slot = iota((NT, LANES), 1) // slot_lanes
-    for zb in range(z_blocks):
-        for g in range(G):
-            at = (g // 4) * LANES
-            value = jnp.zeros((NT, LANES), F32)
-            for comp in range(6):
-                value = jnp.where(
-                    one_slot == (comp + g) % 6, results[comp][zb, :, at : at + LANES], value
-                )
-            out_ref[zb * G + g] = value
+    left = jnp.concatenate(rows, axis=0).astype(BF16)
+    got = jnp.dot(left, pick, preferred_element_type=F32)
+    got = got.reshape(6 * z_blocks, 2, NT, 2 * LANES)
+    got = (got[:, 0] + got[:, 1]).reshape(6, z_blocks * NT, 2 * LANES)
+    slot = iota((z_blocks * NT, LANES), 1) // slot_lanes
+    per_half = LANES // GROUP
+    for g in range(G):
+        at = (g // per_half) * LANES
+        value = jnp.zeros((z_blocks * NT, LANES), F32)
+        for comp in range(6):
+            shift = (comp * slot_lanes - (g % per_half) * GROUP) % LANES
+            part = got[comp, :, at : at + LANES]
+            part = pltpu.roll(part, shift, 1) if shift else part
+            value = jnp.where(slot == comp, part, value)
+        for zb in range(z_blocks):
+            out_ref[zb * G + g] = value[zb * NT : (zb + 1) * NT]
 
 
 def link_times(links, vec):
@@ -218,7 +215,7 @@
     comp = row // CROWS
     z_step = lane % slot_lanes % zh - row % CROWS // block_x
     x_step = lane % slot_lanes // zh - row % block_x
-    here = (lane // slot_lanes == (comp + place % G) % 6) & (row % CROWS < count)
+    here = (lane // slot_lanes == comp) & (row % CROWS < count)
     here = here & (x_step >= 0) & (x_step < 2) & (z_step >= 0) & (z_step < 2)
     table = jnp.broadcast_to(table_ref[0:1], shape)
     for y_step in range(2):

time: 31.9 us -> 32.1 us (level)
  no operation moved by 1% of the time
where the time goes in v13:
time: 32.1 us; the launch traced here: 31.8 us
  starting transfers between devices  12.1 us (38%)
  blocking collectives  9.88 us (31%)
  Pallas kernels  5.31 us (17%)
  waiting for transfers between devices  3.82 us (12%)
  between operations  0.7 us (2%)
    all_to_all x1, blocking collectives, shards(): lax.all_to_all(partial.reshape(devices, 1, LANES), 'zs', split_axis=0, co...  9.88 us
    ppermute x3, starting transfers between devices, passed_along(): return lax.ppermute(block, axis, route)  8.29 us
    all_to_all x1, starting transfers between devices, shards(): got = lax.all_to_all(payload, 'zs', split_axis=0, concat_axis=0, tiled=True)  3.83 us
    ppermute x3, waiting for transfers between devices, passed_along(): return lax.ppermute(block, axis, route)  3.12 us
    pallas_call x1, Pallas kernels, shards(): pl.pallas_call(functools.partial(pack_kernel, block_z, block_x), out_shap...  1.96 us
    pallas_call x1, Pallas kernels, shards(): pl.pallas_call(functools.partial(chain_kernel, depth_z, scale, block_z, b...  1.4 us
    pallas_call x1, Pallas kernels, shards(): pl.pallas_call(functools.partial(meet_kernel, block_z, block_x), out_shap...  1.07 us
    all_to_all x1, waiting for transfers between devices, shards(): got = lax.all_to_all(payload, 'zs', split_axis=0, concat_axis=0, tiled=True)  0.7 us
  transfers between devices with their start and end apart: 4, of which 2 were waited for; matrix products, arithmetic and copies ran while one was open for 0% of the time, Pallas kernels for 11%

profile of v13, /device:TPU:0, one launch (start us, length us, event | category | flops | bytes accessed | tf_op | source)
XLA Modules:
  0.0 31.8 jit_solution(5043733693866510622)
XLA Ops:
  0.6 5.1 %collective-permute-start.1 = (bf16[6,6,2,256]{3,2,1,0:T(2,128)(2,1)}, bf16[6,6,2,256]{3,2,1,0:T(2,128)(2,1)S(1)}, u32[]{:S(2)}, u32[]{:S(2)}) collective-permute-start(bf16[6,6,2,256]{3,2,1,0:T(2,128)(2,1)} %bitcast.19), channel_id=1, source_target_pairs={{8,0},{9,1},{10,2},{11,3},{12,4},{13,5},{14,6},{15,7},{16,8},{17,9... | collective-permute-start | bytes 110600 | tf_op jit(solution)/shard_map/ppermute | solution.py:29
  5.7 0.4 %collective-permute-start = (bf16[18,6,2,256]{3,2,1,0:T(2,128)(2,1)}, bf16[18,6,2,256]{3,2,1,0:T(2,128)(2,1)S(1)}, u32[]{:S(2)}, u32[]{:S(2)}) collective-permute-start(bf16[18,6,2,256]{3,2,1,0:T(2,128)(2,1)} %bitcast.14), channel_id=1, source_target_pairs={{8,0},{9,1},{10,2},{11,3},{12,4},{13,5},{14,6},{15,7},{16,8},{17,9... | collective-permute-start | bytes 331784 | tf_op jit(solution)/shard_map/ppermute | solution.py:29
  6.2 2.0 %pack.1 = (f32[32,8,128]{2,1,0:T(8,128)}, s32[8,128]{1,0:T(8,128)}, f32[8,128]{1,0:T(8,128)}) custom-call(f32[8]{0:T(128)} %weight_ref.1, s32[3,8]{1,0:T(4,128)} %bitcast.27, bf16[2,3,8,384]{3,2,1,0:T(8,128)(2,1)} %up_ref.1, bf16[2,3,8,384]{3,2,1,0:T(8,128)(2,1)} %down_ref.1, s32[8,128]{1,0:T(8,128)} %bitcast.24, s32[8,128]{1,0:T(8,128)} %bitcast.25, ...), custom_call_target="tpu_custom_call" | custom-call | flops 2000000000 | bytes 400000 | tf_op jit(solution)/shard_map/pack/pallas_call | solution.py:356
  8.1 0.0 copy-start
  8.1 0.0 copy-start.1
  8.1 3.8 %all-to-all-start = ((f32[32,8,128]{2,1,0:T(8,128)}), f32[32,8,128]{2,1,0:T(8,128)S(1)}, u32[]{:S(2)}, u32[]{:S(2)}) async-start(f32[32,8,128]{2,1,0:T(8,128)} %get-tuple-element.10), calls=%async_computation | async-start | bytes 262144 | tf_op jit(solution)/shard_map/all_to_all | solution.py:384
  12.0 0.0 copy-start.2
  12.0 0.0 copy-start.3
  12.0 0.0 collective-permute-done.links_next_ref.ready_ref
  12.0 0.0 copy-done
  12.0 0.0 copy-done.1
  12.1 2.7 %collective-permute-start.2 = (bf16[18,2,256]{2,1,0:T(2,128)(2,1)S(1)}, bf16[18,2,256]{2,1,0:T(2,128)(2,1)S(1)}, u32[]{:S(2)}, u32[]{:S(2)}) collective-permute-start(bf16[18,2,256]{2,1,0:T(2,128)(2,1)S(1)} %edge.1), channel_id=1, source_target_pairs={{16,0},{17,1},{18,2},{19,3},{20,4},{21,5},{22,6},{23,7},{24,8},{25... | collective-permute-start | bytes 55304 | tf_op jit(solution)/shard_map/ppermute | solution.py:29
  14.8 0.0 collective-permute-done.1.forward_next_ref
  14.8 0.0 copy-done.2
  14.8 0.0 copy-done.3
  14.8 1.4 %chain.1 = (f32[8,96,256]{2,1,0:T(8,128)S(1)}, bf16[2,192,128]{2,1,0:T(8,128)(2,1)S(1)}, s32[8,128]{1,0:T(8,128)S(1)}) custom-call(f32[8,128]{1,0:T(8,128)S(1)} %copy-done.3, s32[8,128]{1,0:T(8,128)S(1)} %copy-done.2, bf16[18,6,2,256]{3,2,1,0:T(2,128)(2,1)S(1)} %bitcast.16, bf16[18,6,2,256]{3,2,1,0:T(2,128)(2,1)S(1)} %collective-permute-done.links_next_ref.ready_ref, ...), custom_call_target="tpu_custom_call" | custom-call | flops 3000000000 | bytes 200000 | tf_op jit(solution)/shard_map/chain/pallas_call | solution.py:397
  16.2 3.1 %collective-permute-done.2.edge_ref = bf16[18,2,256]{2,1,0:T(2,128)(2,1)S(1)} collective-permute-done((bf16[18,2,256]{2,1,0:T(2,128)(2,1)S(1)}, bf16[18,2,256]{2,1,0:T(2,128)(2,1)S(1)}, u32[]{:S(2)}, u32[]{:S(2)}) %collective-permute-start.2) | collective-permute-done | bytes 18464 | tf_op jit(solution)/shard_map/ppermute | solution.py:29
  19.4 0.2 tail.1.extra_ref
  19.6 0.7 %all-to-all-done.got_ref = f32[32,8,128]{2,1,0:T(8,128)S(1)} async-done(((f32[32,8,128]{2,1,0:T(8,128)}), f32[32,8,128]{2,1,0:T(8,128)S(1)}, u32[]{:S(2)}, u32[]{:S(2)}) %all-to-all-start) | async-done | bytes 131104 | tf_op jit(solution)/shard_map/all_to_all | solution.py:384
  20.3 1.1 %meet.1 = (f32[6,6,2,256]{3,2,1,0:T(2,128)}, f32[32,128]{1,0:T(8,128)S(1)}) custom-call(f32[32,8,128]{2,1,0:T(8,128)S(1)} %all-to-all-done.got_ref, bf16[2,192,128]{2,1,0:T(8,128)(2,1)S(1)} %get-tuple-element.13.corner_ref, f32[8,96,256]{2,1,0:T(8,128)S(1)} %get-tuple-element.14.chain_ref, f32[2,96,256]{2,1,0:T(8,128)S(1)} %tail.1.extra_ref), custom_call_target="tpu_custom_call" | custom-call | flops 2000000000 | bytes 1000000 | tf_op jit(solution)/shard_map/meet/pallas_call | solution.py:425
  21.3 9.9 %all_to_all.10 = f32[32,1,128]{2,1,0:T(1,128)S(1)} all-to-all(f32[32,1,128]{2,1,0:T(1,128)S(1)} %bitcast.22), channel_id=1, replica_groups=mesh['grp'=1,'zs'=32] {'zs'}, dimensions={0} | all-to-all | bytes 32768 | tf_op jit(solution)/shard_map/all_to_all | solution.py:437
  31.2 0.6 %final.1 = f32[2,96]{1,0:T(2,128)} custom-call(f32[32,128]{1,0:T(8,128)S(1)} %bitcast.18, s32[8,128]{1,0:T(8,128)S(1)} %get-tuple-element.17.picked_ref), custom_call_target="tpu_custom_call" | custom-call | tf_op jit(solution)/shard_map/final/pallas_call | solution.py:440
  (1 shorter events, 0.0 us)
Async XLA Ops:
  0.6 14.2 %collective-permute-start.1 = (bf16[6,6,2,256]{3,2,1,0:T(2,128)(2,1)}, bf16[6,6,2,256]{3,2,1,0:T(2,128)(2,1)S(1)}, u32[]{:S(2)}, u32[]{:S(2)}) collective-permute-start(bf16[6,6,2,256]{3,2,1,0:T(2,128)(2,1)} %bitcast.19), channel_id=1, source_target_pairs={{8,0},{9,1},{10,2},{11,3},{12,4},{13,5},{14,6},{15,7},{16,8},{17,9... | collective-permute-start | bytes 110600 | tf_op jit(solution)/shard_map/ppermute | solution.py:29
  5.7 6.3 %collective-permute-start = (bf16[18,6,2,256]{3,2,1,0:T(2,128)(2,1)}, bf16[18,6,2,256]{3,2,1,0:T(2,128)(2,1)S(1)}, u32[]{:S(2)}, u32[]{:S(2)}) collective-permute-start(bf16[18,6,2,256]{3,2,1,0:T(2,128)(2,1)} %bitcast.14), channel_id=1, source_target_pairs={{8,0},{9,1},{10,2},{11,3},{12,4},{13,5},{14,6},{15,7},{16,8},{17,9... | collective-permute-start | bytes 331784 | tf_op jit(solution)/shard_map/ppermute | solution.py:29
  8.1 3.9 %copy-start = (bf16[2,3,3,1,6,2,256]{6,5,4,3,2,1,0:T(2,128)(2,1)S(1)}, bf16[2,3,3,1,6,2,256]{6,5,4,3,2,1,0:T(2,128)(2,1)}, u32[]{:S(2)}) copy-start(bf16[2,3,3,1,6,2,256]{6,5,4,3,2,1,0:T(2,128)(2,1)} %param.12) | copy-start | bytes 331780
  8.1 3.9 %copy-start.1 = (bf16[2,3,1,6,2,256]{5,4,3,2,1,0:T(2,128)(2,1)S(1)}, bf16[2,3,1,6,2,256]{5,4,3,2,1,0:T(2,128)(2,1)}, u32[]{:S(2)}) copy-start(bf16[2,3,1,6,2,256]{5,4,3,2,1,0:T(2,128)(2,1)} %param.11) | copy-start | bytes 110596
  8.1 12.1 %all-to-all-start = ((f32[32,8,128]{2,1,0:T(8,128)}), f32[32,8,128]{2,1,0:T(8,128)S(1)}, u32[]{:S(2)}, u32[]{:S(2)}) async-start(f32[32,8,128]{2,1,0:T(8,128)} %get-tuple-element.10), calls=%async_computation | async-start | bytes 262144 | tf_op jit(solution)/shard_map/all_to_all | solution.py:384
  12.0 2.8 %copy-start.2 = (s32[8,128]{1,0:T(8,128)S(1)}, s32[8,128]{1,0:T(8,128)}, u32[]{:S(2)}) copy-start(s32[8,128]{1,0:T(8,128)} %get-tuple-element.12.request_ref) | copy-start | bytes 12292
  12.0 2.8 %copy-start.3 = (f32[8,128]{1,0:T(8,128)S(1)}, f32[8,128]{1,0:T(8,128)}, u32[]{:S(2)}) copy-start(f32[8,128]{1,0:T(8,128)} %get-tuple-element.11.table_ref) | copy-start | bytes 12292
  12.1 7.3 %collective-permute-start.2 = (bf16[18,2,256]{2,1,0:T(2,128)(2,1)S(1)}, bf16[18,2,256]{2,1,0:T(2,128)(2,1)S(1)}, u32[]{:S(2)}, u32[]{:S(2)}) collective-permute-start(bf16[18,2,256]{2,1,0:T(2,128)(2,1)S(1)} %edge.1), channel_id=1, source_target_pairs={{16,0},{17,1},{18,2},{19,3},{20,4},{21,5},{22,6},{23,7},{24,8},{25... | collective-permute-start | bytes 55304 | tf_op jit(solution)/shard_map/ppermute | solution.py:29

commit v14 on v7

--- a/solution.py
+++ b/solution.py
@@ -3,6 +3,7 @@
 
 import jax
 import jax.numpy as jnp
+import numpy as np
 from jax import lax
 from jax.experimental import pallas as pl
 from jax.experimental.pallas import tpu as pltpu
@@ -35,6 +36,20 @@
 
 def iota(shape, axis):
     return lax.broadcasted_iota(jnp.int32, shape, axis)
+
+
+def pick_matrices(block_z, block_x):
+    zh = block_z + 1
+    lane = np.arange(2 * LANES)
+    half, slot, cell = lane // LANES, lane % LANES // (zh * XH), lane % LANES % (zh * XH)
+    width_x = block_x * G
+    picks = []
+    for comp in range(6):
+        turned = (slot + 12 - comp - 4 * half) % 6
+        source = cell % zh * width_x + (block_x * (turned + 4 * half) + cell // zh) % width_x
+        source = np.where((turned < 4) & (slot < 6), source, -1)
+        picks.append(np.arange(LANES)[:, None] == source[None, :])
+    return jnp.asarray(np.stack(picks), BF16)
 
 
 def pack_kernel(
@@ -47,6 +62,7 @@
     lengths_ref,
     separations_ref,
     owners_ref,
+    pick_ref,
     out_ref,
     request_ref,
     table_ref,
@@ -73,18 +89,8 @@
 
     planes = [cross(0, 0, c) - cross(1, 1, c) for c in range(3)]
     planes += [cross(0, 1, c) + cross(1, 0, c) for c in range(3)]
-    lane = iota((1, 2 * LANES), 1)
-    half = lane // LANES
-    within = lane % LANES
-    slot = within // slot_lanes
-    cell = within % slot_lanes
-    source_row = iota((LANES, 2 * LANES), 0)
     results = []
     for comp in range(6):
-        turned = (slot + 12 - comp - 4 * half) % 6
-        source = (cell % zh) * width_x + (block_x * (turned + 4 * half) + cell // zh) % width_x
-        source = jnp.where((turned < 4) & (slot < 6), source, -1)
-        pick = jnp.where(source_row == source, 1.0, 0.0).astype(BF16)
         wide = jnp.concatenate([planes[comp], planes[comp][:, :LANES]], axis=1)
         rows = []
         for zb in range(z_blocks):
@@ -93,7 +99,7 @@
             high = part.astype(BF16).astype(F32)
             rows += [high, part - high]
         left = jnp.concatenate(rows, axis=0).astype(BF16)
-        got = jnp.dot(left, pick, preferred_element_type=F32)
+        got = jnp.dot(left, pick_ref[comp], preferred_element_type=F32)
         got = got.reshape(z_blocks, 2, NT, 2 * LANES)
         results.append(got[:, 0] + got[:, 1])
     one_slot = iota((NT, LANES), 1) // slot_lanes
@@ -366,7 +372,8 @@
         grid=(1,),
         in_specs=[SMEM] * 2
         + [pl.BlockSpec(quark_up.shape, lambda i: (0, 0, 0, 0))] * 2
-        + [pl.BlockSpec(requests, lambda i: (0, 0))] * 3,
+        + [pl.BlockSpec(requests, lambda i: (0, 0))] * 3
+        + [pl.BlockSpec((6, LANES, 2 * LANES), lambda i: (0, 0, 0))],
         out_specs=(
             pl.BlockSpec((devices, NT, LANES), lambda i: (0, 0, 0)),
             pl.BlockSpec(requests, lambda i: (0, 0)),
@@ -383,6 +390,7 @@
         lengths.reshape(requests),
         separations.reshape(requests),
         owner_map.reshape(requests),
+        pick_matrices(block_z, block_x),
     )
     got = lax.all_to_all(payload, "zs", split_axis=0, concat_axis=0, tiled=True)
 

time: 31.9 us -> 32.1 us (level)
  no operation moved by 1% of the time
where the time goes in v14:
time: 32.1 us; the launch traced here: 31.9 us
  starting transfers between devices  12.1 us (38%)
  blocking collectives  9.88 us (31%)
  Pallas kernels  5.37 us (17%)
  waiting for transfers between devices  3.8 us (12%)
  between operations  0.7 us (2%)
    all_to_all x1, blocking collectives, shards(): lax.all_to_all(partial.reshape(devices, 1, LANES), 'zs', split_axis=0, co...  9.88 us
    ppermute x3, starting transfers between devices, passed_along(): return lax.ppermute(block, axis, route)  8.29 us
    all_to_all x1, starting transfers between devices, shards(): got = lax.all_to_all(payload, 'zs', split_axis=0, concat_axis=0, tiled=True)  3.83 us
    ppermute x3, waiting for transfers between devices, passed_along(): return lax.ppermute(block, axis, route)  3.1 us
    pallas_call x1, Pallas kernels, shards(): pl.pallas_call(functools.partial(pack_kernel, block_z, block_x), out_shap...  2 us
    pallas_call x1, Pallas kernels, shards(): pl.pallas_call(functools.partial(chain_kernel, depth_z, scale, block_z, b...  1.42 us
    pallas_call x1, Pallas kernels, shards(): pl.pallas_call(functools.partial(meet_kernel, block_z, block_x), out_shap...  1.07 us
    all_to_all x1, waiting for transfers between devices, shards(): got = lax.all_to_all(payload, 'zs', split_axis=0, concat_axis=0, tiled=True)  0.7 us
  transfers between devices with their start and end apart: 4, of which 2 were waited for; matrix products, arithmetic and copies ran while one was open for 0% of the time, Pallas kernels for 11%

profile of v14, /device:TPU:0, one launch (start us, length us, event | category | flops | bytes accessed | tf_op | source)
XLA Modules:
  0.0 31.9 jit_solution(5578055471225857859)
XLA Ops:
  0.6 5.1 %collective-permute-start.1 = (bf16[6,6,2,256]{3,2,1,0:T(2,128)(2,1)}, bf16[6,6,2,256]{3,2,1,0:T(2,128)(2,1)S(1)}, u32[]{:S(2)}, u32[]{:S(2)}) collective-permute-start(bf16[6,6,2,256]{3,2,1,0:T(2,128)(2,1)} %bitcast.19), channel_id=1, source_target_pairs={{8,0},{9,1},{10,2},{11,3},{12,4},{13,5},{14,6},{15,7},{16,8},{17,9... | collective-permute-start | bytes 110600 | tf_op jit(solution)/shard_map/ppermute | solution.py:29
  5.7 0.4 %collective-permute-start = (bf16[18,6,2,256]{3,2,1,0:T(2,128)(2,1)}, bf16[18,6,2,256]{3,2,1,0:T(2,128)(2,1)S(1)}, u32[]{:S(2)}, u32[]{:S(2)}) collective-permute-start(bf16[18,6,2,256]{3,2,1,0:T(2,128)(2,1)} %bitcast.14), channel_id=1, source_target_pairs={{8,0},{9,1},{10,2},{11,3},{12,4},{13,5},{14,6},{15,7},{16,8},{17,9... | collective-permute-start | bytes 331784 | tf_op jit(solution)/shard_map/ppermute | solution.py:29
  6.2 2.0 %pack.1 = (f32[32,8,128]{2,1,0:T(8,128)}, s32[8,128]{1,0:T(8,128)}, f32[8,128]{1,0:T(8,128)}) custom-call(f32[8]{0:T(128)} %weight_ref.1, s32[3,8]{1,0:T(4,128)} %bitcast.27, bf16[2,3,8,384]{3,2,1,0:T(8,128)(2,1)} %up_ref.1, bf16[2,3,8,384]{3,2,1,0:T(8,128)(2,1)} %down_ref.1, s32[8,128]{1,0:T(8,128)} %bitcast.24, s32[8,128]{1,0:T(8,128)} %bitcast.25, ...), custom_call_target="tpu_custom_call" | custom-call | flops 2000000000 | bytes 400000 | tf_op jit(solution)/shard_map/pack/pallas_call | solution.py:365
  8.2 0.0 copy-start
  8.2 0.0 copy-start.1
  8.2 3.8 %all-to-all-start = ((f32[32,8,128]{2,1,0:T(8,128)}), f32[32,8,128]{2,1,0:T(8,128)S(1)}, u32[]{:S(2)}, u32[]{:S(2)}) async-start(f32[32,8,128]{2,1,0:T(8,128)} %get-tuple-element.10), calls=%async_computation | async-start | bytes 262144 | tf_op jit(solution)/shard_map/all_to_all | solution.py:395
  12.0 0.0 copy-start.2
  12.0 0.0 copy-start.3
  12.1 0.0 collective-permute-done.links_next_ref.ready_ref
  12.1 0.0 copy-done
  12.1 0.0 copy-done.1
  12.1 2.7 %collective-permute-start.2 = (bf16[18,2,256]{2,1,0:T(2,128)(2,1)S(1)}, bf16[18,2,256]{2,1,0:T(2,128)(2,1)S(1)}, u32[]{:S(2)}, u32[]{:S(2)}) collective-permute-start(bf16[18,2,256]{2,1,0:T(2,128)(2,1)S(1)} %edge.1), channel_id=1, source_target_pairs={{16,0},{17,1},{18,2},{19,3},{20,4},{21,5},{22,6},{23,7},{24,8},{25... | collective-permute-start | bytes 55304 | tf_op jit(solution)/shard_map/ppermute | solution.py:29
  14.9 0.0 collective-permute-done.1.forward_next_ref
  14.9 0.0 copy-done.2
  14.9 0.0 copy-done.3
  14.9 1.4 %chain.1 = (f32[8,96,256]{2,1,0:T(8,128)S(1)}, bf16[2,192,128]{2,1,0:T(8,128)(2,1)S(1)}, s32[8,128]{1,0:T(8,128)S(1)}) custom-call(f32[8,128]{1,0:T(8,128)S(1)} %copy-done.3, s32[8,128]{1,0:T(8,128)S(1)} %copy-done.2, bf16[18,6,2,256]{3,2,1,0:T(2,128)(2,1)S(1)} %bitcast.16, bf16[18,6,2,256]{3,2,1,0:T(2,128)(2,1)S(1)} %collective-permute-done.links_next_ref.ready_ref, ...), custom_call_target="tpu_custom_call" | custom-call | flops 3000000000 | bytes 200000 | tf_op jit(solution)/shard_map/chain/pallas_call | solution.py:408
  16.3 3.1 %collective-permute-done.2.edge_ref = bf16[18,2,256]{2,1,0:T(2,128)(2,1)S(1)} collective-permute-done((bf16[18,2,256]{2,1,0:T(2,128)(2,1)S(1)}, bf16[18,2,256]{2,1,0:T(2,128)(2,1)S(1)}, u32[]{:S(2)}, u32[]{:S(2)}) %collective-permute-start.2) | collective-permute-done | bytes 18464 | tf_op jit(solution)/shard_map/ppermute | solution.py:29
  19.4 0.2 tail.1.extra_ref
  19.6 0.7 %all-to-all-done.got_ref = f32[32,8,128]{2,1,0:T(8,128)S(1)} async-done(((f32[32,8,128]{2,1,0:T(8,128)}), f32[32,8,128]{2,1,0:T(8,128)S(1)}, u32[]{:S(2)}, u32[]{:S(2)}) %all-to-all-start) | async-done | bytes 131104 | tf_op jit(solution)/shard_map/all_to_all | solution.py:395
  20.3 1.1 %meet.1 = (f32[6,6,2,256]{3,2,1,0:T(2,128)}, f32[32,128]{1,0:T(8,128)S(1)}) custom-call(f32[32,8,128]{2,1,0:T(8,128)S(1)} %all-to-all-done.got_ref, bf16[2,192,128]{2,1,0:T(8,128)(2,1)S(1)} %get-tuple-element.13.corner_ref, f32[8,96,256]{2,1,0:T(8,128)S(1)} %get-tuple-element.14.chain_ref, f32[2,96,256]{2,1,0:T(8,128)S(1)} %tail.1.extra_ref), custom_call_target="tpu_custom_call" | custom-call | flops 2000000000 | bytes 1000000 | tf_op jit(solution)/shard_map/meet/pallas_call | solution.py:436
  21.4 9.9 %all_to_all.10 = f32[32,1,128]{2,1,0:T(1,128)S(1)} all-to-all(f32[32,1,128]{2,1,0:T(1,128)S(1)} %bitcast.22), channel_id=1, replica_groups=mesh['grp'=1,'zs'=32] {'zs'}, dimensions={0} | all-to-all | bytes 32768 | tf_op jit(solution)/shard_map/all_to_all | solution.py:448
  31.2 0.6 %final.1 = f32[2,96]{1,0:T(2,128)} custom-call(f32[32,128]{1,0:T(8,128)S(1)} %bitcast.18, s32[8,128]{1,0:T(8,128)S(1)} %get-tuple-element.17.picked_ref), custom_call_target="tpu_custom_call" | custom-call | tf_op jit(solution)/shard_map/final/pallas_call | solution.py:451
  (1 shorter events, 0.0 us)
Async XLA Ops:
  0.6 14.2 %collective-permute-start.1 = (bf16[6,6,2,256]{3,2,1,0:T(2,128)(2,1)}, bf16[6,6,2,256]{3,2,1,0:T(2,128)(2,1)S(1)}, u32[]{:S(2)}, u32[]{:S(2)}) collective-permute-start(bf16[6,6,2,256]{3,2,1,0:T(2,128)(2,1)} %bitcast.19), channel_id=1, source_target_pairs={{8,0},{9,1},{10,2},{11,3},{12,4},{13,5},{14,6},{15,7},{16,8},{17,9... | collective-permute-start | bytes 110600 | tf_op jit(solution)/shard_map/ppermute | solution.py:29
  5.7 6.3 %collective-permute-start = (bf16[18,6,2,256]{3,2,1,0:T(2,128)(2,1)}, bf16[18,6,2,256]{3,2,1,0:T(2,128)(2,1)S(1)}, u32[]{:S(2)}, u32[]{:S(2)}) collective-permute-start(bf16[18,6,2,256]{3,2,1,0:T(2,128)(2,1)} %bitcast.14), channel_id=1, source_target_pairs={{8,0},{9,1},{10,2},{11,3},{12,4},{13,5},{14,6},{15,7},{16,8},{17,9... | collective-permute-start | bytes 331784 | tf_op jit(solution)/shard_map/ppermute | solution.py:29
  8.2 3.9 %copy-start = (bf16[2,3,3,1,6,2,256]{6,5,4,3,2,1,0:T(2,128)(2,1)S(1)}, bf16[2,3,3,1,6,2,256]{6,5,4,3,2,1,0:T(2,128)(2,1)}, u32[]{:S(2)}) copy-start(bf16[2,3,3,1,6,2,256]{6,5,4,3,2,1,0:T(2,128)(2,1)} %param.13) | copy-start | bytes 331780
  8.2 3.9 %copy-start.1 = (bf16[2,3,1,6,2,256]{5,4,3,2,1,0:T(2,128)(2,1)S(1)}, bf16[2,3,1,6,2,256]{5,4,3,2,1,0:T(2,128)(2,1)}, u32[]{:S(2)}) copy-start(bf16[2,3,1,6,2,256]{5,4,3,2,1,0:T(2,128)(2,1)} %param.12) | copy-start | bytes 110596
  8.2 12.1 %all-to-all-start = ((f32[32,8,128]{2,1,0:T(8,128)}), f32[32,8,128]{2,1,0:T(8,128)S(1)}, u32[]{:S(2)}, u32[]{:S(2)}) async-start(f32[32,8,128]{2,1,0:T(8,128)} %get-tuple-element.10), calls=%async_computation | async-start | bytes 262144 | tf_op jit(solution)/shard_map/all_to_all | solution.py:395
  12.0 2.8 %copy-start.2 = (s32[8,128]{1,0:T(8,128)S(1)}, s32[8,128]{1,0:T(8,128)}, u32[]{:S(2)}) copy-start(s32[8,128]{1,0:T(8,128)} %get-tuple-element.12.request_ref) | copy-start | bytes 12292
  12.0 2.8 %copy-start.3 = (f32[8,128]{1,0:T(8,128)S(1)}, f32[8,128]{1,0:T(8,128)}, u32[]{:S(2)}) copy-start(f32[8,128]{1,0:T(8,128)} %get-tuple-element.11.table_ref) | copy-start | bytes 12292
  12.1 7.3 %collective-permute-start.2 = (bf16[18,2,256]{2,1,0:T(2,128)(2,1)S(1)}, bf16[18,2,256]{2,1,0:T(2,128)(2,1)S(1)}, u32[]{:S(2)}, u32[]{:S(2)}) collective-permute-start(bf16[18,2,256]{2,1,0:T(2,128)(2,1)S(1)} %edge.1), channel_id=1, source_target_pairs={{16,0},{17,1},{18,2},{19,3},{20,4},{21,5},{22,6},{23,7},{24,8},{25... | collective-permute-start | bytes 55304 | tf_op jit(solution)/shard_map/ppermute | solution.py:29

commit v15 on v7

--- a/solution.py
+++ b/solution.py
@@ -387,16 +387,6 @@
     got = lax.all_to_all(payload, "zs", split_axis=0, concat_axis=0, tiled=True)
 
     past = LMAX - block_z
-    edge = pl.pallas_call(
-        edge_kernel,
-        out_shape=jax.ShapeDtypeStruct((18, block_x, rows_y), BF16),
-        in_specs=[VMEM] * 2 + [pl.BlockSpec(memory_space=pl.ANY)],
-        out_specs=VMEM,
-        compiler_params=PARAMS,
-        cost_estimate=cost(50_000_000, 60_000),
-        name="edge",
-    )(links, field, links_next)
-    edge_next = passed_along(edge, "zs", -2 * G)
     chain, corner, picked = pl.pallas_call(
         functools.partial(chain_kernel, depth_z, scale, block_z, block_x),
         out_shape=(
@@ -415,6 +405,16 @@
         name="chain",
     )(table, request, links, links_next, field, field_next)
 
+    edge = pl.pallas_call(
+        edge_kernel,
+        out_shape=jax.ShapeDtypeStruct((18, block_x, rows_y), BF16),
+        in_specs=[VMEM] * 2 + [pl.BlockSpec(memory_space=pl.ANY)],
+        out_specs=VMEM,
+        compiler_params=PARAMS,
+        cost_estimate=cost(50_000_000, 60_000),
+        name="edge",
+    )(links, field, corner)
+    edge_next = passed_along(edge, "zs", -2 * G)
     extra = pl.pallas_call(
         functools.partial(tail_kernel, depth_z, scale, block_z, block_x),
         out_shape=jax.ShapeDtypeStruct((past, 6 * CROWS, rows_y), F32),

time: 31.9 us -> 33.2 us (1.041)
  blocking collectives: 9.88 us -> 11.2 us
    all_to_all x1, blocking collectives: 9.88 us -> 11.2 us  [shards(): lax.all_to_all(partial.reshape(devices, 1, LANES), 'zs', split_axis=0, co...]
where the time goes in v15:
time: 33.2 us; the launch traced here: 32.9 us
  starting transfers between devices  12.1 us (36%)
  blocking collectives  11.2 us (34%)
  Pallas kernels  5.17 us (16%)
  waiting for transfers between devices  3.76 us (11%)
  between operations  0.72 us (2%)
    all_to_all x1, blocking collectives, shards(): lax.all_to_all(partial.reshape(devices, 1, LANES), 'zs', split_axis=0, co...  11.2 us
    ppermute x3, starting transfers between devices, passed_along(): return lax.ppermute(block, axis, route)  8.29 us
    all_to_all x1, starting transfers between devices, shards(): got = lax.all_to_all(payload, 'zs', split_axis=0, concat_axis=0, tiled=True)  3.83 us
    ppermute x3, waiting for transfers between devices, passed_along(): return lax.ppermute(block, axis, route)  2.9 us
    pallas_call x1, Pallas kernels, shards(): pl.pallas_call(functools.partial(pack_kernel, block_z, block_x), out_shap...  1.8 us
    pallas_call x1, Pallas kernels, shards(): pl.pallas_call(functools.partial(chain_kernel, depth_z, scale, block_z, b...  1.42 us
    pallas_call x1, Pallas kernels, shards(): pl.pallas_call(functools.partial(meet_kernel, block_z, block_x), out_shap...  1.07 us
    all_to_all x1, waiting for transfers between devices, shards(): got = lax.all_to_all(payload, 'zs', split_axis=0, concat_axis=0, tiled=True)  0.87 us
  transfers between devices with their start and end apart: 4, of which 2 were waited for; matrix products, arithmetic and copies ran while one was open for 0% of the time, Pallas kernels for 11%

profile of v15, /device:TPU:0, one launch (start us, length us, event | category | flops | bytes accessed | tf_op | source)
XLA Modules:
  0.0 32.9 jit_solution(2622580152713471252)
XLA Ops:
  0.6 5.1 %collective-permute-start.1 = (bf16[6,6,2,256]{3,2,1,0:T(2,128)(2,1)}, bf16[6,6,2,256]{3,2,1,0:T(2,128)(2,1)S(1)}, u32[]{:S(2)}, u32[]{:S(2)}) collective-permute-start(bf16[6,6,2,256]{3,2,1,0:T(2,128)(2,1)} %bitcast.19), channel_id=1, source_target_pairs={{8,0},{9,1},{10,2},{11,3},{12,4},{13,5},{14,6},{15,7},{16,8},{17,9... | collective-permute-start | bytes 110600 | tf_op jit(solution)/shard_map/ppermute | solution.py:28
  5.7 0.4 %collective-permute-start = (bf16[18,6,2,256]{3,2,1,0:T(2,128)(2,1)}, bf16[18,6,2,256]{3,2,1,0:T(2,128)(2,1)S(1)}, u32[]{:S(2)}, u32[]{:S(2)}) collective-permute-start(bf16[18,6,2,256]{3,2,1,0:T(2,128)(2,1)} %bitcast.14), channel_id=1, source_target_pairs={{8,0},{9,1},{10,2},{11,3},{12,4},{13,5},{14,6},{15,7},{16,8},{17,9... | collective-permute-start | bytes 331784 | tf_op jit(solution)/shard_map/ppermute | solution.py:28
  6.2 1.8 %pack.1 = (f32[32,8,128]{2,1,0:T(8,128)}, s32[8,128]{1,0:T(8,128)}, f32[8,128]{1,0:T(8,128)}) custom-call(f32[8]{0:T(128)} %weight_ref.1, s32[3,8]{1,0:T(4,128)} %bitcast.27, bf16[2,3,8,384]{3,2,1,0:T(8,128)(2,1)} %up_ref.1, bf16[2,3,8,384]{3,2,1,0:T(8,128)(2,1)} %down_ref.1, s32[8,128]{1,0:T(8,128)} %bitcast.24, s32[8,128]{1,0:T(8,128)} %bitcast.25, ...), custom_call_target="tpu_custom_call" | custom-call | flops 2000000000 | bytes 400000 | tf_op jit(solution)/shard_map/pack/pallas_call | solution.py:359
  8.0 0.0 copy-start
  8.0 0.0 copy-start.1
  8.0 0.0 copy-start.2
  8.0 0.0 copy-start.3
  8.0 3.8 %all-to-all-start = ((f32[32,8,128]{2,1,0:T(8,128)}), f32[32,8,128]{2,1,0:T(8,128)S(1)}, u32[]{:S(2)}, u32[]{:S(2)}) async-start(f32[32,8,128]{2,1,0:T(8,128)} %get-tuple-element.10), calls=%async_computation | async-start | bytes 262144 | tf_op jit(solution)/shard_map/all_to_all | solution.py:387
  11.9 0.0 collective-permute-done.1.forward_next_ref
  11.9 0.0 collective-permute-done.links_next_ref
  11.9 0.0 copy-done
  11.9 0.0 copy-done.1
  11.9 0.0 copy-done.2
  11.9 0.0 copy-done.3
  11.9 1.4 %chain.1 = (f32[8,96,256]{2,1,0:T(8,128)S(1)}, bf16[2,192,128]{2,1,0:T(8,128)(2,1)S(1)}, s32[8,128]{1,0:T(8,128)S(1)}) custom-call(f32[8,128]{1,0:T(8,128)S(1)} %copy-done.3, s32[8,128]{1,0:T(8,128)S(1)} %copy-done.2, bf16[18,6,2,256]{3,2,1,0:T(2,128)(2,1)S(1)} %bitcast.15, bf16[18,6,2,256]{3,2,1,0:T(2,128)(2,1)S(1)} %collective-permute-done.links_next_ref, ...), custom_call_target="tpu_custom_call" | custom-call | flops 3000000000 | bytes 200000 | tf_op jit(solution)/shard_map/chain/pallas_call | solution.py:390
  13.4 2.7 %collective-permute-start.2 = (bf16[18,2,256]{2,1,0:T(2,128)(2,1)S(1)}, bf16[18,2,256]{2,1,0:T(2,128)(2,1)S(1)}, u32[]{:S(2)}, u32[]{:S(2)}) collective-permute-start(bf16[18,2,256]{2,1,0:T(2,128)(2,1)S(1)} %edge.1), channel_id=1, source_target_pairs={{16,0},{17,1},{18,2},{19,3},{20,4},{21,5},{22,6},{23,7},{24,8},{25... | collective-permute-start | bytes 55304 | tf_op jit(solution)/shard_map/ppermute | solution.py:28
  16.1 2.9 %collective-permute-done.2.edge_ref = bf16[18,2,256]{2,1,0:T(2,128)(2,1)S(1)} collective-permute-done((bf16[18,2,256]{2,1,0:T(2,128)(2,1)S(1)}, bf16[18,2,256]{2,1,0:T(2,128)(2,1)S(1)}, u32[]{:S(2)}, u32[]{:S(2)}) %collective-permute-start.2) | collective-permute-done | bytes 18464 | tf_op jit(solution)/shard_map/ppermute | solution.py:28
  19.0 0.2 tail.1.extra_ref
  19.2 0.9 %all-to-all-done.got_ref = f32[32,8,128]{2,1,0:T(8,128)S(1)} async-done(((f32[32,8,128]{2,1,0:T(8,128)}), f32[32,8,128]{2,1,0:T(8,128)S(1)}, u32[]{:S(2)}, u32[]{:S(2)}) %all-to-all-start) | async-done | bytes 131104 | tf_op jit(solution)/shard_map/all_to_all | solution.py:387
  20.1 1.1 %meet.1 = (f32[6,6,2,256]{3,2,1,0:T(2,128)}, f32[32,128]{1,0:T(8,128)S(1)}) custom-call(f32[32,8,128]{2,1,0:T(8,128)S(1)} %all-to-all-done.got_ref, bf16[2,192,128]{2,1,0:T(8,128)(2,1)S(1)} %get-tuple-element.13.ready_ref.corner_ref, f32[8,96,256]{2,1,0:T(8,128)S(1)} %get-tuple-element.14.chain_ref, f32[2,96,256]{2,1,0:T(8,128)S(1)} %tail.1.extra_ref), custom_call_target="tpu_custom_call" | custom-call | flops 2000000000 | bytes 1000000 | tf_op jit(solution)/shard_map/meet/pallas_call | solution.py:428
  21.2 11.2 %all_to_all.10 = f32[32,1,128]{2,1,0:T(1,128)S(1)} all-to-all(f32[32,1,128]{2,1,0:T(1,128)S(1)} %bitcast.22), channel_id=1, replica_groups=mesh['grp'=1,'zs'=32] {'zs'}, dimensions={0} | all-to-all | bytes 32768 | tf_op jit(solution)/shard_map/all_to_all | solution.py:440
  32.3 0.6 %final.1 = f32[2,96]{1,0:T(2,128)} custom-call(f32[32,128]{1,0:T(8,128)S(1)} %bitcast.18, s32[8,128]{1,0:T(8,128)S(1)} %get-tuple-element.17.picked_ref), custom_call_target="tpu_custom_call" | custom-call | tf_op jit(solution)/shard_map/final/pallas_call | solution.py:443
  (1 shorter events, 0.0 us)
Async XLA Ops:
  0.6 11.2 %collective-permute-start.1 = (bf16[6,6,2,256]{3,2,1,0:T(2,128)(2,1)}, bf16[6,6,2,256]{3,2,1,0:T(2,128)(2,1)S(1)}, u32[]{:S(2)}, u32[]{:S(2)}) collective-permute-start(bf16[6,6,2,256]{3,2,1,0:T(2,128)(2,1)} %bitcast.19), channel_id=1, source_target_pairs={{8,0},{9,1},{10,2},{11,3},{12,4},{13,5},{14,6},{15,7},{16,8},{17,9... | collective-permute-start | bytes 110600 | tf_op jit(solution)/shard_map/ppermute | solution.py:28
  5.7 6.1 %collective-permute-start = (bf16[18,6,2,256]{3,2,1,0:T(2,128)(2,1)}, bf16[18,6,2,256]{3,2,1,0:T(2,128)(2,1)S(1)}, u32[]{:S(2)}, u32[]{:S(2)}) collective-permute-start(bf16[18,6,2,256]{3,2,1,0:T(2,128)(2,1)} %bitcast.14), channel_id=1, source_target_pairs={{8,0},{9,1},{10,2},{11,3},{12,4},{13,5},{14,6},{15,7},{16,8},{17,9... | collective-permute-start | bytes 331784 | tf_op jit(solution)/shard_map/ppermute | solution.py:28
  8.0 3.9 %copy-start = (bf16[2,3,3,1,6,2,256]{6,5,4,3,2,1,0:T(2,128)(2,1)S(1)}, bf16[2,3,3,1,6,2,256]{6,5,4,3,2,1,0:T(2,128)(2,1)}, u32[]{:S(2)}) copy-start(bf16[2,3,3,1,6,2,256]{6,5,4,3,2,1,0:T(2,128)(2,1)} %param.12) | copy-start | bytes 331780
  8.0 3.9 %copy-start.1 = (bf16[2,3,1,6,2,256]{5,4,3,2,1,0:T(2,128)(2,1)S(1)}, bf16[2,3,1,6,2,256]{5,4,3,2,1,0:T(2,128)(2,1)}, u32[]{:S(2)}) copy-start(bf16[2,3,1,6,2,256]{5,4,3,2,1,0:T(2,128)(2,1)} %param.11) | copy-start | bytes 110596
  8.0 3.9 %copy-start.2 = (s32[8,128]{1,0:T(8,128)S(1)}, s32[8,128]{1,0:T(8,128)}, u32[]{:S(2)}) copy-start(s32[8,128]{1,0:T(8,128)} %get-tuple-element.12.request_ref) | copy-start | bytes 12292
  8.0 3.9 %copy-start.3 = (f32[8,128]{1,0:T(8,128)S(1)}, f32[8,128]{1,0:T(8,128)}, u32[]{:S(2)}) copy-start(f32[8,128]{1,0:T(8,128)} %get-tuple-element.11.table_ref) | copy-start | bytes 12292
  8.0 12.1 %all-to-all-start = ((f32[32,8,128]{2,1,0:T(8,128)}), f32[32,8,128]{2,1,0:T(8,128)S(1)}, u32[]{:S(2)}, u32[]{:S(2)}) async-start(f32[32,8,128]{2,1,0:T(8,128)} %get-tuple-element.10), calls=%async_computation | async-start | bytes 262144 | tf_op jit(solution)/shard_map/all_to_all | solution.py:387
  13.4 5.6 %collective-permute-start.2 = (bf16[18,2,256]{2,1,0:T(2,128)(2,1)S(1)}, bf16[18,2,256]{2,1,0:T(2,128)(2,1)S(1)}, u32[]{:S(2)}, u32[]{:S(2)}) collective-permute-start(bf16[18,2,256]{2,1,0:T(2,128)(2,1)S(1)} %edge.1), channel_id=1, source_target_pairs={{16,0},{17,1},{18,2},{19,3},{20,4},{21,5},{22,6},{23,7},{24,8},{25... | collective-permute-start | bytes 55304 | tf_op jit(solution)/shard_map/ppermute | solution.py:28

commit v16 on v7

--- a/solution.py
+++ b/solution.py
@@ -225,8 +225,8 @@
         corner = jnp.where(here, 4 * x_step + 2 * y_step + z_step, 0)
         weights = jnp.where(here, jnp.take_along_axis(table, corner, axis=1), 0.0)
         high, low = split_two(weights)
-        corner_ref[0, y_step * 6 * CROWS : (y_step + 1) * 6 * CROWS] = high
-        corner_ref[1, y_step * 6 * CROWS : (y_step + 1) * 6 * CROWS] = low
+        rows = slice(y_step * 6 * CROWS, (y_step + 1) * 6 * CROWS)
+        corner_ref[rows] = jnp.concatenate([high, high, low], axis=1)
 
     request = request_ref[...]
     mine = request // LANES == place
@@ -279,10 +279,8 @@
     rows_y = got_ref.shape[0] * NT
     got = got_ref[...].reshape(rows_y, LANES)
     high, low = split_two(got)
-    dot = functools.partial(
-        lax.dot_general, dimension_numbers=NT_DIMS, preferred_element_type=F32
-    )
-    both = dot(corner_ref[0], high) + dot(corner_ref[0], low) + dot(corner_ref[1], high)
+    terms = jnp.concatenate([high, low, high], axis=1)
+    both = lax.dot_general(corner_ref[...], terms, NT_DIMS, preferred_element_type=F32)
     size = 6 * CROWS
     seq = both[:size] + pltpu.roll(both[size:], rows_y - NT, 1)
     for comp in range(6):
@@ -303,11 +301,15 @@
             narrow = part[:, :LANES]
             for at in range(LANES, rows_y, LANES):
                 narrow = narrow + part[:, at : at + LANES]
-            sums.append(jnp.sum(narrow, axis=0, keepdims=True))
-    table = jnp.concatenate(sums, axis=0)
-    for shift in (64, 32, 16, 8):
-        table = table + pltpu.roll(table, shift, 1)
-    mine = iota((2 * LMAX, LANES), 1) // NT == iota((2 * LMAX, LANES), 0)
+            sums.append(narrow)
+    rows = 2 * LMAX * 8
+    high, low = split_two(jnp.concatenate(sums, axis=0))
+    same_t = jnp.where(iota((LANES, LANES), 0) % NT == iota((LANES, LANES), 1) % NT, 1.0, 0.0)
+    table = jnp.dot(
+        jnp.concatenate([high, low], axis=0), same_t.astype(BF16), preferred_element_type=F32
+    )
+    table = table[:rows] + table[rows:]
+    mine = iota((rows, LANES), 1) // NT == iota((rows, LANES), 0) // 8
     flat = jnp.sum(jnp.where(mine, table, 0.0), axis=0, keepdims=True)
     table_ref[...] = jnp.broadcast_to(flat, table_ref.shape)
 
@@ -401,7 +403,7 @@
         functools.partial(chain_kernel, depth_z, scale, block_z, block_x),
         out_shape=(
             jax.ShapeDtypeStruct((LMAX, 6 * CROWS, rows_y), F32),
-            jax.ShapeDtypeStruct((2, 12 * CROWS, LANES), BF16),
+            jax.ShapeDtypeStruct((12 * CROWS, 3 * LANES), BF16),
             jax.ShapeDtypeStruct((8, LANES), jnp.int32),
         ),
         in_specs=[VMEM] * 6,

time: 31.9 us -> 31.9 us (level)
  no operation moved by 1% of the time
where the time goes in v16:
time: 31.9 us; the launch traced here: 31.7 us
  starting transfers between devices  12.1 us (38%)
  blocking collectives  9.87 us (31%)
  Pallas kernels  5.17 us (16%)
  waiting for transfers between devices  3.8 us (12%)
  between operations  0.7 us (2%)
    all_to_all x1, blocking collectives, shards(): lax.all_to_all(partial.reshape(devices, 1, LANES), 'zs', split_axis=0, co...  9.87 us
    ppermute x3, starting transfers between devices, passed_along(): return lax.ppermute(block, axis, route)  8.29 us
    all_to_all x1, starting transfers between devices, shards(): got = lax.all_to_all(payload, 'zs', split_axis=0, concat_axis=0, tiled=True)  3.83 us
    ppermute x3, waiting for transfers between devices, passed_along(): return lax.ppermute(block, axis, route)  3.1 us
    pallas_call x1, Pallas kernels, shards(): pl.pallas_call(functools.partial(pack_kernel, block_z, block_x), out_shap...  1.8 us
    pallas_call x1, Pallas kernels, shards(): pl.pallas_call(functools.partial(chain_kernel, depth_z, scale, block_z, b...  1.43 us
    pallas_call x1, Pallas kernels, shards(): pl.pallas_call(functools.partial(meet_kernel, block_z, block_x), out_shap...  1.06 us
    all_to_all x1, waiting for transfers between devices, shards(): got = lax.all_to_all(payload, 'zs', split_axis=0, concat_axis=0, tiled=True)  0.7 us
  transfers between devices with their start and end apart: 4, of which 2 were waited for; matrix products, arithmetic and copies ran while one was open for 0% of the time, Pallas kernels for 11%

profile of v16, /device:TPU:0, one launch (start us, length us, event | category | flops | bytes accessed | tf_op | source)
XLA Modules:
  0.0 31.7 jit_solution(9133121335706207127)
XLA Ops:
  0.6 5.1 %collective-permute-start.1 = (bf16[6,6,2,256]{3,2,1,0:T(2,128)(2,1)}, bf16[6,6,2,256]{3,2,1,0:T(2,128)(2,1)S(1)}, u32[]{:S(2)}, u32[]{:S(2)}) collective-permute-start(bf16[6,6,2,256]{3,2,1,0:T(2,128)(2,1)} %bitcast.19), channel_id=1, source_target_pairs={{8,0},{9,1},{10,2},{11,3},{12,4},{13,5},{14,6},{15,7},{16,8},{17,9... | collective-permute-start | bytes 110600 | tf_op jit(solution)/shard_map/ppermute | solution.py:28
  5.7 0.4 %collective-permute-start = (bf16[18,6,2,256]{3,2,1,0:T(2,128)(2,1)}, bf16[18,6,2,256]{3,2,1,0:T(2,128)(2,1)S(1)}, u32[]{:S(2)}, u32[]{:S(2)}) collective-permute-start(bf16[18,6,2,256]{3,2,1,0:T(2,128)(2,1)} %bitcast.14), channel_id=1, source_target_pairs={{8,0},{9,1},{10,2},{11,3},{12,4},{13,5},{14,6},{15,7},{16,8},{17,9... | collective-permute-start | bytes 331784 | tf_op jit(solution)/shard_map/ppermute | solution.py:28
  6.2 1.8 %pack.1 = (f32[32,8,128]{2,1,0:T(8,128)}, s32[8,128]{1,0:T(8,128)}, f32[8,128]{1,0:T(8,128)}) custom-call(f32[8]{0:T(128)} %weight_ref.1, s32[3,8]{1,0:T(4,128)} %bitcast.27, bf16[2,3,8,384]{3,2,1,0:T(8,128)(2,1)} %up_ref.1, bf16[2,3,8,384]{3,2,1,0:T(8,128)(2,1)} %down_ref.1, s32[8,128]{1,0:T(8,128)} %bitcast.24, s32[8,128]{1,0:T(8,128)} %bitcast.25, ...), custom_call_target="tpu_custom_call" | custom-call | flops 2000000000 | bytes 400000 | tf_op jit(solution)/shard_map/pack/pallas_call | solution.py:361
  8.0 0.0 copy-start
  8.0 0.0 copy-start.1
  8.0 3.8 %all-to-all-start = ((f32[32,8,128]{2,1,0:T(8,128)}), f32[32,8,128]{2,1,0:T(8,128)S(1)}, u32[]{:S(2)}, u32[]{:S(2)}) async-start(f32[32,8,128]{2,1,0:T(8,128)} %get-tuple-element.10), calls=%async_computation | async-start | bytes 262144 | tf_op jit(solution)/shard_map/all_to_all | solution.py:389
  11.8 0.0 copy-start.2
  11.8 0.0 copy-start.3
  11.9 0.0 collective-permute-done.links_next_ref.ready_ref
  11.9 0.0 copy-done
  11.9 0.0 copy-done.1
  11.9 2.7 %collective-permute-start.2 = (bf16[18,2,256]{2,1,0:T(2,128)(2,1)S(1)}, bf16[18,2,256]{2,1,0:T(2,128)(2,1)S(1)}, u32[]{:S(2)}, u32[]{:S(2)}) collective-permute-start(bf16[18,2,256]{2,1,0:T(2,128)(2,1)S(1)} %edge.1), channel_id=1, source_target_pairs={{16,0},{17,1},{18,2},{19,3},{20,4},{21,5},{22,6},{23,7},{24,8},{25... | collective-permute-start | bytes 55304 | tf_op jit(solution)/shard_map/ppermute | solution.py:28
  14.7 0.0 collective-permute-done.1.forward_next_ref
  14.7 0.0 copy-done.2
  14.7 0.0 copy-done.3
  14.7 1.4 %chain.1 = (f32[8,96,256]{2,1,0:T(8,128)S(1)}, bf16[192,384]{1,0:T(8,128)(2,1)S(1)}, s32[8,128]{1,0:T(8,128)S(1)}) custom-call(f32[8,128]{1,0:T(8,128)S(1)} %copy-done.3, s32[8,128]{1,0:T(8,128)S(1)} %copy-done.2, bf16[18,6,2,256]{3,2,1,0:T(2,128)(2,1)S(1)} %bitcast.16, bf16[18,6,2,256]{3,2,1,0:T(2,128)(2,1)S(1)} %collective-permute-done.links_next_ref.ready_ref, ...), custom_call_target="tpu_custom_call" | custom-call | flops 3000000000 | bytes 200000 | tf_op jit(solution)/shard_map/chain/pallas_call | solution.py:402
  16.1 3.1 %collective-permute-done.2.edge_ref = bf16[18,2,256]{2,1,0:T(2,128)(2,1)S(1)} collective-permute-done((bf16[18,2,256]{2,1,0:T(2,128)(2,1)S(1)}, bf16[18,2,256]{2,1,0:T(2,128)(2,1)S(1)}, u32[]{:S(2)}, u32[]{:S(2)}) %collective-permute-start.2) | collective-permute-done | bytes 18464 | tf_op jit(solution)/shard_map/ppermute | solution.py:28
  19.2 0.2 tail.1.extra_ref
  19.4 0.7 %all-to-all-done.got_ref = f32[32,8,128]{2,1,0:T(8,128)S(1)} async-done(((f32[32,8,128]{2,1,0:T(8,128)}), f32[32,8,128]{2,1,0:T(8,128)S(1)}, u32[]{:S(2)}, u32[]{:S(2)}) %all-to-all-start) | async-done | bytes 131104 | tf_op jit(solution)/shard_map/all_to_all | solution.py:389
  20.1 1.1 %meet.1 = (f32[6,6,2,256]{3,2,1,0:T(2,128)}, f32[32,128]{1,0:T(8,128)S(1)}) custom-call(f32[32,8,128]{2,1,0:T(8,128)S(1)} %all-to-all-done.got_ref, bf16[192,384]{1,0:T(8,128)(2,1)S(1)} %get-tuple-element.13.corner_ref, f32[8,96,256]{2,1,0:T(8,128)S(1)} %get-tuple-element.14.chain_ref, f32[2,96,256]{2,1,0:T(8,128)S(1)} %tail.1.extra_ref), custom_call_target="tpu_custom_call" | custom-call | flops 2000000000 | bytes 1000000 | tf_op jit(solution)/shard_map/meet/pallas_call | solution.py:430
  21.2 9.9 %all_to_all.10 = f32[32,1,128]{2,1,0:T(1,128)S(1)} all-to-all(f32[32,1,128]{2,1,0:T(1,128)S(1)} %bitcast.22), channel_id=1, replica_groups=mesh['grp'=1,'zs'=32] {'zs'}, dimensions={0} | all-to-all | bytes 32768 | tf_op jit(solution)/shard_map/all_to_all | solution.py:442
  31.0 0.6 %final.1 = f32[2,96]{1,0:T(2,128)} custom-call(f32[32,128]{1,0:T(8,128)S(1)} %bitcast.18, s32[8,128]{1,0:T(8,128)S(1)} %get-tuple-element.17.picked_ref), custom_call_target="tpu_custom_call" | custom-call | tf_op jit(solution)/shard_map/final/pallas_call | solution.py:445
  (1 shorter events, 0.0 us)
Async XLA Ops:
  0.6 14.0 %collective-permute-start.1 = (bf16[6,6,2,256]{3,2,1,0:T(2,128)(2,1)}, bf16[6,6,2,256]{3,2,1,0:T(2,128)(2,1)S(1)}, u32[]{:S(2)}, u32[]{:S(2)}) collective-permute-start(bf16[6,6,2,256]{3,2,1,0:T(2,128)(2,1)} %bitcast.19), channel_id=1, source_target_pairs={{8,0},{9,1},{10,2},{11,3},{12,4},{13,5},{14,6},{15,7},{16,8},{17,9... | collective-permute-start | bytes 110600 | tf_op jit(solution)/shard_map/ppermute | solution.py:28
  5.7 6.1 %collective-permute-start = (bf16[18,6,2,256]{3,2,1,0:T(2,128)(2,1)}, bf16[18,6,2,256]{3,2,1,0:T(2,128)(2,1)S(1)}, u32[]{:S(2)}, u32[]{:S(2)}) collective-permute-start(bf16[18,6,2,256]{3,2,1,0:T(2,128)(2,1)} %bitcast.14), channel_id=1, source_target_pairs={{8,0},{9,1},{10,2},{11,3},{12,4},{13,5},{14,6},{15,7},{16,8},{17,9... | collective-permute-start | bytes 331784 | tf_op jit(solution)/shard_map/ppermute | solution.py:28
  8.0 3.9 %copy-start = (bf16[2,3,3,1,6,2,256]{6,5,4,3,2,1,0:T(2,128)(2,1)S(1)}, bf16[2,3,3,1,6,2,256]{6,5,4,3,2,1,0:T(2,128)(2,1)}, u32[]{:S(2)}) copy-start(bf16[2,3,3,1,6,2,256]{6,5,4,3,2,1,0:T(2,128)(2,1)} %param.12) | copy-start | bytes 331780
  8.0 3.9 %copy-start.1 = (bf16[2,3,1,6,2,256]{5,4,3,2,1,0:T(2,128)(2,1)S(1)}, bf16[2,3,1,6,2,256]{5,4,3,2,1,0:T(2,128)(2,1)}, u32[]{:S(2)}) copy-start(bf16[2,3,1,6,2,256]{5,4,3,2,1,0:T(2,128)(2,1)} %param.11) | copy-start | bytes 110596
  8.0 12.1 %all-to-all-start = ((f32[32,8,128]{2,1,0:T(8,128)}), f32[32,8,128]{2,1,0:T(8,128)S(1)}, u32[]{:S(2)}, u32[]{:S(2)}) async-start(f32[32,8,128]{2,1,0:T(8,128)} %get-tuple-element.10), calls=%async_computation | async-start | bytes 262144 | tf_op jit(solution)/shard_map/all_to_all | solution.py:389
  11.8 2.8 %copy-start.2 = (s32[8,128]{1,0:T(8,128)S(1)}, s32[8,128]{1,0:T(8,128)}, u32[]{:S(2)}) copy-start(s32[8,128]{1,0:T(8,128)} %get-tuple-element.12.request_ref) | copy-start | bytes 12292
  11.8 2.8 %copy-start.3 = (f32[8,128]{1,0:T(8,128)S(1)}, f32[8,128]{1,0:T(8,128)}, u32[]{:S(2)}) copy-start(f32[8,128]{1,0:T(8,128)} %get-tuple-element.11.table_ref) | copy-start | bytes 12292
  11.9 7.3 %collective-permute-start.2 = (bf16[18,2,256]{2,1,0:T(2,128)(2,1)S(1)}, bf16[18,2,256]{2,1,0:T(2,128)(2,1)S(1)}, u32[]{:S(2)}, u32[]{:S(2)}) collective-permute-start(bf16[18,2,256]{2,1,0:T(2,128)(2,1)S(1)} %edge.1), channel_id=1, source_target_pairs={{16,0},{17,1},{18,2},{19,3},{20,4},{21,5},{22,6},{23,7},{24,8},{25... | collective-permute-start | bytes 55304 | tf_op jit(solution)/shard_map/ppermute | solution.py:28

commit v17 on v16

--- a/solution.py
+++ b/solution.py
@@ -100,8 +100,8 @@
     for zb in range(z_blocks):
         for g in range(G):
             at = (g // 4) * LANES
-            value = jnp.zeros((NT, LANES), F32)
-            for comp in range(6):
+            value = results[0][zb, :, at : at + LANES]
+            for comp in range(1, 6):
                 value = jnp.where(
                     one_slot == (comp + g) % 6, results[comp][zb, :, at : at + LANES], value
                 )

time: 31.9 us -> 31.9 us (level)
  no operation moved by 1% of the time
where the time goes in v17:
time: 31.9 us; the launch traced here: 31.7 us
  starting transfers between devices  12.1 us (38%)
  blocking collectives  9.87 us (31%)
  Pallas kernels  5.17 us (16%)
  waiting for transfers between devices  3.8 us (12%)
  between operations  0.7 us (2%)
    all_to_all x1, blocking collectives, shards(): lax.all_to_all(partial.reshape(devices, 1, LANES), 'zs', split_axis=0, co...  9.87 us
    ppermute x3, starting transfers between devices, passed_along(): return lax.ppermute(block, axis, route)  8.29 us
    all_to_all x1, starting transfers between devices, shards(): got = lax.all_to_all(payload, 'zs', split_axis=0, concat_axis=0, tiled=True)  3.83 us
    ppermute x3, waiting for transfers between devices, passed_along(): return lax.ppermute(block, axis, route)  3.1 us
    pallas_call x1, Pallas kernels, shards(): pl.pallas_call(functools.partial(pack_kernel, block_z, block_x), out_shap...  1.8 us
    pallas_call x1, Pallas kernels, shards(): pl.pallas_call(functools.partial(chain_kernel, depth_z, scale, block_z, b...  1.43 us
    pallas_call x1, Pallas kernels, shards(): pl.pallas_call(functools.partial(meet_kernel, block_z, block_x), out_shap...  1.06 us
    all_to_all x1, waiting for transfers between devices, shards(): got = lax.all_to_all(payload, 'zs', split_axis=0, concat_axis=0, tiled=True)  0.7 us
  transfers between devices with their start and end apart: 4, of which 2 were waited for; matrix products, arithmetic and copies ran while one was open for 0% of the time, Pallas kernels for 11%

profile of v17, /device:TPU:0, one launch (start us, length us, event | category | flops | bytes accessed | tf_op | source)
XLA Modules:
  0.0 31.7 jit_solution(7487554070523584977)
XLA Ops:
  0.6 5.1 %collective-permute-start.1 = (bf16[6,6,2,256]{3,2,1,0:T(2,128)(2,1)}, bf16[6,6,2,256]{3,2,1,0:T(2,128)(2,1)S(1)}, u32[]{:S(2)}, u32[]{:S(2)}) collective-permute-start(bf16[6,6,2,256]{3,2,1,0:T(2,128)(2,1)} %bitcast.19), channel_id=1, source_target_pairs={{8,0},{9,1},{10,2},{11,3},{12,4},{13,5},{14,6},{15,7},{16,8},{17,9... | collective-permute-start | bytes 110600 | tf_op jit(solution)/shard_map/ppermute | solution.py:28
  5.7 0.4 %collective-permute-start = (bf16[18,6,2,256]{3,2,1,0:T(2,128)(2,1)}, bf16[18,6,2,256]{3,2,1,0:T(2,128)(2,1)S(1)}, u32[]{:S(2)}, u32[]{:S(2)}) collective-permute-start(bf16[18,6,2,256]{3,2,1,0:T(2,128)(2,1)} %bitcast.14), channel_id=1, source_target_pairs={{8,0},{9,1},{10,2},{11,3},{12,4},{13,5},{14,6},{15,7},{16,8},{17,9... | collective-permute-start | bytes 331784 | tf_op jit(solution)/shard_map/ppermute | solution.py:28
  6.2 1.8 %pack.1 = (f32[32,8,128]{2,1,0:T(8,128)}, s32[8,128]{1,0:T(8,128)}, f32[8,128]{1,0:T(8,128)}) custom-call(f32[8]{0:T(128)} %weight_ref.1, s32[3,8]{1,0:T(4,128)} %bitcast.27, bf16[2,3,8,384]{3,2,1,0:T(8,128)(2,1)} %up_ref.1, bf16[2,3,8,384]{3,2,1,0:T(8,128)(2,1)} %down_ref.1, s32[8,128]{1,0:T(8,128)} %bitcast.24, s32[8,128]{1,0:T(8,128)} %bitcast.25, ...), custom_call_target="tpu_custom_call" | custom-call | flops 2000000000 | bytes 400000 | tf_op jit(solution)/shard_map/pack/pallas_call | solution.py:361
  8.0 0.0 copy-start
  8.0 0.0 copy-start.1
  8.0 3.8 %all-to-all-start = ((f32[32,8,128]{2,1,0:T(8,128)}), f32[32,8,128]{2,1,0:T(8,128)S(1)}, u32[]{:S(2)}, u32[]{:S(2)}) async-start(f32[32,8,128]{2,1,0:T(8,128)} %get-tuple-element.10), calls=%async_computation | async-start | bytes 262144 | tf_op jit(solution)/shard_map/all_to_all | solution.py:389
  11.8 0.0 copy-start.2
  11.8 0.0 copy-start.3
  11.9 0.0 collective-permute-done.links_next_ref.ready_ref
  11.9 0.0 copy-done
  11.9 0.0 copy-done.1
  11.9 2.7 %collective-permute-start.2 = (bf16[18,2,256]{2,1,0:T(2,128)(2,1)S(1)}, bf16[18,2,256]{2,1,0:T(2,128)(2,1)S(1)}, u32[]{:S(2)}, u32[]{:S(2)}) collective-permute-start(bf16[18,2,256]{2,1,0:T(2,128)(2,1)S(1)} %edge.1), channel_id=1, source_target_pairs={{16,0},{17,1},{18,2},{19,3},{20,4},{21,5},{22,6},{23,7},{24,8},{25... | collective-permute-start | bytes 55304 | tf_op jit(solution)/shard_map/ppermute | solution.py:28
  14.7 0.0 collective-permute-done.1.forward_next_ref
  14.7 0.0 copy-done.2
  14.7 0.0 copy-done.3
  14.7 1.4 %chain.1 = (f32[8,96,256]{2,1,0:T(8,128)S(1)}, bf16[192,384]{1,0:T(8,128)(2,1)S(1)}, s32[8,128]{1,0:T(8,128)S(1)}) custom-call(f32[8,128]{1,0:T(8,128)S(1)} %copy-done.3, s32[8,128]{1,0:T(8,128)S(1)} %copy-done.2, bf16[18,6,2,256]{3,2,1,0:T(2,128)(2,1)S(1)} %bitcast.16, bf16[18,6,2,256]{3,2,1,0:T(2,128)(2,1)S(1)} %collective-permute-done.links_next_ref.ready_ref, ...), custom_call_target="tpu_custom_call" | custom-call | flops 3000000000 | bytes 200000 | tf_op jit(solution)/shard_map/chain/pallas_call | solution.py:402
  16.1 3.1 %collective-permute-done.2.edge_ref = bf16[18,2,256]{2,1,0:T(2,128)(2,1)S(1)} collective-permute-done((bf16[18,2,256]{2,1,0:T(2,128)(2,1)S(1)}, bf16[18,2,256]{2,1,0:T(2,128)(2,1)S(1)}, u32[]{:S(2)}, u32[]{:S(2)}) %collective-permute-start.2) | collective-permute-done | bytes 18464 | tf_op jit(solution)/shard_map/ppermute | solution.py:28
  19.2 0.2 tail.1.extra_ref
  19.4 0.7 %all-to-all-done.got_ref = f32[32,8,128]{2,1,0:T(8,128)S(1)} async-done(((f32[32,8,128]{2,1,0:T(8,128)}), f32[32,8,128]{2,1,0:T(8,128)S(1)}, u32[]{:S(2)}, u32[]{:S(2)}) %all-to-all-start) | async-done | bytes 131104 | tf_op jit(solution)/shard_map/all_to_all | solution.py:389
  20.1 1.1 %meet.1 = (f32[6,6,2,256]{3,2,1,0:T(2,128)}, f32[32,128]{1,0:T(8,128)S(1)}) custom-call(f32[32,8,128]{2,1,0:T(8,128)S(1)} %all-to-all-done.got_ref, bf16[192,384]{1,0:T(8,128)(2,1)S(1)} %get-tuple-element.13.corner_ref, f32[8,96,256]{2,1,0:T(8,128)S(1)} %get-tuple-element.14.chain_ref, f32[2,96,256]{2,1,0:T(8,128)S(1)} %tail.1.extra_ref), custom_call_target="tpu_custom_call" | custom-call | flops 2000000000 | bytes 1000000 | tf_op jit(solution)/shard_map/meet/pallas_call | solution.py:430
  21.2 9.9 %all_to_all.10 = f32[32,1,128]{2,1,0:T(1,128)S(1)} all-to-all(f32[32,1,128]{2,1,0:T(1,128)S(1)} %bitcast.22), channel_id=1, replica_groups=mesh['grp'=1,'zs'=32] {'zs'}, dimensions={0} | all-to-all | bytes 32768 | tf_op jit(solution)/shard_map/all_to_all | solution.py:442
  31.0 0.6 %final.1 = f32[2,96]{1,0:T(2,128)} custom-call(f32[32,128]{1,0:T(8,128)S(1)} %bitcast.18, s32[8,128]{1,0:T(8,128)S(1)} %get-tuple-element.17.picked_ref), custom_call_target="tpu_custom_call" | custom-call | tf_op jit(solution)/shard_map/final/pallas_call | solution.py:445
  (1 shorter events, 0.0 us)
Async XLA Ops:
  0.6 14.0 %collective-permute-start.1 = (bf16[6,6,2,256]{3,2,1,0:T(2,128)(2,1)}, bf16[6,6,2,256]{3,2,1,0:T(2,128)(2,1)S(1)}, u32[]{:S(2)}, u32[]{:S(2)}) collective-permute-start(bf16[6,6,2,256]{3,2,1,0:T(2,128)(2,1)} %bitcast.19), channel_id=1, source_target_pairs={{8,0},{9,1},{10,2},{11,3},{12,4},{13,5},{14,6},{15,7},{16,8},{17,9... | collective-permute-start | bytes 110600 | tf_op jit(solution)/shard_map/ppermute | solution.py:28
  5.7 6.1 %collective-permute-start = (bf16[18,6,2,256]{3,2,1,0:T(2,128)(2,1)}, bf16[18,6,2,256]{3,2,1,0:T(2,128)(2,1)S(1)}, u32[]{:S(2)}, u32[]{:S(2)}) collective-permute-start(bf16[18,6,2,256]{3,2,1,0:T(2,128)(2,1)} %bitcast.14), channel_id=1, source_target_pairs={{8,0},{9,1},{10,2},{11,3},{12,4},{13,5},{14,6},{15,7},{16,8},{17,9... | collective-permute-start | bytes 331784 | tf_op jit(solution)/shard_map/ppermute | solution.py:28
  8.0 3.9 %copy-start = (bf16[2,3,3,1,6,2,256]{6,5,4,3,2,1,0:T(2,128)(2,1)S(1)}, bf16[2,3,3,1,6,2,256]{6,5,4,3,2,1,0:T(2,128)(2,1)}, u32[]{:S(2)}) copy-start(bf16[2,3,3,1,6,2,256]{6,5,4,3,2,1,0:T(2,128)(2,1)} %param.12) | copy-start | bytes 331780
  8.0 3.9 %copy-start.1 = (bf16[2,3,1,6,2,256]{5,4,3,2,1,0:T(2,128)(2,1)S(1)}, bf16[2,3,1,6,2,256]{5,4,3,2,1,0:T(2,128)(2,1)}, u32[]{:S(2)}) copy-start(bf16[2,3,1,6,2,256]{5,4,3,2,1,0:T(2,128)(2,1)} %param.11) | copy-start | bytes 110596
  8.0 12.1 %all-to-all-start = ((f32[32,8,128]{2,1,0:T(8,128)}), f32[32,8,128]{2,1,0:T(8,128)S(1)}, u32[]{:S(2)}, u32[]{:S(2)}) async-start(f32[32,8,128]{2,1,0:T(8,128)} %get-tuple-element.10), calls=%async_computation | async-start | bytes 262144 | tf_op jit(solution)/shard_map/all_to_all | solution.py:389
  11.8 2.8 %copy-start.2 = (s32[8,128]{1,0:T(8,128)S(1)}, s32[8,128]{1,0:T(8,128)}, u32[]{:S(2)}) copy-start(s32[8,128]{1,0:T(8,128)} %get-tuple-element.12.request_ref) | copy-start | bytes 12292
  11.8 2.8 %copy-start.3 = (f32[8,128]{1,0:T(8,128)S(1)}, f32[8,128]{1,0:T(8,128)}, u32[]{:S(2)}) copy-start(f32[8,128]{1,0:T(8,128)} %get-tuple-element.11.table_ref) | copy-start | bytes 12292
  11.9 7.3 %collective-permute-start.2 = (bf16[18,2,256]{2,1,0:T(2,128)(2,1)S(1)}, bf16[18,2,256]{2,1,0:T(2,128)(2,1)S(1)}, u32[]{:S(2)}, u32[]{:S(2)}) collective-permute-start(bf16[18,2,256]{2,1,0:T(2,128)(2,1)S(1)} %edge.1), channel_id=1, source_target_pairs={{16,0},{17,1},{18,2},{19,3},{20,4},{21,5},{22,6},{23,7},{24,8},{25... | collective-permute-start | bytes 55304 | tf_op jit(solution)/shard_map/ppermute | solution.py:28
